TPU v7x, 256 devices: a whole 4x4x8 slice. The times are simulated.
256 devices in a mesh: dp: 16 (over y, z_lo), owner: 16 (over x, z_hi, core).
Axes of the slice: x: 4, y: 4, z: 8 (z_hi: 2, z_lo: 4; z = z_hi * 4 + z_lo), core: 2. Of those that a mesh axis runs over, the one named last changes fastest.
Arguments:
- inputs: bfloat16 [8192, 4096], P('dp'), may hold values from -6 to 6
- out_grads: bfloat16 [8192, 16384], P('dp', 'owner'), may hold values from -0.0625 to 0.0625
- basis_in: bfloat16 [1024, 4096], P(None, 'owner'), may hold values from -0.1875 to 0.1875
- basis_out: bfloat16 [1024, 16384], P(None, 'owner'), may hold values from -0.1875 to 0.1875
- eigenvalues: float32 [4096, 16384], P('dp', 'owner'), may hold values from 0.2 to 5
Outputs:
- precond: bfloat16 [4096, 16384], P('dp', 'owner')
All inputs are finite; a program needn't handle non-finite values.
Results may differ from a plain program's by a relative error of at most 0.023.
Values may be sent and summed in bfloat16 or wider, within the bound.
No kernel may reach another device: no remote copies, remote signals or barrier semaphores. Data moves between devices by JAX's collectives and lax.ppermute only.
A program may use at most 64 MiB of HBM per device.

v0:
```python
import jax
import jax.numpy as jnp
from jax import lax
from jax.sharding import PartitionSpec as P

DAMPING = 0.05


def swapped(block, axis, bit):
    count = lax.axis_size(axis)
    route = []
    for low in range(count):
        high = low | 1 << bit
        if high != low and high < count:
            route += [(low, high), (high, low)]
    return lax.ppermute(block, axis, route)


def tokens_product(column_piece, rotated_g):
    return lax.dot_general(
        column_piece, rotated_g, (((0,), (0,)), ((), ())), preferred_element_type=jnp.float32
    )


def on_device(inputs, out_grads, basis_in, basis_out, eigenvalues):
    block = basis_in.shape[0]
    input_cols = basis_in.shape[1]
    output_cols = basis_out.shape[1]
    tok_rows = inputs.shape[0]
    tile_rows = eigenvalues.shape[0]
    owner_at = lax.axis_index("owner")
    data_at = lax.axis_index("dp")
    blocks_here = output_cols // block
    in_start = owner_at * input_cols // block * block
    inputs_block = lax.dynamic_slice_in_dim(inputs, in_start, block, 1)
    rotated_own = jnp.dot(inputs_block, basis_in, preferred_element_type=jnp.float32).astype(
        jnp.bfloat16
    )
    out_panels = basis_out.reshape(block, blocks_here, block)
    grad_rot = jnp.einsum(
        "tnj,jnl->tnl",
        out_grads.reshape(tok_rows, blocks_here, block),
        out_panels,
        preferred_element_type=jnp.float32,
    )
    grad_rot = grad_rot.reshape(tok_rows, output_cols).astype(jnp.bfloat16)
    partials = tokens_product(lax.all_gather(rotated_own, "owner", axis=1, tiled=True), grad_rot)
    summed = lax.psum_scatter(
        partials.astype(jnp.bfloat16), "dp", scatter_dimension=0, tiled=True
    ).astype(jnp.float32)
    scaled = (summed / (eigenvalues + DAMPING)).astype(jnp.bfloat16)
    rotated_back = jnp.einsum(
        "knl,jnl->knj",
        scaled.reshape(tile_rows, blocks_here, block),
        out_panels,
        preferred_element_type=jnp.float32,
    )
    right_done = rotated_back.reshape(tile_rows, output_cols).astype(jnp.bfloat16)
    row_start = data_at * tile_rows % block
    own_rows = lax.dynamic_slice_in_dim(basis_in, row_start, tile_rows, 0)
    panel_all = lax.all_gather(own_rows, "owner", axis=1, tiled=True)
    block_start = data_at * tile_rows // block * block
    row_panel = lax.dynamic_slice_in_dim(panel_all, block_start, block, 1)
    block_rows = right_done
    for level in range((block // tile_rows).bit_length() - 1):
        partner = swapped(block_rows, "dp", level)
        lower_half = data_at >> level & 1 == 0
        block_rows = jnp.where(
            lower_half,
            jnp.concatenate([block_rows, partner], 0),
            jnp.concatenate([partner, block_rows], 0),
        )
    return jnp.dot(row_panel, block_rows, preferred_element_type=jnp.float32).astype(jnp.bfloat16)


def solution(mesh):
    placed = (P("dp", None), P("dp", "owner"), P(None, "owner"), P(None, "owner"), P("dp", "owner"))
    return jax.shard_map(
        on_device, mesh=mesh, in_specs=placed, out_specs=P("dp", "owner"), check_vma=False
    )
```

profile of v0, /device:TPU:8, one launch (start us, length us, event | category | flops | bytes accessed | tf_op | source)
XLA Modules:
  0.0 372.1 jit_solution(2335890615986052842)
XLA Ops:
  6.5 0.0 copy-start
  6.5 0.0 copy-start.2
  6.5 0.0 all-gather.5.cloned.1.call-start
  6.5 2.7 convolution_convert_fusion.3
  9.2 0.0 all-gather.5.cloned.1.call-update
  9.2 0.0 reduce-scatter.2.cloned.1.call-start
  9.3 81.7 %all-gather.5.cloned.1.call-done = bf16[512,4096]{1,0:T(8,128)(2,1)} async-done(((bf16[512,256]{1,0:T(8,128)(2,1)}), bf16[512,4096]{1,0:T(8,128)(2,1)}) %all-gather.5.cloned.1.call-update) | async-done | bytes 4194320 | tf_op jit(solution)/shard_map/all_gather | solution.py:47
  91.0 0.0 copy-done
  91.0 0.0 copy-done.2
  91.0 10.3 %convolution_convert_fusion = bf16[4096,1024]{1,0:T(8,128)(2,1)} fusion(bf16[512,4096]{1,0:T(8,128)(2,1)} %all-gather.5.cloned.1.call-done, bf16[1024,1024]{1,0:T(8,128)(2,1)S(1)} %copy-done, bf16[512,1024]{1,0:T(8,128)(2,1)S(1)} %copy-done.2), kind=kOutput, calls=%fused_computation | convolution fusion | flops 5373427712 | bytes 15728640 | tf_op jit(solution)/shard_map/dot_general | solution.py:20
  101.4 0.0 reduce-scatter.2.cloned.1.call-update
  101.4 0.0 all-gather.3.cloned.1.call-start
  101.4 1.6 constant_dynamic-slice_fusion
  103.0 0.0 all-gather.3.cloned.1.call-update
  103.0 180.3 %reduce-scatter.2.cloned.1.call-done = bf16[256,1024]{1,0:T(8,128)(2,1)} async-done(((bf16[4096,1024]{1,0:T(8,128)(2,1)}), bf16[256,1024]{1,0:T(8,128)(2,1)}) %reduce-scatter.2.cloned.1.call-update) | async-done | bytes 524304 | tf_op jit(solution)/shard_map/reduce_scatter | solution.py:48
  283.3 2.1 convolution_convert_fusion.2
  285.4 0.0 copy-start.1
  285.4 0.1 collective-permute-start
  285.5 0.7 copy-done.1
  286.2 12.9 %collective-permute-done = bf16[256,1024]{1,0:T(8,128)(2,1)} collective-permute-done((bf16[256,1024]{1,0:T(8,128)(2,1)S(1)}, bf16[256,1024]{1,0:T(8,128)(2,1)}, u32[]{:S(2)}, u32[]{:S(2)}) %collective-permute-start) | collective-permute-done | bytes 524320 | tf_op jit(solution)/shard_map/ppermute | solution.py:16
  299.1 2.1 maximum_select_fusion.4
  301.2 2.1 collective-permute-start.1
  303.3 49.3 %all-gather.3.cloned.1.call-done = bf16[256,4096]{1,0:T(8,128)(2,1)} async-done(((bf16[256,256]{1,0:T(8,128)(2,1)}), bf16[256,4096]{1,0:T(8,128)(2,1)}) %all-gather.3.cloned.1.call-update) | async-done | bytes 2097168 | tf_op jit(solution)/shard_map/all_gather | solution.py:61
  352.6 9.7 %collective-permute-done.1 = bf16[512,1024]{1,0:T(8,128)(2,1)} collective-permute-done((bf16[512,1024]{1,0:T(8,128)(2,1)S(1)}, bf16[512,1024]{1,0:T(8,128)(2,1)}, u32[]{:S(2)}, u32[]{:S(2)}) %collective-permute-start.1) | collective-permute-done | bytes 1048608 | tf_op jit(solution)/shard_map/ppermute | solution.py:16
  362.3 3.2 fusion.8
Async XLA Ops:
  6.5 84.5 %copy-start = (bf16[1024,1024]{1,0:T(8,128)(2,1)S(1)}, bf16[1024,1024]{1,0:T(8,128)(2,1)}, u32[]{:S(2)}) copy-start(bf16[1024,1024]{1,0:T(8,128)(2,1)} %param.8) | copy-start | bytes 6291460
  6.5 84.5 %copy-start.2 = (bf16[512,1024]{1,0:T(8,128)(2,1)S(1)}, bf16[512,1024]{1,0:T(8,128)(2,1)}, u32[]{:S(2)}) copy-start(bf16[512,1024]{1,0:T(8,128)(2,1)} %param.6) | copy-start | bytes 3145732
  6.5 84.5 %all-gather.5.cloned.1.call-start = ((), (), s32[]{:S(2)}) async-start(), calls=%async_computation.2 | async-start | bytes 4456448 | tf_op jit(solution)/shard_map/all_gather | solution.py:47
  9.2 274.1 %reduce-scatter.2.cloned.1.call-start = ((), (), s32[]{:S(2)}) async-start(), calls=%async_computation.3 | async-start | bytes 8912896 | tf_op jit(solution)/shard_map/reduce_scatter | solution.py:48
  101.4 251.2 %all-gather.3.cloned.1.call-start = ((), (), s32[]{:S(2)}) async-start(), calls=%async_computation.1 | async-start | bytes 2228224 | tf_op jit(solution)/shard_map/all_gather | solution.py:61
  285.4 0.8 copy-start.1
  285.4 13.7 %collective-permute-start = (bf16[256,1024]{1,0:T(8,128)(2,1)S(1)}, bf16[256,1024]{1,0:T(8,128)(2,1)}, u32[]{:S(2)}, u32[]{:S(2)}) collective-permute-start(bf16[256,1024]{1,0:T(8,128)(2,1)S(1)} %convolution_convert_fusion.2), channel_id=1, source_target_pairs={{0,16},{16,0},{32,48},{48,32},{64,80},{80,64},{96,112},{112,96},{1... | collective-permute-start | bytes 1572872 | tf_op jit(solution)/shard_map/ppermute | solution.py:16
  301.2 61.1 %collective-permute-start.1 = (bf16[512,1024]{1,0:T(8,128)(2,1)S(1)}, bf16[512,1024]{1,0:T(8,128)(2,1)}, u32[]{:S(2)}, u32[]{:S(2)}) collective-permute-start(bf16[512,1024]{1,0:T(8,128)(2,1)S(1)} %maximum_select_fusion.4), channel_id=1, source_target_pairs={{0,32},{32,0},{16,48},{48,16},{64,96},{96,64},{80,112},{112,80},{1... | collective-permute-start | bytes 3145736 | tf_op jit(solution)/shard_map/ppermute | solution.py:16
Sparse Core Ops, SparseCore 0:
  9.9 81.0 all-gather.4
  101.5 181.7 reduce-scatter.1
  285.8 66.6 all-gather.2
where the time goes:
time: 374 us; the launch traced here: 372 us
  waiting for transfers between devices  334 us (89%)
  matrix products  18.4 us (5%)
  between operations  13.2 us (4%)
    reduce_scatter x1, waiting for transfers between devices, on_device(): lax.psum_scatter(partials.astype(jnp.bfloat16), 'dp', scatter_dimension=0...  180 us
    all_gather x1, waiting for transfers between devices, on_device(): lax.all_gather(rotated_own, 'owner', axis=1, tiled=True)  81.7 us
    all_gather x1, waiting for transfers between devices, on_device(): panel_all = lax.all_gather(own_rows, 'owner', axis=1, tiled=True)  49.3 us
    ppermute x2, waiting for transfers between devices, swapped(): return lax.ppermute(block, axis, route)  22.6 us
    dot_general x1, matrix products, tokens_product(): lax.dot_general(column_piece, rotated_g, (((0,), (0,)), ((), ())), prefer...  10.3 us
  transfers between devices with their start and end apart: 5, of which 5 were waited for; matrix products, arithmetic and copies ran while one was open for 2% of the time, Pallas kernels for 0%

commit v1 on v0

v1 whole, which is shorter than its diff:
```python
import jax
import jax.numpy as jnp
from jax import lax
from jax.sharding import PartitionSpec as P

DAMPING = 0.05
NX, NY, NZ = 4, 4, 4
L_PARTS = 1
K_PARTS = 1
BF = jnp.bfloat16
F32 = jnp.float32


def moved(block, place):
    route = []
    for y in range(NY):
        for z in range(NZ):
            for x in range(NX):
                for h in range(2):
                    for c in range(2):
                        to = place(x, y, z, h, c)
                        if to is None:
                            continue
                        tx, ty, tz, th, tc = to
                        source = (y * NZ + z) * 16 + x * 4 + h * 2 + c
                        target = (ty % NY * NZ + tz) * 16 + tx % NX * 4 + th * 2 + tc
                        route.append((source, target))
    return lax.ppermute(block, ("dp", "owner"), route)


def along_x(block, k):
    return moved(block, lambda x, y, z, h, c: (x + k, y, z, h, c))


def along_y(block, k):
    return moved(block, lambda x, y, z, h, c: (x, y + k, z, h, c))


def z_step(block, k, sources):
    return moved(block, lambda x, y, z, h, c: (x, y, z + k, h, c) if z in sources else None)


def from_diagonal(block, k):
    return moved(block, lambda x, y, z, h, c: (x + k, y, z, h, c) if x == y else None)


def other_half(block):
    return moved(block, lambda x, y, z, h, c: (x, y, z, 1 - h, c))


def other_core(block):
    return moved(block, lambda x, y, z, h, c: (x, y, z, h, 1 - c))


def dot(a, b, dims):
    return lax.dot_general(a, b, ((dims[:1], dims[1:]), ((), ())), preferred_element_type=F32)


def on_device(inputs, out_grads, basis_in, basis_out, eigenvalues):
    tok = inputs.shape[0]
    block = basis_in.shape[0]
    quarter = block // 4
    half = tok // 2
    owner = lax.axis_index("owner")
    data = lax.axis_index("dp")
    x, h, c = owner // 4, owner // 2 % 2, owner % 2
    y, z = data // NZ, data % NZ
    hc = owner % 4

    def basis_piece(k):
        return lax.dynamic_slice_in_dim(basis_in, (x + k) % NX * quarter, quarter, 0)

    piece = jnp.where(x == y, basis_piece(0), jnp.zeros((), BF))
    for k in (1, 3, 2):
        piece = piece + from_diagonal(basis_piece(k), k)
    pieces = jnp.stack([piece, other_half(piece)])
    mine = [pieces] + [along_x(pieces, k) for k in (1, 2, 3)]
    mine = jnp.stack(mine, 1)
    both = jnp.stack([mine, other_core(mine)], 1).reshape(4, block, quarter)

    own_half = lax.dynamic_slice_in_dim(inputs, c * half, half, 0)
    rest_half = lax.dynamic_slice_in_dim(inputs, (1 - c) * half, half, 0)

    def columns(rows, b, at):
        return lax.dynamic_slice_in_dim(rows, b % NY * block + at % NX * quarter, quarter, 1)

    got = jnp.stack([along_y(columns(own_half, y + k, x), k) for k in (1, 2, 3)])
    got = jnp.stack([got] + [along_x(got, k) for k in (1, 2, 3)])
    got_other = other_core(got)
    x_all = []
    for j in range(NX):
        x_all.append(
            jnp.concatenate(
                [columns(own_half, y, x - j), columns(rest_half, y, x - j)]
                + [got[j].reshape(3 * half, quarter), got_other[j].reshape(3 * half, quarter)],
                0,
            )
        )
    x_all = jnp.concatenate(x_all, 1)

    og_own = lax.dynamic_slice_in_dim(out_grads, c * half, half, 0)
    og_rest = lax.dynamic_slice_in_dim(out_grads, (1 - c) * half, half, 0)
    lw = block // L_PARTS
    kw = quarter // K_PARTS
    m_parts = []
    for g in range(L_PARTS):
        s_part = basis_out[:, g * lw : (g + 1) * lw]
        gt = jnp.stack([dot(s_part, og_own, (0, 1)), dot(s_part, og_rest, (0, 1))]).astype(BF)
        others = [along_y(gt, k) for k in (1, 2, 3)]
        g_all = jnp.concatenate(
            [gt[0], gt[1]] + [o[0] for o in others] + [o[1] for o in others], 1
        )
        m_parts.append(dot(g_all, x_all, (1, 0)).astype(BF))

    inverse = (1.0 / (eigenvalues + DAMPING)).T

    def basis_for(d):
        return lax.dynamic_index_in_dim(both, (z + d) % NZ ^ hc, 0, keepdims=False)

    bases = [basis_for(d) for d in range(4)]
    row_at = (x - z) % NX * quarter
    rows = [lax.dynamic_slice_in_dim(b, row_at, quarter, 0) for b in bases]
    out = None
    for n in range(K_PARTS):
        cols = slice(n * kw, (n + 1) * kw)
        scaled = []
        for g in range(L_PARTS):
            part = [dot(m_parts[g], bases[d][:, cols], (1, 0)) for d in range(4)]
            low = z == 0
            first = jnp.where(low, part[3], part[1]).astype(BF)
            up = z_step(first, 1, (0,))
            down = z_step(first, -1, (3,))
            up = z_step((part[2] + up.astype(F32)).astype(BF), 1, (0, 1))
            down = z_step((part[2] + down.astype(F32)).astype(BF), -1, (2, 3))
            up = z_step((part[1] + up.astype(F32)).astype(BF), 1, (0, 1, 2))
            down = z_step((part[3] + down.astype(F32)).astype(BF), -1, (1, 2, 3))
            total = part[0] + up.astype(F32) + down.astype(F32)
            scaled.append((total * inverse[g * lw : (g + 1) * lw, cols]).astype(BF))
        right = dot(basis_out, jnp.concatenate(scaled, 0), (1, 0)).astype(BF)
        up1 = z_step(right, 1, (0, 1, 2))
        down1 = z_step(right, -1, (1, 2, 3))
        up2 = z_step(up1, 1, (1, 2))
        down2 = z_step(down1, -1, (1, 2))
        up3 = z_step(up2, 1, (2,))
        down3 = z_step(down2, -1, (1,))
        for d, r in enumerate((right, down1 + up3, down2 + up2, up1 + down3)):
            term = dot(rows[d][:, cols], r, (1, 1))
            out = term if out is None else out + term
    return out.astype(BF)


def solution(mesh):
    placed = (P("dp", None), P("dp", "owner"), P(None, "owner"), P(None, "owner"), P("dp", "owner"))
    return jax.shard_map(
        on_device, mesh=mesh, in_specs=placed, out_specs=P("dp", "owner"), check_vma=False
    )
```

time: 374 us -> 216 us (0.58)
  waiting for transfers between devices: 334 us -> 81.6 us
  starting transfers between devices: 2.26 us -> 66.1 us
  matrix products: 18.4 us -> 44.6 us
  between operations: 13.2 us -> 0.47 us
  local copies, waits for them, and re-layouts: 2.24 us -> 14.1 us
  other arithmetic: 2.13 us -> 8.67 us
    reduce_scatter x1 -> x0, waiting for transfers between devices: 180 us -> none  [on_device(): lax.psum_scatter(partials.astype(jnp.bfloat16), 'dp', scatter_dimension=0...]
    all_gather x2 -> x0, waiting for transfers between devices: 131 us -> none  [the longest x1 81.7 us: on_device(): lax.all_gather(rotated_own, 'owner', axis=1, tiled=True)]
    ppermute x2 -> x30, starting transfers between devices: 2.17 us -> 66.1 us  [moved(): return lax.ppermute(block, ('dp', 'owner'), route)]
    ppermute x2 -> x30, waiting for transfers between devices: 22.6 us -> 81.6 us  [moved(): return lax.ppermute(block, ('dp', 'owner'), route)]
    dot_general x4 -> x11, matrix products: 18.4 us -> 44.6 us  [dot(): lax.dot_general(a, b, ((dims[:1], dims[1:]), ((), ())), preferred_element...]
    unnamed x6 -> x38, local copies, waits for them, and re-layouts: 0.69 us -> 7.01 us
    another operation x0 -> x6, other arithmetic: none -> 5.67 us  [the longest x2 2.37 us: on_device(): got = jnp.stack([got] + [along_x(got, k) for k in (1, 2, 3)])]
    dynamic_slice x1 -> x2, local copies, waits for them, and re-layouts: 1.55 us -> 5.8 us  [the longest x1 4.01 us: columns(): lax.dynamic_slice_in_dim(rows, b % NY * block + at % NX * quarter, quarte...]
  transfers between devices with their start and end apart: 5 -> 30, of which waited for: 5 -> 14; matrix products, arithmetic and copies ran while one was open for 2% -> 13% of each run, Pallas kernels for 0% -> 0%
where the time goes in v1:
time: 216 us
  waiting for transfers between devices  81.6 us (38%)
  starting transfers between devices  66.1 us (31%)
  matrix products  44.6 us (21%)
  local copies, waits for them, and re-layouts  14.1 us (7%)
  other arithmetic  8.67 us (4%)
    ppermute x30, waiting for transfers between devices, moved(): return lax.ppermute(block, ('dp', 'owner'), route)  81.6 us
    ppermute x30, starting transfers between devices, moved(): return lax.ppermute(block, ('dp', 'owner'), route)  66.1 us
    dot_general x11, matrix products, dot(): lax.dot_general(a, b, ((dims[:1], dims[1:]), ((), ())), preferred_element...  44.6 us
    unnamed x38, local copies, waits for them, and re-layouts  7.01 us
  transfers between devices with their start and end apart: 30, of which 14 were waited for; matrix products, arithmetic and copies ran while one was open for 13% of the time, Pallas kernels for 0%

profile of v1, /device:TPU:8, one launch (start us, length us, event | category | flops | bytes accessed | tf_op | source)
XLA Modules:
  0.0 215.6 jit_solution(9469954301808000054)
XLA Ops:
  0.0 4.0 %fusion.94 = (bf16[256,256]{1,0:T(8,128)(2,1)}, bf16[256,256]{1,0:T(8,128)(2,1)}, bf16[256,256]{1,0:T(8,128)(2,1)}, bf16[256,256]{1,0:T(8,128)(2,1)}, bf16[256,2...) fusion(bf16[512,4096]{1,0:T(8,128)(2,1)} %param.5, ...), kind=kLoop, calls=%fused_computation.115 | loop fusion | bytes 2883620 | tf_op jit(solution)/shard_map/dynamic_slice | solution.py:85
  4.0 2.2 %collective-permute-start.13 = (bf16[256,256]{1,0:T(8,128)(2,1)}, bf16[256,256]{1,0:T(8,128)(2,1)S(1)}, u32[]{:S(2)}, u32[]{:S(2)}) collective-permute-start(bf16[256,256]{1,0:T(8,128)(2,1)} %get-tuple-element.10), channel_id=1, source_target_pairs={{0,192},{1,193},{2,194},{3,195},{4,196},{5,197},{6,198},{7,199},{8... | collective-permute-start | bytes 393224 | tf_op jit(solution)/shard_map/ppermute | solution.py:28
  6.2 0.9 collective-permute-start.12
  7.1 1.8 collective-permute-start.11
  8.9 1.8 constant_dynamic-slice_fusion.2
  10.7 1.3 collective-permute-start.2
  12.0 1.3 collective-permute-start.1
  13.3 2.6 %bitcast_dynamic-update-slice_fusion.1 = (bf16[1024,2048]{0,1:T(8,128)(2,1)}, bf16[256,1024]{1,0:T(8,128)(2,1)S(1)}) fusion(bf16[1024,1024]{1,0:T(8,128)(2,1)S(1)} %copy-done, bf16[512,1024]{1,0:T(8,128)(2,1)} %param.6, s32[]{:T(128)S(6)} %select_n.245), kind=kOutput, calls=%fused_computation.72 | convolution fusion | flops 537133056 | bytes 3670020 | tf_op jit(solution)/shard_map/dot_general | solution.py:56
  15.8 1.5 bitcast_dynamic-update-slice_fusion
  18.0 1.1 pad_maximum_fusion.3
  19.1 1.4 collective-permute-start.8
  20.5 1.0 fusion.92
  21.6 2.0 collective-permute-start.16
  23.6 4.8 %collective-permute-start.15 = (bf16[3,256,256]{2,1,0:T(8,128)(2,1)S(1)}, bf16[3,256,256]{2,1,0:T(8,128)(2,1)S(1)}, u32[]{:S(2)}, u32[]{:S(2)}) collective-permute-start(bf16[3,256,256]{2,1,0:T(8,128)(2,1)S(1)} %get-tuple-element.28), channel_id=1, source_target_pairs={{0,8},{1,9},{2,10},{3,11},{4,12},{5,13},{6,14},{7,15},{8,0},{9,1},... | collective-permute-start | bytes 1179656 | tf_op jit(solution)/shard_map/ppermute | solution.py:28
  28.4 1.1 add_add_fusion
  29.5 7.3 %collective-permute-start.3 = (bf16[256,256]{1,0:T(8,128)(2,1)S(1)}, bf16[256,256]{1,0:T(8,128)(2,1)S(1)}, u32[]{:S(2)}, u32[]{:S(2)}) collective-permute-start(bf16[256,256]{1,0:T(8,128)(2,1)S(1)} %add_add_fusion), channel_id=1, source_target_pairs={{0,2},{1,3},{2,0},{3,1},{4,6},{5,7},{6,4},{7,5},{8,10},{9,11},{10,... | collective-permute-start | bytes 393224 | tf_op jit(solution)/shard_map/ppermute | solution.py:28
  37.5 2.8 %collective-permute-done.3 = bf16[256,256]{1,0:T(8,128)(2,1)S(1)} collective-permute-done((bf16[256,256]{1,0:T(8,128)(2,1)S(1)}, bf16[256,256]{1,0:T(8,128)(2,1)S(1)}, u32[]{:S(2)}, u32[]{:S(2)}) %collective-permute-start.3) | collective-permute-done | bytes 131104 | tf_op jit(solution)/shard_map/ppermute | solution.py:28
  40.3 0.8 fusion.91
  41.0 3.2 %collective-permute-start.6 = (bf16[2,256,256]{2,1,0:T(8,128)(2,1)}, bf16[2,256,256]{2,1,0:T(8,128)(2,1)}, u32[]{:S(2)}, u32[]{:S(2)}) collective-permute-start(bf16[2,256,256]{2,1,0:T(8,128)(2,1)} %get-tuple-element.30), channel_id=1, source_target_pairs={{0,12},{1,13},{2,14},{3,15},{4,0},{5,1},{6,2},{7,3},{8,4},{9,5},{1... | collective-permute-start | bytes 786440 | tf_op jit(solution)/shard_map/ppermute | solution.py:28
  44.3 2.0 collective-permute-start.10
  46.3 3.2 %collective-permute-done.14 = bf16[3,256,256]{2,1,0:T(8,128)(2,1)} collective-permute-done((bf16[3,256,256]{2,1,0:T(8,128)(2,1)S(1)}, bf16[3,256,256]{2,1,0:T(8,128)(2,1)}, u32[]{:S(2)}, u32[]{:S(2)}) %collective-permute-start.14) | collective-permute-done | bytes 393248 | tf_op jit(solution)/shard_map/ppermute | solution.py:28
  49.5 2.4 %collective-permute-done.6 = bf16[2,256,256]{2,1,0:T(8,128)(2,1)} collective-permute-done((bf16[2,256,256]{2,1,0:T(8,128)(2,1)}, bf16[2,256,256]{2,1,0:T(8,128)(2,1)}, u32[]{:S(2)}, u32[]{:S(2)}) %collective-permute-start.6) | collective-permute-done | bytes 262176 | tf_op jit(solution)/shard_map/ppermute | solution.py:28
  51.9 5.4 %collective-permute-start.4 = (bf16[2,256,256]{2,1,0:T(8,128)(2,1)}, bf16[2,256,256]{2,1,0:T(8,128)(2,1)}, u32[]{:S(2)}, u32[]{:S(2)}) collective-permute-start(bf16[2,256,256]{2,1,0:T(8,128)(2,1)} %get-tuple-element.30), channel_id=1, source_target_pairs={{0,4},{1,5},{2,6},{3,7},{4,8},{5,9},{6,10},{7,11},{8,12},{9,13},{1... | collective-permute-start | bytes 786440 | tf_op jit(solution)/shard_map/ppermute | solution.py:28
  57.3 1.3 pad_maximum_fusion.1
  58.8 2.7 %collective-permute-done.4 = bf16[2,256,256]{2,1,0:T(8,128)(2,1)} collective-permute-done((bf16[2,256,256]{2,1,0:T(8,128)(2,1)}, bf16[2,256,256]{2,1,0:T(8,128)(2,1)}, u32[]{:S(2)}, u32[]{:S(2)}) %collective-permute-start.4) | collective-permute-done | bytes 262176 | tf_op jit(solution)/shard_map/ppermute | solution.py:28
  61.5 1.3 fusion.93
  62.9 1.1 fusion.43
  64.0 0.8 collective-permute-done.9
  64.8 1.1 fusion.42
  65.9 18.2 %collective-permute-done.10 = bf16[2,1024,256]{1,2,0:T(8,128)(2,1)} collective-permute-done((bf16[2,1024,256]{1,2,0:T(8,128)(2,1)}, bf16[2,1024,256]{1,2,0:T(8,128)(2,1)}, u32[]{:S(2)}, u32[]{:S(2)}) %collective-permute-start.10) | collective-permute-done | bytes 1048608 | tf_op jit(solution)/shard_map/ppermute | solution.py:28
  84.0 1.1 fusion.41
  85.1 1.1 fusion.40
  86.2 1.1 fusion.39
  87.4 1.2 fusion.38
  89.0 23.8 %fusion.32 = bf16[1024,1024]{1,0:T(8,128)(2,1)S(1)} fusion(bf16[1024,2048]{0,1:T(8,128)(2,1)S(1)} %fusion.38, bf16[768,256]{1,0:T(8,128)(2,1)S(1)} %bitcast.133, bf16[768,256]{1,0:T(8,128)(2,1)S(1)} %bitcast.129, bf16[256,256]{1,0:T(8,128)(2,1)S(1)} %copy-done.13, bf16[256,256]{1,0:T(8,128)(2,1)S(1)} %copy-done.14, bf16[768,256]{1,0:T(8,128)(2,1)S(1)} %bitcast.134, ...), kind=kOutput, calls=%fused_computation.33 | convolution fusion | flops 4363124736 | bytes 10485760 | tf_op jit(solution)/shard_map/dot_general | solution.py:56
  113.5 1.9 select_convert_fusion
  115.4 3.7 %collective-permute-start.18 = (bf16[1024,256]{1,0:T(8,128)(2,1)}, bf16[1024,256]{1,0:T(8,128)(2,1)}, u32[]{:S(2)}, u32[]{:S(2)}) collective-permute-start(bf16[1024,256]{1,0:T(8,128)(2,1)} %get-tuple-element.35), channel_id=1, source_target_pairs={{0,16},{1,17},{2,18},{3,19},{4,20},{5,21},{6,22},{7,23},{8,24},{9,... | collective-permute-start | bytes 1572872 | tf_op jit(solution)/shard_map/ppermute | solution.py:28
  119.1 1.5 collective-permute-start.21
  120.6 9.4 %collective-permute-done.18 = bf16[1024,256]{1,0:T(8,128)(2,1)} collective-permute-done((bf16[1024,256]{1,0:T(8,128)(2,1)}, bf16[1024,256]{1,0:T(8,128)(2,1)}, u32[]{:S(2)}, u32[]{:S(2)}) %collective-permute-start.18) | collective-permute-done | bytes 524320 | tf_op jit(solution)/shard_map/ppermute | solution.py:28
  130.0 2.7 %add_convert_fusion.3 = (bf16[1024,256]{1,0:T(8,128)(2,1)S(1)}, bf16[1024,256]{1,0:T(8,128)(2,1)S(1)}) fusion(bf16[1024,256]{1,0:T(8,128)(2,1)} %collective-permute-done.18, bf16[1024,256]{1,0:T(8,128)(2,1)} %collective-permute-done.21, bf16[1024,1024]{1,0:T(8,128)(2,1)} %copy-done.1, bf16[4,1024,256]{2,1,0:T(8,128)(2,1)} %bitcast.116, s32[]{:T(128)S(6)} %select_n.273), kind=kOutput, calls=%fused_computation.49 | convolution fusion | flops 538443776 | bytes 4718596 | tf_op jit(solution)/shard_map/dot_general | solution.py:56
  133.4 5.0 %collective-permute-start.19 = (bf16[1024,256]{1,0:T(8,128)(2,1)S(1)}, bf16[1024,256]{1,0:T(8,128)(2,1)S(1)}, u32[]{:S(2)}, u32[]{:S(2)}) collective-permute-start(bf16[1024,256]{1,0:T(8,128)(2,1)S(1)} %get-tuple-element.20), channel_id=1, source_target_pairs={{0,16},{1,17},{2,18},{3,19},{4,20},{5,21},{6,22},{7,23},{8,24},{9,... | collective-permute-start | bytes 1572872 | tf_op jit(solution)/shard_map/ppermute | solution.py:28
  138.4 1.0 add_convert_fusion
  139.4 1.3 collective-permute-start.23
  140.7 8.2 %collective-permute-done.19 = bf16[1024,256]{1,0:T(8,128)(2,1)S(1)} collective-permute-done((bf16[1024,256]{1,0:T(8,128)(2,1)S(1)}, bf16[1024,256]{1,0:T(8,128)(2,1)S(1)}, u32[]{:S(2)}, u32[]{:S(2)}) %collective-permute-start.19) | collective-permute-done | bytes 524320 | tf_op jit(solution)/shard_map/ppermute | solution.py:28
  148.9 0.9 add_convert_fusion.2
  149.8 7.5 %collective-permute-start.20 = (bf16[1024,256]{1,0:T(8,128)(2,1)}, bf16[1024,256]{1,0:T(8,128)(2,1)}, u32[]{:S(2)}, u32[]{:S(2)}) collective-permute-start(bf16[1024,256]{1,0:T(8,128)(2,1)} %add_convert_fusion.2), channel_id=1, source_target_pairs={{0,16},{1,17},{2,18},{3,19},{4,20},{5,21},{6,22},{7,23},{8,24},{9,... | collective-permute-start | bytes 1572872 | tf_op jit(solution)/shard_map/ppermute | solution.py:28
  157.4 1.6 copy.11
  158.9 5.7 %collective-permute-done.23 = bf16[1024,256]{1,0:T(8,128)(2,1)} collective-permute-done((bf16[1024,256]{1,0:T(8,128)(2,1)}, bf16[1024,256]{1,0:T(8,128)(2,1)}, u32[]{:S(2)}, u32[]{:S(2)}) %collective-permute-start.23) | collective-permute-done | bytes 524320 | tf_op jit(solution)/shard_map/ppermute | solution.py:28
  164.6 2.1 collective-permute-done.20
  166.7 5.0 %convolution_convert_fusion = bf16[256,1024]{1,0:T(8,128)(2,1)} fusion(bf16[1024,1024]{1,0:T(8,128)(2,1)S(1)} %copy-done, f32[256,1024]{0,1:T(8,128)S(1)} %copy.11, bf16[1024,256]{1,0:T(8,128)(2,1)} %collective-permute-done.23, bf16[1024,256]{1,0:T(8,128)(2,1)} %collective-permute-done.20, bf16[1024,1024]{1,0:T(8,128)(2,1)} %copy-done.1, ...), kind=kOutput, calls=%fused_computation.38 | convolution fusion | flops 1076101120 | bytes 7340036 | tf_op jit(solution)/shard_map/dot_general | solution.py:56
  171.8 4.4 %collective-permute-start.25 = (bf16[1024,256]{0,1:T(8,128)(2,1)}, bf16[1024,256]{0,1:T(8,128)(2,1)S(1)}, u32[]{:S(2)}, u32[]{:S(2)}) collective-permute-start(bf16[1024,256]{0,1:T(8,128)(2,1)} %bitcast.124), channel_id=1, source_target_pairs={{0,16},{1,17},{2,18},{3,19},{4,20},{5,21},{6,22},{7,23},{8,24},{9,... | collective-permute-start | bytes 1572872 | tf_op jit(solution)/shard_map/ppermute | solution.py:28
  176.2 1.3 collective-permute-start.24
  177.5 7.9 %collective-permute-done.25 = bf16[1024,256]{0,1:T(8,128)(2,1)S(1)} collective-permute-done((bf16[1024,256]{0,1:T(8,128)(2,1)}, bf16[1024,256]{0,1:T(8,128)(2,1)S(1)}, u32[]{:S(2)}, u32[]{:S(2)}) %collective-permute-start.25) | collective-permute-done | bytes 524320 | tf_op jit(solution)/shard_map/ppermute | solution.py:28
  185.4 1.4 collective-permute-start.26
  186.9 2.6 %collective-permute-done.24 = bf16[1024,256]{0,1:T(8,128)(2,1)S(1)} collective-permute-done((bf16[1024,256]{0,1:T(8,128)(2,1)}, bf16[1024,256]{0,1:T(8,128)(2,1)S(1)}, u32[]{:S(2)}, u32[]{:S(2)}) %collective-permute-start.24) | collective-permute-done | bytes 524320 | tf_op jit(solution)/shard_map/ppermute | solution.py:28
  189.5 1.3 collective-permute-start.28
  190.8 1.5 collective-permute-start.27
  192.2 1.4 fusion.71
  193.6 8.5 %collective-permute-done.28 = bf16[1024,256]{0,1:T(8,128)(2,1)} collective-permute-done((bf16[1024,256]{0,1:T(8,128)(2,1)S(1)}, bf16[1024,256]{0,1:T(8,128)(2,1)}, u32[]{:S(2)}, u32[]{:S(2)}) %collective-permute-start.28) | collective-permute-done | bytes 524320 | tf_op jit(solution)/shard_map/ppermute | solution.py:28
  202.2 1.3 collective-permute-start.29
  203.4 1.4 convolution_add_fusion.2
  204.9 1.6 convolution_add_fusion.1
  206.5 7.1 %collective-permute-done.29 = bf16[1024,256]{0,1:T(8,128)(2,1)S(1)} collective-permute-done((bf16[1024,256]{0,1:T(8,128)(2,1)}, bf16[1024,256]{0,1:T(8,128)(2,1)S(1)}, u32[]{:S(2)}, u32[]{:S(2)}) %collective-permute-start.29) | collective-permute-done | bytes 524320 | tf_op jit(solution)/shard_map/ppermute | solution.py:28
  213.6 2.0 fusion.35
  (58 shorter events, 3.3 us)
Async XLA Ops:
  0.0 13.3 %copy-start = (bf16[1024,1024]{1,0:T(8,128)(2,1)S(1)}, bf16[1024,1024]{1,0:T(8,128)(2,1)}, u32[]{:S(2)}) copy-start(bf16[1024,1024]{1,0:T(8,128)(2,1)} %param.8) | copy-start | bytes 6291460
  0.0 15.8 %copy-start.6 = (bf16[512,1024]{1,0:T(8,128)(2,1)S(1)}, bf16[512,1024]{1,0:T(8,128)(2,1)}, u32[]{:S(2)}) copy-start(bf16[512,1024]{1,0:T(8,128)(2,1)} %param.6) | copy-start | bytes 3145732
  4.0 13.3 %collective-permute-start.13 = (bf16[256,256]{1,0:T(8,128)(2,1)}, bf16[256,256]{1,0:T(8,128)(2,1)S(1)}, u32[]{:S(2)}, u32[]{:S(2)}) collective-permute-start(bf16[256,256]{1,0:T(8,128)(2,1)} %get-tuple-element.10), channel_id=1, source_target_pairs={{0,192},{1,193},{2,194},{3,195},{4,196},{5,197},{6,198},{7,199},{8... | collective-permute-start | bytes 393224 | tf_op jit(solution)/shard_map/ppermute | solution.py:28
  6.2 12.9 %collective-permute-start.12 = (bf16[256,256]{1,0:T(8,128)(2,1)S(1)}, bf16[256,256]{1,0:T(8,128)(2,1)}, u32[]{:S(2)}, u32[]{:S(2)}) collective-permute-start(bf16[256,256]{1,0:T(8,128)(2,1)S(1)} %get-tuple-element.11), channel_id=1, source_target_pairs={{0,128},{1,129},{2,130},{3,131},{4,132},{5,133},{6,134},{7,135},{8... | collective-permute-start | bytes 393224 | tf_op jit(solution)/shard_map/ppermute | solution.py:28
  7.1 13.4 %collective-permute-start.11 = (bf16[256,256]{1,0:T(8,128)(2,1)S(1)}, bf16[256,256]{1,0:T(8,128)(2,1)}, u32[]{:S(2)}, u32[]{:S(2)}) collective-permute-start(bf16[256,256]{1,0:T(8,128)(2,1)S(1)} %get-tuple-element.12), channel_id=1, source_target_pairs={{0,64},{1,65},{2,66},{3,67},{4,68},{5,69},{6,70},{7,71},{8,72},{9,... | collective-permute-start | bytes 393224 | tf_op jit(solution)/shard_map/ppermute | solution.py:28
  10.7 12.9 %collective-permute-start.2 = (bf16[256,256]{1,0:T(8,128)(2,1)}, bf16[256,256]{1,0:T(8,128)(2,1)}, u32[]{:S(2)}, u32[]{:S(2)}) collective-permute-start(bf16[256,256]{1,0:T(8,128)(2,1)} %get-tuple-element.25), channel_id=1, source_target_pairs={{0,8},{1,9},{2,10},{3,11},{16,24},{17,25},{18,26},{19,27},{32,40},... | collective-permute-start | bytes 393224 | tf_op jit(solution)/shard_map/ppermute | solution.py:28
  12.0 16.4 %collective-permute-start.1 = (bf16[256,256]{1,0:T(8,128)(2,1)}, bf16[256,256]{1,0:T(8,128)(2,1)}, u32[]{:S(2)}, u32[]{:S(2)}) collective-permute-start(bf16[256,256]{1,0:T(8,128)(2,1)} %get-tuple-element.26), channel_id=1, source_target_pairs={{0,12},{1,13},{2,14},{3,15},{16,28},{17,29},{18,30},{19,31},{32,44... | collective-permute-start | bytes 393224 | tf_op jit(solution)/shard_map/ppermute | solution.py:28
  17.4 11.1 %collective-permute-start = (bf16[256,256]{1,0:T(8,128)(2,1)}, bf16[256,256]{1,0:T(8,128)(2,1)S(1)}, u32[]{:S(2)}, u32[]{:S(2)}) collective-permute-start(bf16[256,256]{1,0:T(8,128)(2,1)} %get-tuple-element.24), channel_id=1, source_target_pairs={{0,4},{1,5},{2,6},{3,7},{16,20},{17,21},{18,22},{19,23},{32,36},{3... | collective-permute-start | bytes 393224 | tf_op jit(solution)/shard_map/ppermute | solution.py:28
  19.1 43.8 %collective-permute-start.8 = (bf16[2,1024,256]{1,2,0:T(8,128)(2,1)}, bf16[2,1024,256]{1,2,0:T(8,128)(2,1)}, u32[]{:S(2)}, u32[]{:S(2)}) collective-permute-start(bf16[2,1024,256]{1,2,0:T(8,128)(2,1)} %pad_maximum_fusion.3), channel_id=1, source_target_pairs={{0,64},{1,65},{2,66},{3,67},{4,68},{5,69},{6,70},{7,71},{8,72},{9,... | collective-permute-start | bytes 3145736 | tf_op jit(solution)/shard_map/ppermute | solution.py:28
  21.5 22.7 %copy-start.4 = (bf16[3,256,256]{2,1,0:T(8,128)(2,1)}, bf16[3,256,256]{2,1,0:T(8,128)(2,1)S(1)}, u32[]{:S(2)}) copy-start(bf16[3,256,256]{2,1,0:T(8,128)(2,1)S(1)} %get-tuple-element.28) | copy-start | bytes 1179652
  21.6 19.5 %collective-permute-start.16 = (bf16[3,256,256]{2,1,0:T(8,128)(2,1)S(1)}, bf16[3,256,256]{2,1,0:T(8,128)(2,1)S(1)}, u32[]{:S(2)}, u32[]{:S(2)}) collective-permute-start(bf16[3,256,256]{2,1,0:T(8,128)(2,1)S(1)} %get-tuple-element.28), channel_id=1, source_target_pairs={{0,12},{1,13},{2,14},{3,15},{4,0},{5,1},{6,2},{7,3},{8,4},{9,5},{1... | collective-permute-start | bytes 1179656 | tf_op jit(solution)/shard_map/ppermute | solution.py:28
  23.6 20.7 %collective-permute-start.15 = (bf16[3,256,256]{2,1,0:T(8,128)(2,1)S(1)}, bf16[3,256,256]{2,1,0:T(8,128)(2,1)S(1)}, u32[]{:S(2)}, u32[]{:S(2)}) collective-permute-start(bf16[3,256,256]{2,1,0:T(8,128)(2,1)S(1)} %get-tuple-element.28), channel_id=1, source_target_pairs={{0,8},{1,9},{2,10},{3,11},{4,12},{5,13},{6,14},{7,15},{8,0},{9,1},... | collective-permute-start | bytes 1179656 | tf_op jit(solution)/shard_map/ppermute | solution.py:28
  29.5 10.7 %collective-permute-start.3 = (bf16[256,256]{1,0:T(8,128)(2,1)S(1)}, bf16[256,256]{1,0:T(8,128)(2,1)S(1)}, u32[]{:S(2)}, u32[]{:S(2)}) collective-permute-start(bf16[256,256]{1,0:T(8,128)(2,1)S(1)} %add_add_fusion), channel_id=1, source_target_pairs={{0,2},{1,3},{2,0},{3,1},{4,6},{5,7},{6,4},{7,5},{8,10},{9,11},{10,... | collective-permute-start | bytes 393224 | tf_op jit(solution)/shard_map/ppermute | solution.py:28
  36.8 28.0 %collective-permute-start.9 = (bf16[2,1024,256]{1,2,0:T(8,128)(2,1)}, bf16[2,1024,256]{1,2,0:T(8,128)(2,1)}, u32[]{:S(2)}, u32[]{:S(2)}) collective-permute-start(bf16[2,1024,256]{1,2,0:T(8,128)(2,1)} %pad_maximum_fusion.3), channel_id=1, source_target_pairs={{0,128},{1,129},{2,130},{3,131},{4,132},{5,133},{6,134},{7,135},{8... | collective-permute-start | bytes 3145736 | tf_op jit(solution)/shard_map/ppermute | solution.py:28
  40.3 9.2 %collective-permute-start.14 = (bf16[3,256,256]{2,1,0:T(8,128)(2,1)S(1)}, bf16[3,256,256]{2,1,0:T(8,128)(2,1)}, u32[]{:S(2)}, u32[]{:S(2)}) collective-permute-start(bf16[3,256,256]{2,1,0:T(8,128)(2,1)S(1)} %get-tuple-element.28), channel_id=1, source_target_pairs={{0,4},{1,5},{2,6},{3,7},{4,8},{5,9},{6,10},{7,11},{8,12},{9,13},{1... | collective-permute-start | bytes 1179656 | tf_op jit(solution)/shard_map/ppermute | solution.py:28
  41.0 10.9 %collective-permute-start.6 = (bf16[2,256,256]{2,1,0:T(8,128)(2,1)}, bf16[2,256,256]{2,1,0:T(8,128)(2,1)}, u32[]{:S(2)}, u32[]{:S(2)}) collective-permute-start(bf16[2,256,256]{2,1,0:T(8,128)(2,1)} %get-tuple-element.30), channel_id=1, source_target_pairs={{0,12},{1,13},{2,14},{3,15},{4,0},{5,1},{6,2},{7,3},{8,4},{9,5},{1... | collective-permute-start | bytes 786440 | tf_op jit(solution)/shard_map/ppermute | solution.py:28
  44.3 39.8 %collective-permute-start.10 = (bf16[2,1024,256]{1,2,0:T(8,128)(2,1)}, bf16[2,1024,256]{1,2,0:T(8,128)(2,1)}, u32[]{:S(2)}, u32[]{:S(2)}) collective-permute-start(bf16[2,1024,256]{1,2,0:T(8,128)(2,1)} %pad_maximum_fusion.3), channel_id=1, source_target_pairs={{0,192},{1,193},{2,194},{3,195},{4,196},{5,197},{6,198},{7,199},{8... | collective-permute-start | bytes 3145736 | tf_op jit(solution)/shard_map/ppermute | solution.py:28
  49.5 9.2 %collective-permute-start.5 = (bf16[2,256,256]{2,1,0:T(8,128)(2,1)}, bf16[2,256,256]{2,1,0:T(8,128)(2,1)}, u32[]{:S(2)}, u32[]{:S(2)}) collective-permute-start(bf16[2,256,256]{2,1,0:T(8,128)(2,1)} %get-tuple-element.30), channel_id=1, source_target_pairs={{0,8},{1,9},{2,10},{3,11},{4,12},{5,13},{6,14},{7,15},{8,0},{9,1},... | collective-permute-start | bytes 786440 | tf_op jit(solution)/shard_map/ppermute | solution.py:28
  51.9 9.6 %collective-permute-start.4 = (bf16[2,256,256]{2,1,0:T(8,128)(2,1)}, bf16[2,256,256]{2,1,0:T(8,128)(2,1)}, u32[]{:S(2)}, u32[]{:S(2)}) collective-permute-start(bf16[2,256,256]{2,1,0:T(8,128)(2,1)} %get-tuple-element.30), channel_id=1, source_target_pairs={{0,4},{1,5},{2,6},{3,7},{4,8},{5,9},{6,10},{7,11},{8,12},{9,13},{1... | collective-permute-start | bytes 786440 | tf_op jit(solution)/shard_map/ppermute | solution.py:28
  57.3 5.6 %copy-start.15 = (bf16[1024,2048]{0,1:T(8,128)(2,1)S(1)}, bf16[1024,2048]{0,1:T(8,128)(2,1)}, u32[]{:S(2)}) copy-start(bf16[1024,2048]{0,1:T(8,128)(2,1)} %get-tuple-element.33) | copy-start | bytes 12582916
  58.7 30.1 %collective-permute-start.17 = (bf16[4,3,256,256]{3,2,1,0:T(8,128)(2,1)S(1)}, bf16[4,3,256,256]{3,2,1,0:T(8,128)(2,1)S(1)}, u32[]{:S(2)}, u32[]{:S(2)}) collective-permute-start(bf16[4,3,256,256]{3,2,1,0:T(8,128)(2,1)S(1)} %pad_maximum_fusion.1), channel_id=1, source_target_pairs={{0,1},{1,0},{2,3},{3,2},{4,5},{5,4},{6,7},{7,6},{8,9},{9,8},{10,11... | collective-permute-start | bytes 4718600 | tf_op jit(solution)/shard_map/ppermute | solution.py:28
  62.8 25.7 %collective-permute-start.7 = (bf16[2,4,256,256]{3,2,1,0:T(8,128)(2,1)S(1)}, bf16[2,4,256,256]{3,2,1,0:T(8,128)(2,1)S(1)}, u32[]{:S(2)}, u32[]{:S(2)}) collective-permute-start(bf16[2,4,256,256]{3,2,1,0:T(8,128)(2,1)S(1)} %get-tuple-element.23), channel_id=1, source_target_pairs={{0,1},{1,0},{2,3},{3,2},{4,5},{5,4},{6,7},{7,6},{8,9},{9,8},{10,11... | collective-permute-start | bytes 3145736 | tf_op jit(solution)/shard_map/ppermute | solution.py:28
  87.3 1.6 copy-start.5
  87.3 1.6 copy-start.7
  87.3 1.6 copy-start.8
  87.3 1.6 copy-start.9
  87.3 1.6 copy-start.10
  87.3 1.6 copy-start.11
  87.3 1.6 copy-start.12
  87.3 1.6 copy-start.13
  87.4 1.6 copy-start.14
  88.8 24.7 %copy-start.2 = (bf16[2,2,4,256,256]{4,3,2,1,0:T(8,128)(2,1)}, bf16[2,2,4,256,256]{4,3,2,1,0:T(8,128)(2,1)S(1)}, u32[]{:S(2)}) copy-start(bf16[2,2,4,256,256]{4,3,2,1,0:T(8,128)(2,1)S(1)} %pad_maximum_fusion) | copy-start | bytes 6291460
  112.8 2.6 %copy-start.1 = (bf16[1024,1024]{1,0:T(8,128)(2,1)}, bf16[1024,1024]{1,0:T(8,128)(2,1)S(1)}, u32[]{:S(2)}) copy-start(bf16[1024,1024]{1,0:T(8,128)(2,1)S(1)} %fusion.32) | copy-start | bytes 6291460
  115.4 14.6 %collective-permute-start.18 = (bf16[1024,256]{1,0:T(8,128)(2,1)}, bf16[1024,256]{1,0:T(8,128)(2,1)}, u32[]{:S(2)}, u32[]{:S(2)}) collective-permute-start(bf16[1024,256]{1,0:T(8,128)(2,1)} %get-tuple-element.35), channel_id=1, source_target_pairs={{0,16},{1,17},{2,18},{3,19},{4,20},{5,21},{6,22},{7,23},{8,24},{9,... | collective-permute-start | bytes 1572872 | tf_op jit(solution)/shard_map/ppermute | solution.py:28
  119.1 10.8 %collective-permute-start.21 = (bf16[1024,256]{1,0:T(8,128)(2,1)}, bf16[1024,256]{1,0:T(8,128)(2,1)}, u32[]{:S(2)}, u32[]{:S(2)}) collective-permute-start(bf16[1024,256]{1,0:T(8,128)(2,1)} %get-tuple-element.35), channel_id=1, source_target_pairs={{48,32},{49,33},{50,34},{51,35},{52,36},{53,37},{54,38},{55,39},{5... | collective-permute-start | bytes 1572872 | tf_op jit(solution)/shard_map/ppermute | solution.py:28
  120.6 17.8 %copy-start.3 = (f32[1024,256]{1,0:T(8,128)S(1)}, f32[1024,256]{1,0:T(8,128)}, u32[]{:S(2)}) copy-start(f32[1024,256]{1,0:T(8,128)} %get-tuple-element.36) | copy-start | bytes 3145732
  132.7 5.7 %collective-permute-start.22 = (bf16[1024,256]{1,0:T(8,128)(2,1)S(1)}, bf16[1024,256]{1,0:T(8,128)(2,1)S(1)}, u32[]{:S(2)}, u32[]{:S(2)}) collective-permute-start(bf16[1024,256]{1,0:T(8,128)(2,1)S(1)} %get-tuple-element.21), channel_id=1, source_target_pairs={{32,16},{33,17},{34,18},{35,19},{36,20},{37,21},{38,22},{39,23},{4... | collective-permute-start | bytes 1572872 | tf_op jit(solution)/shard_map/ppermute | solution.py:28
  133.4 15.5 %collective-permute-start.19 = (bf16[1024,256]{1,0:T(8,128)(2,1)S(1)}, bf16[1024,256]{1,0:T(8,128)(2,1)S(1)}, u32[]{:S(2)}, u32[]{:S(2)}) collective-permute-start(bf16[1024,256]{1,0:T(8,128)(2,1)S(1)} %get-tuple-element.20), channel_id=1, source_target_pairs={{0,16},{1,17},{2,18},{3,19},{4,20},{5,21},{6,22},{7,23},{8,24},{9,... | collective-permute-start | bytes 1572872 | tf_op jit(solution)/shard_map/ppermute | solution.py:28
  139.4 25.2 %collective-permute-start.23 = (bf16[1024,256]{1,0:T(8,128)(2,1)}, bf16[1024,256]{1,0:T(8,128)(2,1)}, u32[]{:S(2)}, u32[]{:S(2)}) collective-permute-start(bf16[1024,256]{1,0:T(8,128)(2,1)} %add_convert_fusion), channel_id=1, source_target_pairs={{16,0},{17,1},{18,2},{19,3},{20,4},{21,5},{22,6},{23,7},{24,8},{25... | collective-permute-start | bytes 1572872 | tf_op jit(solution)/shard_map/ppermute | solution.py:28
  149.8 16.9 %collective-permute-start.20 = (bf16[1024,256]{1,0:T(8,128)(2,1)}, bf16[1024,256]{1,0:T(8,128)(2,1)}, u32[]{:S(2)}, u32[]{:S(2)}) collective-permute-start(bf16[1024,256]{1,0:T(8,128)(2,1)} %add_convert_fusion.2), channel_id=1, source_target_pairs={{0,16},{1,17},{2,18},{3,19},{4,20},{5,21},{6,22},{7,23},{8,24},{9,... | collective-permute-start | bytes 1572872 | tf_op jit(solution)/shard_map/ppermute | solution.py:28
  171.8 13.6 %collective-permute-start.25 = (bf16[1024,256]{0,1:T(8,128)(2,1)}, bf16[1024,256]{0,1:T(8,128)(2,1)S(1)}, u32[]{:S(2)}, u32[]{:S(2)}) collective-permute-start(bf16[1024,256]{0,1:T(8,128)(2,1)} %bitcast.124), channel_id=1, source_target_pairs={{0,16},{1,17},{2,18},{3,19},{4,20},{5,21},{6,22},{7,23},{8,24},{9,... | collective-permute-start | bytes 1572872 | tf_op jit(solution)/shard_map/ppermute | solution.py:28
  176.2 13.3 %collective-permute-start.24 = (bf16[1024,256]{0,1:T(8,128)(2,1)}, bf16[1024,256]{0,1:T(8,128)(2,1)S(1)}, u32[]{:S(2)}, u32[]{:S(2)}) collective-permute-start(bf16[1024,256]{0,1:T(8,128)(2,1)} %bitcast.125), channel_id=1, source_target_pairs={{16,0},{17,1},{18,2},{19,3},{20,4},{21,5},{22,6},{23,7},{24,8},{25... | collective-permute-start | bytes 1572872 | tf_op jit(solution)/shard_map/ppermute | solution.py:28
  185.4 5.3 %collective-permute-start.26 = (bf16[1024,256]{0,1:T(8,128)(2,1)S(1)}, bf16[1024,256]{0,1:T(8,128)(2,1)}, u32[]{:S(2)}, u32[]{:S(2)}) collective-permute-start(bf16[1024,256]{0,1:T(8,128)(2,1)S(1)} %collective-permute-done.25), channel_id=1, source_target_pairs={{16,32},{17,33},{18,34},{19,35},{20,36},{21,37},{22,38},{23,39},{2... | collective-permute-start | bytes 1572872 | tf_op jit(solution)/shard_map/ppermute | solution.py:28
  189.5 12.7 %collective-permute-start.28 = (bf16[1024,256]{0,1:T(8,128)(2,1)S(1)}, bf16[1024,256]{0,1:T(8,128)(2,1)}, u32[]{:S(2)}, u32[]{:S(2)}) collective-permute-start(bf16[1024,256]{0,1:T(8,128)(2,1)S(1)} %collective-permute-done.24), channel_id=1, source_target_pairs={{16,0},{17,1},{18,2},{19,3},{20,4},{21,5},{22,6},{23,7},{24,8},{25... | collective-permute-start | bytes 1572872 | tf_op jit(solution)/shard_map/ppermute | solution.py:28
  190.8 12.7 %collective-permute-start.27 = (bf16[1024,256]{0,1:T(8,128)(2,1)}, bf16[1024,256]{0,1:T(8,128)(2,1)}, u32[]{:S(2)}, u32[]{:S(2)}) collective-permute-start(bf16[1024,256]{0,1:T(8,128)(2,1)} %collective-permute-done.26), channel_id=1, source_target_pairs={{32,48},{33,49},{34,50},{35,51},{36,52},{37,53},{38,54},{39,55},{4... | collective-permute-start | bytes 1572872 | tf_op jit(solution)/shard_map/ppermute | solution.py:28
  202.2 11.4 %collective-permute-start.29 = (bf16[1024,256]{0,1:T(8,128)(2,1)}, bf16[1024,256]{0,1:T(8,128)(2,1)S(1)}, u32[]{:S(2)}, u32[]{:S(2)}) collective-permute-start(bf16[1024,256]{0,1:T(8,128)(2,1)} %collective-permute-done.28), channel_id=1, source_target_pairs={{16,0},{17,1},{18,2},{19,3},{20,4},{21,5},{22,6},{23,7},{24,8},{25... | collective-permute-start | bytes 1572872 | tf_op jit(solution)/shard_map/ppermute | solution.py:28

commit v2 on v0

v2 whole, which is shorter than its diff:
```python
import functools

import jax
import jax.numpy as jnp
from jax import lax
from jax.experimental import pallas as pl
from jax.experimental.pallas import tpu as pltpu
from jax.sharding import PartitionSpec as P

DAMPING = 0.05
NX, NY, NZ = 4, 4, 4
BF = jnp.bfloat16
F32 = jnp.float32


def moved(block, place):
    route = []
    for y in range(NY):
        for z in range(NZ):
            for x in range(NX):
                for h in range(2):
                    for c in range(2):
                        tx, ty, tz, th, tc = place(x, y, z, h, c)
                        source = (y * NZ + z) * 16 + x * 4 + h * 2 + c
                        target = (ty % NY * NZ + tz % NZ) * 16 + tx % NX * 4 + th * 2 + tc
                        route.append((source, target))
    return lax.ppermute(block, ("dp", "owner"), route)


def along_x(block, k):
    return moved(block, lambda x, y, z, h, c: (x + k, y, z, h, c))


def along_y(block, k):
    return moved(block, lambda x, y, z, h, c: (x, y + k, z, h, c))


def across_z(block, e):
    return moved(block, lambda x, y, z, h, c: (x, y, z ^ e, h, c))


def crossed(block, flip):
    return moved(block, lambda x, y, z, h, c: (y, x, z, h ^ flip, c))


def other_core(block):
    return moved(block, lambda x, y, z, h, c: (x, y, z, h, 1 - c))


def dot(a, b, dims):
    return lax.dot_general(a, b, ((dims[:1], dims[1:]), ((), ())), preferred_element_type=F32)


def vmem(count):
    return [pl.BlockSpec(memory_space=pltpu.VMEM)] * count


def scalars():
    return [pl.BlockSpec(memory_space=pltpu.SMEM)]


def product_kernel(start, place, g0, g1, g2, g3, mine, rest, *refs):
    count = len(refs) - 12
    own, other, outs = refs[0:4], refs[4:8], refs[8 : 8 + count]
    g_held, m_held, x_held, sems = refs[8 + count :]
    x = place[3]
    half = mine.shape[0]
    rows = outs[0].shape[0]
    total = count * rows
    copies = []

    def fetch(source, target):
        copies.append(pltpu.make_async_copy(source, target, sems.at[len(copies)]))
        copies[-1].start()

    fetch(g0.at[pl.ds(start, total)], g_held.at[0])
    fetch(mine, m_held.at[0])
    fetch(rest, m_held.at[1])
    for k, g in enumerate((g1, g2, g3)):
        fetch(g.at[pl.ds(start, total)], g_held.at[k + 1])
    first = len(copies)
    for j in range(4):
        fetch(own[j], x_held.at[0, j])
        fetch(other[j], x_held.at[1, j])
    for copy in copies[:first]:
        copy.wait()
    for j in range(4):
        cols = pl.ds(pl.multiple_of(lax.rem(x + 4 - j, 4) * half, half), half)
        copies[first + 2 * j].wait()
        copies[first + 2 * j + 1].wait()
        for n, out in enumerate(outs):
            at = slice(n * rows, (n + 1) * rows)
            acc = dot(g_held[0, at, 0:half], m_held[0, :, cols], (1, 0))
            acc += dot(g_held[0, at, half : 2 * half], m_held[1, :, cols], (1, 0))
            for k in range(3):
                acc += dot(g_held[k + 1, at, 0:half], x_held[0, j, k], (1, 0))
                acc += dot(g_held[k + 1, at, half : 2 * half], x_held[1, j, k], (1, 0))
            out[:, j * half : (j + 1) * half] = acc.astype(BF)


def product(place, start, count, rows, grads, mine, rest, own, other):
    tok = grads[0].shape[1]
    half, width = mine.shape
    return pl.pallas_call(
        functools.partial(product_kernel, start),
        out_shape=[jax.ShapeDtypeStruct((rows, width), BF)] * count,
        in_specs=scalars() + [pl.BlockSpec(memory_space=pl.ANY)] * 14,
        out_specs=vmem(count),
        scratch_shapes=[
            pltpu.VMEM((4, count * rows, tok), BF),
            pltpu.VMEM((2, half, width), BF),
            pltpu.VMEM((2, 4) + own[0].shape, BF),
            pltpu.SemaphoreType.DMA((14,)),
        ],
        compiler_params=pltpu.CompilerParams(vmem_limit_bytes=16 << 20),
        cost_estimate=pl.CostEstimate(
            flops=8 * count * rows * tok * width, bytes_accessed=6 << 20, transcendentals=0
        ),
    )(place, *grads, mine, rest, *own, *other)


def middle_kernel(place, m0, m1, m2, inverse, *refs):
    own, other, out, summed, scaled, held, sems = refs[0:4], refs[4:8], *refs[8:]
    z, h, c, x = place[0], place[1], place[2], place[3]
    quarter = m0.shape[0]
    copies = []
    for n, ref in enumerate(own + other):
        copies.append(pltpu.make_async_copy(ref, held.at[n // 4, n % 4], sems.at[n]))
        copies[-1].start()
    total = m0[...].astype(F32) + m1[...].astype(F32) + m2[...].astype(F32)
    summed[...] = total.astype(BF)
    for copy in copies:
        copy.wait()
    bases = [(core, side) for core in (0, 1) for side in (0, 1)]
    for n, (core, side) in enumerate(bases):
        acc = None
        for j in range(4):
            term = dot(summed[:, j * quarter : (j + 1) * quarter], held[core, j, side], (1, 0))
            acc = term if acc is None else acc + term
        q = 2 * jnp.bitwise_xor(h, side) + jnp.bitwise_xor(c, core)
        scaled[n] = (acc * inverse[jnp.bitwise_xor(z, q)].astype(F32)).astype(BF)
    for j in range(4):
        acc = None
        for n, (core, side) in enumerate(bases):
            term = dot(held[core, j, side], scaled[n], (1, 1))
            acc = term if acc is None else acc + term
        out[jnp.bitwise_xor(z, lax.rem(x + 4 - j, 4))] = acc.astype(BF)


def middle(place, sums, inverse, own, other):
    quarter, width = sums[0].shape
    return pl.pallas_call(
        middle_kernel,
        out_shape=jax.ShapeDtypeStruct((4, quarter, quarter), BF),
        in_specs=scalars() + vmem(4) + [pl.BlockSpec(memory_space=pl.ANY)] * 8,
        out_specs=pl.BlockSpec(memory_space=pltpu.VMEM),
        scratch_shapes=[
            pltpu.VMEM((quarter, width), BF),
            pltpu.VMEM((4, quarter, quarter), BF),
            pltpu.VMEM((2, 4) + own[0].shape, BF),
            pltpu.SemaphoreType.DMA((8,)),
        ],
        compiler_params=pltpu.CompilerParams(vmem_limit_bytes=16 << 20),
        cost_estimate=pl.CostEstimate(
            flops=4 * quarter * width * width, bytes_accessed=6 << 20, transcendentals=0
        ),
    )(place, *sums, inverse, *own, *other)


def last_kernel(place, basis, b0, b1, b2, b3, out):
    z = place[0]
    quarter = b0.shape[1]
    for n in range(0, out.shape[1], 512):
        acc = None
        for e, b in enumerate((b0, b1, b2, b3)):
            at = pl.multiple_of(jnp.bitwise_xor(z, e) * quarter, quarter)
            term = dot(b[...], basis[n : n + 512, pl.ds(at, quarter)], (1, 1))
            acc = term if acc is None else acc + term
        out[:, n : n + 512] = acc.astype(BF)


def last(place, basis, parts):
    rows = parts[0].shape[0]
    width = basis.shape[0]
    return pl.pallas_call(
        last_kernel,
        out_shape=jax.ShapeDtypeStruct((rows, width), BF),
        in_specs=scalars() + vmem(5),
        out_specs=pl.BlockSpec(memory_space=pltpu.VMEM),
        compiler_params=pltpu.CompilerParams(vmem_limit_bytes=14 << 20),
        cost_estimate=pl.CostEstimate(
            flops=2 * rows * width * width, bytes_accessed=3 << 20, transcendentals=0
        ),
    )(place, basis, *parts)


def on_device(inputs, out_grads, basis_in, basis_out, eigenvalues):
    tok = inputs.shape[0]
    block = basis_in.shape[0]
    quarter = block // 4
    half = tok // 2
    owner = lax.axis_index("owner")
    data = lax.axis_index("dp")
    x, h, c = owner // 4, owner // 2 % 2, owner % 2
    y, z = data // NZ, data % NZ
    place = jnp.stack([z, h, c, x]).astype(jnp.int32)

    def after(value, *earlier):
        return lax.optimization_barrier((value,) + earlier)[0]

    def piece(rows, b, col, width):
        return lax.dynamic_slice(inputs, (rows * half, b % NY * block + col), (half, width))

    got = {k: along_y(piece(c, y + k, x * quarter, quarter), k) for k in (1, 3, 2)}

    og = jnp.concatenate(
        [
            lax.dynamic_slice_in_dim(out_grads, c * half, half, 0),
            lax.dynamic_slice_in_dim(out_grads, (1 - c) * half, half, 0),
        ],
        0,
    )
    def turned(group):
        cols = [
            lax.dynamic_slice_in_dim(basis_out, (z ^ e) * quarter, quarter, 1) for e in group
        ]
        return dot(jnp.concatenate(cols, 1), og, (0, 1)).astype(BF)

    def spread(gt, *earlier):
        go = after(gt, *earlier)
        one = {k: along_y(go, k) for k in (1, 3, 2)}
        return [gt] + [one[k] for k in (1, 2, 3)]

    upper = spread(turned((3, 2)), got[1])
    lower = spread(turned((1, 0)), upper[1])

    def over_x(pieces):
        got = {j: along_x(pieces, j) for j in (1, 3)}
        got[2] = along_x(after(pieces, got[1]), 2)
        own = [pieces] + [got[j] for j in (1, 2, 3)]
        return own, [other_core(o) for o in own]

    own, other = over_x(jnp.stack([got[1], got[2], got[3]]))
    mine, rest = piece(c, y, 0, block), piece(1 - c, y, 0, block)

    inverse = (1.0 / (eigenvalues + DAMPING)).T.astype(BF)

    def level(e):
        return lax.dynamic_slice_in_dim(inverse, (z ^ e) * quarter, quarter, 0)

    inverse = jnp.stack([level(0)] + [across_z(after(level(e), own[1]), e) for e in (1, 2, 3)])

    local = (mine, rest, own, other)
    (m3,) = product(place, 0, 1, quarter, upper, *local)
    near3 = across_z(after(m3, inverse), 1)
    (m2,) = product(place, quarter, 1, quarter, upper, *local)
    far2 = (m2.astype(F32) + near3.astype(F32)).astype(BF)
    m1, m0 = product(place, 0, 2, quarter, lower, *local)
    near1 = across_z(m1, 1)

    at = lax.dynamic_slice_in_dim(after(basis_in, far2), y * quarter, quarter, 0)
    a_own, a_other = over_x(jnp.stack([crossed(at, 0), crossed(at, 1)]))
    parts = middle(place, [m0, near1, across_z(far2, 2)], inverse, a_own, a_other)
    parts = [parts[0]] + [across_z(parts[e], e) for e in (1, 2, 3)]
    return last(place, basis_out, parts)


def solution(mesh):
    placed = (P("dp", None), P("dp", "owner"), P(None, "owner"), P(None, "owner"), P("dp", "owner"))
    return jax.shard_map(
        on_device, mesh=mesh, in_specs=placed, out_specs=P("dp", "owner"), check_vma=False
    )
```

time: 374 us -> 153 us (0.41)
  waiting for transfers between devices: 334 us -> 48.6 us
  starting transfers between devices: 2.26 us -> 61.2 us
  Pallas kernels: 0 us -> 19.5 us
  matrix products: 18.4 us -> 3.1 us
  between operations: 13.2 us -> 0.39 us
  local copies, waits for them, and re-layouts: 2.24 us -> 13.9 us
    reduce_scatter x1 -> x0, waiting for transfers between devices: 180 us -> none  [on_device(): lax.psum_scatter(partials.astype(jnp.bfloat16), 'dp', scatter_dimension=0...]
    all_gather x2 -> x0, waiting for transfers between devices: 131 us -> none  [the longest x1 81.7 us: on_device(): lax.all_gather(rotated_own, 'owner', axis=1, tiled=True)]
    ppermute x2 -> x34, starting transfers between devices: 2.17 us -> 61.2 us  [moved(): return lax.ppermute(block, ('dp', 'owner'), route)]
    ppermute x2 -> x34, waiting for transfers between devices: 22.6 us -> 48.6 us  [moved(): return lax.ppermute(block, ('dp', 'owner'), route)]
    pallas_call x0 -> x5, Pallas kernels: none -> 19.5 us  [the longest x3 15.1 us: product(): pl.pallas_call(functools.partial(product_kernel, start), out_shape=[jax.S...]
    dot_general x4 -> x2, matrix products: 18.4 us -> 3.1 us  [dot(): lax.dot_general(a, b, ((dims[:1], dims[1:]), ((), ())), preferred_element...]
    unnamed x6 -> x53, local copies, waits for them, and re-layouts: 0.69 us -> 7.93 us
  transfers between devices with their start and end apart: 5 -> 34, of which waited for: 5 -> 16; matrix products, arithmetic and copies ran while one was open for 2% -> 9% of each run, Pallas kernels for 0% -> 6%
where the time goes in v2:
time: 153 us; the launch traced here: 150 us
  starting transfers between devices  61.2 us (40%)
  waiting for transfers between devices  48.6 us (32%)
  Pallas kernels  19.5 us (13%)
  local copies, waits for them, and re-layouts  13.9 us (9%)
  other arithmetic  3.76 us (2%)
  matrix products  3.1 us (2%)
    ppermute x34, starting transfers between devices, moved(): return lax.ppermute(block, ('dp', 'owner'), route)  61.2 us
    ppermute x34, waiting for transfers between devices, moved(): return lax.ppermute(block, ('dp', 'owner'), route)  48.6 us
    pallas_call x3, Pallas kernels, product(): pl.pallas_call(functools.partial(product_kernel, start), out_shape=[jax.S...  15.1 us
    unnamed x53, local copies, waits for them, and re-layouts  7.93 us
    dot_general x2, matrix products, dot(): lax.dot_general(a, b, ((dims[:1], dims[1:]), ((), ())), preferred_element...  3.1 us
  transfers between devices with their start and end apart: 34, of which 16 were waited for; matrix products, arithmetic and copies ran while one was open for 9% of the time, Pallas kernels for 6%

profile of v2, /device:TPU:8, one launch (start us, length us, event | category | flops | bytes accessed | tf_op | source)
XLA Modules:
  0.0 150.4 jit_solution(6246825248386017602)
XLA Ops:
  0.0 1.2 fusion.8
  1.2 1.7 %collective-permute-start = (bf16[256,256]{1,0:T(8,128)(2,1)S(1)}, bf16[256,256]{1,0:T(8,128)(2,1)S(1)}, u32[]{:S(2)}, u32[]{:S(2)}) collective-permute-start(bf16[256,256]{1,0:T(8,128)(2,1)S(1)} %get-tuple-element.28), channel_id=1, source_target_pairs={{0,64},{1,65},{2,66},{3,67},{4,68},{5,69},{6,70},{7,71},{8,72},{9,... | collective-permute-start | bytes 393224 | tf_op jit(solution)/shard_map/ppermute | solution.py:27
  2.9 0.7 collective-permute-start.6
  3.6 2.0 %collective-permute-start.5 = (bf16[256,256]{1,0:T(8,128)(2,1)S(1)}, bf16[256,256]{1,0:T(8,128)(2,1)S(1)}, u32[]{:S(2)}, u32[]{:S(2)}) collective-permute-start(bf16[256,256]{1,0:T(8,128)(2,1)S(1)} %get-tuple-element.27), channel_id=1, source_target_pairs={{0,128},{1,129},{2,130},{3,131},{4,132},{5,133},{6,134},{7,135},{8... | collective-permute-start | bytes 393224 | tf_op jit(solution)/shard_map/ppermute | solution.py:27
  5.6 0.9 collective-permute-done
  6.5 2.1 %collective-permute-done.6 = bf16[256,256]{1,0:T(8,128)(2,1)S(1)} collective-permute-done((bf16[256,256]{1,0:T(8,128)(2,1)S(1)}, bf16[256,256]{1,0:T(8,128)(2,1)S(1)}, u32[]{:S(2)}, u32[]{:S(2)}) %collective-permute-start.6) | collective-permute-done | bytes 131104 | tf_op jit(solution)/shard_map/ppermute | solution.py:27
  8.6 2.8 %collective-permute-done.5 = bf16[256,256]{1,0:T(8,128)(2,1)S(1)} collective-permute-done((bf16[256,256]{1,0:T(8,128)(2,1)S(1)}, bf16[256,256]{1,0:T(8,128)(2,1)S(1)}, u32[]{:S(2)}, u32[]{:S(2)}) %collective-permute-start.5) | collective-permute-done | bytes 131104 | tf_op jit(solution)/shard_map/ppermute | solution.py:27
  11.4 1.6 %collective-permute-start.7 = (bf16[3,256,256]{2,1,0:T(8,128)(2,1)S(1)}, bf16[3,256,256]{2,1,0:T(8,128)(2,1)}, u32[]{:S(2)}, u32[]{:S(2)}) collective-permute-start(bf16[3,256,256]{2,1,0:T(8,128)(2,1)S(1)} %pad_maximum_fusion.4.refs_0_), channel_id=1, source_target_pairs={{0,4},{1,5},{2,6},{3,7},{4,8},{5,9},{6,10},{7,11},{8,12},{9,13},{1... | collective-permute-start | bytes 1179656 | tf_op jit(solution)/shard_map/ppermute | solution.py:27
  13.0 1.3 constant_dynamic-slice_fusion.4
  14.3 1.3 constant_dynamic-slice_fusion.2
  15.6 1.5 %convolution_convert_fusion.g0 = bf16[512,512]{1,0:T(8,128)(2,1)} fusion(bf16[1024,256]{1,0:T(8,128)(2,1)S(1)} %get-tuple-element.35, bf16[1024,256]{1,0:T(8,128)(2,1)S(1)} %get-tuple-element.32, bf16[256,1024]{1,0:T(8,128)(2,1)S(1)} %get-tuple-element.37, bf16[256,1024]{1,0:T(8,128)(2,1)S(1)} %get-tuple-element.36), kind=kOutput, calls=%fused_computation | convolution fusion | flops 541327360 | bytes 2621440 | tf_op jit(solution)/shard_map/dot_general | solution.py:51
  17.1 2.6 %copy.6 = f32[256,1024]{0,1:T(8,128)} copy(f32[256,1024]{1,0:T(8,128)} %param.9) | data formatting | bytes 2097152 | tf_op args[4]
  19.7 1.7 %collective-permute-start.9 = (bf16[3,256,256]{2,1,0:T(8,128)(2,1)S(1)}, bf16[3,256,256]{2,1,0:T(8,128)(2,1)}, u32[]{:S(2)}, u32[]{:S(2)}) collective-permute-start(bf16[3,256,256]{2,1,0:T(8,128)(2,1)S(1)} %pad_maximum_fusion.4.refs_0_), channel_id=1, source_target_pairs={{0,12},{1,13},{2,14},{3,15},{4,0},{5,1},{6,2},{7,3},{8,4},{9,5},{1... | collective-permute-start | bytes 1179656 | tf_op jit(solution)/shard_map/ppermute | solution.py:27
  21.5 0.7 collective-permute-done.7.refs_1_
  22.2 1.8 %collective-permute-start.8 = (bf16[3,256,256]{2,1,0:T(8,128)(2,1)S(1)}, bf16[3,256,256]{2,1,0:T(8,128)(2,1)}, u32[]{:S(2)}, u32[]{:S(2)}) collective-permute-start(bf16[3,256,256]{2,1,0:T(8,128)(2,1)S(1)} %pad_maximum_fusion.4.refs_0_), channel_id=1, source_target_pairs={{0,8},{1,9},{2,10},{3,11},{4,12},{5,13},{6,14},{7,15},{8,0},{9,1},... | collective-permute-start | bytes 1179656 | tf_op jit(solution)/shard_map/ppermute | solution.py:27
  24.0 1.4 divide_convert_fusion
  25.4 0.7 dynamic-slice_bitcast_fusion.3
  26.1 4.6 %collective-permute-start.19 = (bf16[256,256]{1,0:T(8,128)(2,1)S(1)}, bf16[256,256]{1,0:T(8,128)(2,1)S(1)}, u32[]{:S(2)}, u32[]{:S(2)}) collective-permute-start(bf16[256,256]{1,0:T(8,128)(2,1)S(1)} %get-tuple-element.23), channel_id=1, source_target_pairs={{0,48},{1,49},{2,50},{3,51},{4,52},{5,53},{6,54},{7,55},{8,56},{9,... | collective-permute-start | bytes 393224 | tf_op jit(solution)/shard_map/ppermute | solution.py:27
  30.7 5.8 %collective-permute-done.9.refs_3_ = bf16[3,256,256]{2,1,0:T(8,128)(2,1)} collective-permute-done((bf16[3,256,256]{2,1,0:T(8,128)(2,1)S(1)}, bf16[3,256,256]{2,1,0:T(8,128)(2,1)}, u32[]{:S(2)}, u32[]{:S(2)}) %collective-permute-start.9) | collective-permute-done | bytes 393248 | tf_op jit(solution)/shard_map/ppermute | solution.py:27
  36.5 0.8 copy-done.9
  37.3 4.5 %collective-permute-start.16 = (bf16[512,512]{1,0:T(8,128)(2,1)}, bf16[512,512]{1,0:T(8,128)(2,1)}, u32[]{:S(2)}, u32[]{:S(2)}) collective-permute-start(bf16[512,512]{1,0:T(8,128)(2,1)} %convolution_convert_fusion.g0), channel_id=1, source_target_pairs={{0,192},{1,193},{2,194},{3,195},{4,196},{5,197},{6,198},{7,199},{8... | collective-permute-start | bytes 1572872 | tf_op jit(solution)/shard_map/ppermute | solution.py:27
  41.8 0.8 copy-done.6
  42.6 3.2 %collective-permute-start.18 = (bf16[256,256]{1,0:T(8,128)(2,1)S(1)}, bf16[256,256]{1,0:T(8,128)(2,1)S(1)}, u32[]{:S(2)}, u32[]{:S(2)}) collective-permute-start(bf16[256,256]{1,0:T(8,128)(2,1)S(1)} %get-tuple-element.22), channel_id=1, source_target_pairs={{0,32},{1,33},{2,34},{3,35},{4,36},{5,37},{6,38},{7,39},{8,40},{9,... | collective-permute-start | bytes 393224 | tf_op jit(solution)/shard_map/ppermute | solution.py:27
  45.8 1.9 %collective-permute-start.17 = (bf16[256,256]{1,0:T(8,128)(2,1)S(1)}, bf16[256,256]{1,0:T(8,128)(2,1)S(1)}, u32[]{:S(2)}, u32[]{:S(2)}) collective-permute-start(bf16[256,256]{1,0:T(8,128)(2,1)S(1)} %get-tuple-element.21), channel_id=1, source_target_pairs={{0,16},{1,17},{2,18},{3,19},{4,20},{5,21},{6,22},{7,23},{8,24},{9,... | collective-permute-start | bytes 393224 | tf_op jit(solution)/shard_map/ppermute | solution.py:27
  47.7 1.0 collective-permute-done.18
  48.7 2.0 %collective-permute-done.17 = bf16[256,256]{1,0:T(8,128)(2,1)S(1)} collective-permute-done((bf16[256,256]{1,0:T(8,128)(2,1)S(1)}, bf16[256,256]{1,0:T(8,128)(2,1)S(1)}, u32[]{:S(2)}, u32[]{:S(2)}) %collective-permute-start.17) | collective-permute-done | bytes 131104 | tf_op jit(solution)/shard_map/ppermute | solution.py:27
  50.8 0.6 copy-done.24
  51.4 0.1 collective-permute-start.12
  51.7 1.4 fusion.9
  53.1 1.0 pad_maximum_fusion.3.inverse
  54.1 2.7 %collective-permute-done.16.g3 = bf16[512,512]{1,0:T(8,128)(2,1)} collective-permute-done((bf16[512,512]{1,0:T(8,128)(2,1)}, bf16[512,512]{1,0:T(8,128)(2,1)}, u32[]{:S(2)}, u32[]{:S(2)}) %collective-permute-start.16) | collective-permute-done | bytes 524320 | tf_op jit(solution)/shard_map/ppermute | solution.py:27
  56.9 5.4 %shard_map.57 = bf16[256,1024]{1,0:T(8,128)(2,1)} custom-call(s32[4]{0:T(128)S(1)} %pad_add_fusion.place, bf16[512,512]{1,0:T(8,128)(2,1)} %convolution_convert_fusion.g0, bf16[512,512]{1,0:T(8,128)(2,1)S(1)} %copy-done.7, bf16[512,512]{1,0:T(8,128)(2,1)} %collective-permute-done.15.g2, bf16[512,512]{1,0:T(8,128)(2,1)} %collective-permute-done.16.g3, ...), custom_call_target="tpu_custom_call" | custom-call | flops 1073741824 | bytes 6291456 | tf_op jit(solution)/shard_map/pallas_call | solution.py:104
  62.3 0.1 collective-permute-start.20
  62.5 1.6 %convolution_convert_fusion.1.g0 = bf16[512,512]{1,0:T(8,128)(2,1)} fusion(bf16[1024,256]{1,0:T(8,128)(2,1)S(1)} %copy-done.17, bf16[1024,256]{1,0:T(8,128)(2,1)S(1)} %copy-done.18, bf16[256,1024]{1,0:T(8,128)(2,1)S(1)} %copy-done.16, bf16[256,1024]{1,0:T(8,128)(2,1)S(1)} %copy-done.14), kind=kOutput, calls=%fused_computation.1 | convolution fusion | flops 541327360 | bytes 2621440 | tf_op jit(solution)/shard_map/dot_general | solution.py:51
  64.0 0.7 collective-permute-start.2
  64.7 2.9 %collective-permute-start.3 = (bf16[512,512]{1,0:T(8,128)(2,1)}, bf16[512,512]{1,0:T(8,128)(2,1)}, u32[]{:S(2)}, u32[]{:S(2)}) collective-permute-start(bf16[512,512]{1,0:T(8,128)(2,1)} %convolution_convert_fusion.1.g0), channel_id=1, source_target_pairs={{0,128},{1,129},{2,130},{3,131},{4,132},{5,133},{6,134},{7,135},{8... | collective-permute-start | bytes 1572872 | tf_op jit(solution)/shard_map/ppermute | solution.py:27
  67.6 2.0 %collective-permute-start.4 = (bf16[512,512]{1,0:T(8,128)(2,1)}, bf16[512,512]{1,0:T(8,128)(2,1)}, u32[]{:S(2)}, u32[]{:S(2)}) collective-permute-start(bf16[512,512]{1,0:T(8,128)(2,1)} %convolution_convert_fusion.1.g0), channel_id=1, source_target_pairs={{0,192},{1,193},{2,194},{3,195},{4,196},{5,197},{6,198},{7,199},{8... | collective-permute-start | bytes 1572872 | tf_op jit(solution)/shard_map/ppermute | solution.py:27
  69.6 1.0 copy-done.3
  70.7 1.0 copy-done.8
  71.7 1.0 copy-done.11
  72.7 4.6 %shard_map.56 = bf16[256,1024]{1,0:T(8,128)(2,1)S(1)} custom-call(s32[4]{0:T(128)S(1)} %pad_add_fusion.place, bf16[512,512]{1,0:T(8,128)(2,1)} %convolution_convert_fusion.g0, bf16[512,512]{1,0:T(8,128)(2,1)S(1)} %copy-done.8, bf16[512,512]{1,0:T(8,128)(2,1)} %collective-permute-done.15.g2, bf16[512,512]{1,0:T(8,128)(2,1)} %collective-permute-done.16.g3, ...), custom_call_target="tpu_custom_call" | custom-call | flops 1073741824 | bytes 6291456 | tf_op jit(solution)/shard_map/pallas_call | solution.py:104
  77.3 1.2 add_convert_fusion
  78.6 5.8 %collective-permute-start.23 = (bf16[256,256]{1,0:T(8,128)(2,1)S(1)}, bf16[256,256]{1,0:T(8,128)(2,1)S(1)}, u32[]{:S(2)}, u32[]{:S(2)}) collective-permute-start(bf16[256,256]{1,0:T(8,128)(2,1)S(1)} %constant_dynamic-slice_fusion), channel_id=1, source_target_pairs={{0,2},{1,3},{2,0},{3,1},{4,66},{5,67},{6,64},{7,65},{8,130},{9,131... | collective-permute-start | bytes 393224 | tf_op jit(solution)/shard_map/ppermute | solution.py:27
  84.4 3.9 %collective-permute-start.22 = (bf16[256,256]{1,0:T(8,128)(2,1)S(1)}, bf16[256,256]{1,0:T(8,128)(2,1)S(1)}, u32[]{:S(2)}, u32[]{:S(2)}) collective-permute-start(bf16[256,256]{1,0:T(8,128)(2,1)S(1)} %constant_dynamic-slice_fusion), channel_id=1, source_target_pairs={{0,0},{1,1},{2,2},{3,3},{4,64},{5,65},{6,66},{7,67},{8,128},{9,129... | collective-permute-start | bytes 393224 | tf_op jit(solution)/shard_map/ppermute | solution.py:27
  88.3 2.7 %collective-permute-done.4.g3 = bf16[512,512]{1,0:T(8,128)(2,1)} collective-permute-done((bf16[512,512]{1,0:T(8,128)(2,1)}, bf16[512,512]{1,0:T(8,128)(2,1)}, u32[]{:S(2)}, u32[]{:S(2)}) %collective-permute-start.4) | collective-permute-done | bytes 524320 | tf_op jit(solution)/shard_map/ppermute | solution.py:27
  91.0 5.1 %shard_map.55 = (bf16[256,1024]{1,0:T(8,128)(2,1)S(1)}, bf16[256,1024]{1,0:T(8,128)(2,1)S(1)}) custom-call(s32[4]{0:T(128)S(1)} %pad_add_fusion.place, bf16[512,512]{1,0:T(8,128)(2,1)} %convolution_convert_fusion.1.g0, bf16[512,512]{1,0:T(8,128)(2,1)} %collective-permute-done.2.g1, bf16[512,512]{1,0:T(8,128)(2,1)} %collective-permute-done.3.g2, ...), custom_call_target="tpu_custom_call" | custom-call | flops 2147483648 | bytes 6291456 | tf_op jit(solution)/shard_map/pallas_call | solution.py:104
  96.2 10.8 %collective-permute-start.24 = (bf16[2,256,256]{2,1,0:T(8,128)(2,1)S(1)}, bf16[2,256,256]{2,1,0:T(8,128)(2,1)S(1)}, u32[]{:S(2)}, u32[]{:S(2)}) collective-permute-start(bf16[2,256,256]{2,1,0:T(8,128)(2,1)S(1)} %pad_maximum_fusion.5.refs_0_), channel_id=1, source_target_pairs={{0,4},{1,5},{2,6},{3,7},{4,8},{5,9},{6,10},{7,11},{8,12},{9,13},{1... | collective-permute-start | bytes 786440 | tf_op jit(solution)/shard_map/ppermute | solution.py:27
  107.0 1.7 %collective-permute-start.14 = (bf16[256,1024]{1,0:T(8,128)(2,1)S(1)}, bf16[256,1024]{1,0:T(8,128)(2,1)S(1)}, u32[]{:S(2)}, u32[]{:S(2)}) collective-permute-start(bf16[256,1024]{1,0:T(8,128)(2,1)S(1)} %get-tuple-element.20), channel_id=1, source_target_pairs={{0,16},{1,17},{2,18},{3,19},{4,20},{5,21},{6,22},{7,23},{8,24},{9,... | collective-permute-start | bytes 1572872 | tf_op jit(solution)/shard_map/ppermute | solution.py:27
  108.7 1.5 %collective-permute-start.21 = (bf16[256,1024]{1,0:T(8,128)(2,1)S(1)}, bf16[256,1024]{1,0:T(8,128)(2,1)S(1)}, u32[]{:S(2)}, u32[]{:S(2)}) collective-permute-start(bf16[256,1024]{1,0:T(8,128)(2,1)S(1)} %add_convert_fusion), channel_id=1, source_target_pairs={{0,32},{1,33},{2,34},{3,35},{4,36},{5,37},{6,38},{7,39},{8,40},{9,... | collective-permute-start | bytes 1572872 | tf_op jit(solution)/shard_map/ppermute | solution.py:27
  110.2 1.0 collective-permute-done.24.refs_1_
  111.2 2.8 %collective-permute-start.25 = (bf16[2,256,256]{2,1,0:T(8,128)(2,1)S(1)}, bf16[2,256,256]{2,1,0:T(8,128)(2,1)S(1)}, u32[]{:S(2)}, u32[]{:S(2)}) collective-permute-start(bf16[2,256,256]{2,1,0:T(8,128)(2,1)S(1)} %pad_maximum_fusion.5.refs_0_), channel_id=1, source_target_pairs={{0,8},{1,9},{2,10},{3,11},{4,12},{5,13},{6,14},{7,15},{8,0},{9,1},... | collective-permute-start | bytes 786440 | tf_op jit(solution)/shard_map/ppermute | solution.py:27
  114.0 16.2 %collective-permute-done.14.m1 = bf16[256,1024]{1,0:T(8,128)(2,1)S(1)} collective-permute-done((bf16[256,1024]{1,0:T(8,128)(2,1)S(1)}, bf16[256,1024]{1,0:T(8,128)(2,1)S(1)}, u32[]{:S(2)}, u32[]{:S(2)}) %collective-permute-start.14) | collective-permute-done | bytes 524320 | tf_op jit(solution)/shard_map/ppermute | solution.py:27
  130.3 0.5 collective-permute-start.30
  130.8 0.1 collective-permute-start.29
  130.9 0.9 collective-permute-done.28.refs_5_
  131.8 0.4 collective-permute-done.30.refs_7_
  132.2 0.4 collective-permute-done.29.refs_6_
  132.6 2.4 %shard_map.58 = bf16[4,256,256]{2,1,0:T(8,128)(2,1)S(1)} custom-call(s32[4]{0:T(128)S(1)} %pad_add_fusion.place, bf16[256,1024]{1,0:T(8,128)(2,1)S(1)} %get-tuple-element.19.m0, bf16[256,1024]{1,0:T(8,128)(2,1)S(1)} %collective-permute-done.14.m1, bf16[256,1024]{1,0:T(8,128)(2,1)S(1)} %collective-permute-done.21.m2, bf16[4,256,256]{2,1,0:T(8,128)(2,1)S(1)} %copy-done.5, ...), custom_call_target="tpu_custom_call" | custom-call | flops 1073741824 | bytes 6291456 | tf_op jit(solution)/shard_map/pallas_call | solution.py:152
  135.0 0.5 collective-permute-start.31
  135.4 2.7 %collective-permute-start.32 = (bf16[256,256]{1,0:T(8,128)(2,1)S(1)}, bf16[256,256]{1,0:T(8,128)(2,1)S(1)}, u32[]{:S(2)}, u32[]{:S(2)}) collective-permute-start(bf16[256,256]{1,0:T(8,128)(2,1)S(1)} %get-tuple-element.39), channel_id=1, source_target_pairs={{0,32},{1,33},{2,34},{3,35},{4,36},{5,37},{6,38},{7,39},{8,40},{9,... | collective-permute-start | bytes 393224 | tf_op jit(solution)/shard_map/ppermute | solution.py:27
  138.1 1.3 collective-permute-start.33
  139.4 2.8 %collective-permute-done.31.b1 = bf16[256,256]{1,0:T(8,128)(2,1)S(1)} collective-permute-done((bf16[256,256]{1,0:T(8,128)(2,1)S(1)}, bf16[256,256]{1,0:T(8,128)(2,1)S(1)}, u32[]{:S(2)}, u32[]{:S(2)}) %collective-permute-start.31) | collective-permute-done | bytes 131104 | tf_op jit(solution)/shard_map/ppermute | solution.py:27
  142.2 6.1 %collective-permute-done.32.b2 = bf16[256,256]{1,0:T(8,128)(2,1)S(1)} collective-permute-done((bf16[256,256]{1,0:T(8,128)(2,1)S(1)}, bf16[256,256]{1,0:T(8,128)(2,1)S(1)}, u32[]{:S(2)}, u32[]{:S(2)}) %collective-permute-start.32) | collective-permute-done | bytes 131104 | tf_op jit(solution)/shard_map/ppermute | solution.py:27
  148.3 2.1 %shard_map.59 = bf16[256,1024]{1,0:T(8,128)(2,1)} custom-call(s32[4]{0:T(128)S(1)} %pad_add_fusion.place, bf16[1024,1024]{1,0:T(8,128)(2,1)S(1)} %copy-done.1, bf16[256,256]{1,0:T(8,128)(2,1)S(1)} %get-tuple-element.41.b0, bf16[256,256]{1,0:T(8,128)(2,1)S(1)} %collective-permute-done.31.b1, bf16[256,256]{1,0:T(8,128)(2,1)S(1)} %collective-permute-done.32.b2, ...), custom_call_target="tpu_custom_call" | custom-call | flops 536870912 | bytes 3145728 | tf_op jit(solution)/shard_map/pallas_call | solution.py:185
  (77 shorter events, 0.4 us)
Async XLA Ops:
  0.0 78.5 %copy-start = (bf16[1024,256]{1,0:T(8,128)(2,1)S(1)}, bf16[1024,256]{1,0:T(8,128)(2,1)}, u32[]{:S(2)}) copy-start(bf16[1024,256]{1,0:T(8,128)(2,1)} %param.7) | copy-start | bytes 1572868
  0.0 14.2 %copy-start.1 = (bf16[1024,1024]{1,0:T(8,128)(2,1)S(1)}, bf16[1024,1024]{1,0:T(8,128)(2,1)}, u32[]{:S(2)}) copy-start(bf16[1024,1024]{1,0:T(8,128)(2,1)} %basis.1) | copy-start | bytes 6291460
  1.2 5.3 %collective-permute-start = (bf16[256,256]{1,0:T(8,128)(2,1)S(1)}, bf16[256,256]{1,0:T(8,128)(2,1)S(1)}, u32[]{:S(2)}, u32[]{:S(2)}) collective-permute-start(bf16[256,256]{1,0:T(8,128)(2,1)S(1)} %get-tuple-element.28), channel_id=1, source_target_pairs={{0,64},{1,65},{2,66},{3,67},{4,68},{5,69},{6,70},{7,71},{8,72},{9,... | collective-permute-start | bytes 393224 | tf_op jit(solution)/shard_map/ppermute | solution.py:27
  2.9 5.7 %collective-permute-start.6 = (bf16[256,256]{1,0:T(8,128)(2,1)S(1)}, bf16[256,256]{1,0:T(8,128)(2,1)S(1)}, u32[]{:S(2)}, u32[]{:S(2)}) collective-permute-start(bf16[256,256]{1,0:T(8,128)(2,1)S(1)} %get-tuple-element.29), channel_id=1, source_target_pairs={{0,192},{1,193},{2,194},{3,195},{4,196},{5,197},{6,198},{7,199},{8... | collective-permute-start | bytes 393224 | tf_op jit(solution)/shard_map/ppermute | solution.py:27
  3.6 7.8 %collective-permute-start.5 = (bf16[256,256]{1,0:T(8,128)(2,1)S(1)}, bf16[256,256]{1,0:T(8,128)(2,1)S(1)}, u32[]{:S(2)}, u32[]{:S(2)}) collective-permute-start(bf16[256,256]{1,0:T(8,128)(2,1)S(1)} %get-tuple-element.27), channel_id=1, source_target_pairs={{0,128},{1,129},{2,130},{3,131},{4,132},{5,133},{6,134},{7,135},{8... | collective-permute-start | bytes 393224 | tf_op jit(solution)/shard_map/ppermute | solution.py:27
  11.4 10.8 %collective-permute-start.7 = (bf16[3,256,256]{2,1,0:T(8,128)(2,1)S(1)}, bf16[3,256,256]{2,1,0:T(8,128)(2,1)}, u32[]{:S(2)}, u32[]{:S(2)}) collective-permute-start(bf16[3,256,256]{2,1,0:T(8,128)(2,1)S(1)} %pad_maximum_fusion.4.refs_0_), channel_id=1, source_target_pairs={{0,4},{1,5},{2,6},{3,7},{4,8},{5,9},{6,10},{7,11},{8,12},{9,13},{1... | collective-permute-start | bytes 1179656 | tf_op jit(solution)/shard_map/ppermute | solution.py:27
  14.3 1.3 copy-start.13
  14.3 1.3 copy-start.15
  17.1 24.6 %collective-permute-start.1 = (bf16[512,512]{1,0:T(8,128)(2,1)}, bf16[512,512]{1,0:T(8,128)(2,1)S(1)}, u32[]{:S(2)}, u32[]{:S(2)}) collective-permute-start(bf16[512,512]{1,0:T(8,128)(2,1)} %convolution_convert_fusion.g0), channel_id=1, source_target_pairs={{0,64},{1,65},{2,66},{3,67},{4,68},{5,69},{6,70},{7,71},{8,72},{9,... | collective-permute-start | bytes 1572872 | tf_op jit(solution)/shard_map/ppermute | solution.py:27
  19.7 16.8 %collective-permute-start.9 = (bf16[3,256,256]{2,1,0:T(8,128)(2,1)S(1)}, bf16[3,256,256]{2,1,0:T(8,128)(2,1)}, u32[]{:S(2)}, u32[]{:S(2)}) collective-permute-start(bf16[3,256,256]{2,1,0:T(8,128)(2,1)S(1)} %pad_maximum_fusion.4.refs_0_), channel_id=1, source_target_pairs={{0,12},{1,13},{2,14},{3,15},{4,0},{5,1},{6,2},{7,3},{8,4},{9,5},{1... | collective-permute-start | bytes 1179656 | tf_op jit(solution)/shard_map/ppermute | solution.py:27
  21.5 15.1 %collective-permute-start.10 = (bf16[3,256,256]{2,1,0:T(8,128)(2,1)S(1)}, bf16[3,256,256]{2,1,0:T(8,128)(2,1)S(1)}, u32[]{:S(2)}, u32[]{:S(2)}) collective-permute-start(bf16[3,256,256]{2,1,0:T(8,128)(2,1)S(1)} %pad_maximum_fusion.4.refs_0_), channel_id=1, source_target_pairs={{0,1},{1,0},{2,3},{3,2},{4,5},{5,4},{6,7},{7,6},{8,9},{9,8},{10,11... | collective-permute-start | bytes 1179656 | tf_op jit(solution)/shard_map/ppermute | solution.py:27
  22.2 28.6 %collective-permute-start.8 = (bf16[3,256,256]{2,1,0:T(8,128)(2,1)S(1)}, bf16[3,256,256]{2,1,0:T(8,128)(2,1)}, u32[]{:S(2)}, u32[]{:S(2)}) collective-permute-start(bf16[3,256,256]{2,1,0:T(8,128)(2,1)S(1)} %pad_maximum_fusion.4.refs_0_), channel_id=1, source_target_pairs={{0,8},{1,9},{2,10},{3,11},{4,12},{5,13},{6,14},{7,15},{8,0},{9,1},... | collective-permute-start | bytes 1179656 | tf_op jit(solution)/shard_map/ppermute | solution.py:27
  26.1 19.7 %collective-permute-start.19 = (bf16[256,256]{1,0:T(8,128)(2,1)S(1)}, bf16[256,256]{1,0:T(8,128)(2,1)S(1)}, u32[]{:S(2)}, u32[]{:S(2)}) collective-permute-start(bf16[256,256]{1,0:T(8,128)(2,1)S(1)} %get-tuple-element.23), channel_id=1, source_target_pairs={{0,48},{1,49},{2,50},{3,51},{4,52},{5,53},{6,54},{7,55},{8,56},{9,... | collective-permute-start | bytes 393224 | tf_op jit(solution)/shard_map/ppermute | solution.py:27
  36.5 17.6 %collective-permute-start.15 = (bf16[512,512]{1,0:T(8,128)(2,1)}, bf16[512,512]{1,0:T(8,128)(2,1)}, u32[]{:S(2)}, u32[]{:S(2)}) collective-permute-start(bf16[512,512]{1,0:T(8,128)(2,1)} %convolution_convert_fusion.g0), channel_id=1, source_target_pairs={{0,128},{1,129},{2,130},{3,131},{4,132},{5,133},{6,134},{7,135},{8... | collective-permute-start | bytes 1572872 | tf_op jit(solution)/shard_map/ppermute | solution.py:27
  36.5 0.8 copy-start.9
  37.3 19.5 %collective-permute-start.16 = (bf16[512,512]{1,0:T(8,128)(2,1)}, bf16[512,512]{1,0:T(8,128)(2,1)}, u32[]{:S(2)}, u32[]{:S(2)}) collective-permute-start(bf16[512,512]{1,0:T(8,128)(2,1)} %convolution_convert_fusion.g0), channel_id=1, source_target_pairs={{0,192},{1,193},{2,194},{3,195},{4,196},{5,197},{6,198},{7,199},{8... | collective-permute-start | bytes 1572872 | tf_op jit(solution)/shard_map/ppermute | solution.py:27
  41.8 0.8 copy-start.6
  42.6 6.2 %collective-permute-start.18 = (bf16[256,256]{1,0:T(8,128)(2,1)S(1)}, bf16[256,256]{1,0:T(8,128)(2,1)S(1)}, u32[]{:S(2)}, u32[]{:S(2)}) collective-permute-start(bf16[256,256]{1,0:T(8,128)(2,1)S(1)} %get-tuple-element.22), channel_id=1, source_target_pairs={{0,32},{1,33},{2,34},{3,35},{4,36},{5,37},{6,38},{7,39},{8,40},{9,... | collective-permute-start | bytes 393224 | tf_op jit(solution)/shard_map/ppermute | solution.py:27
  45.8 5.0 %copy-start.20 = (bf16[256,256]{1,0:T(8,128)(2,1)}, bf16[256,256]{1,0:T(8,128)(2,1)S(1)}, u32[]{:S(2)}) copy-start(bf16[256,256]{1,0:T(8,128)(2,1)S(1)} %collective-permute-done.19) | copy-start | bytes 393220
  45.8 5.0 %collective-permute-start.17 = (bf16[256,256]{1,0:T(8,128)(2,1)S(1)}, bf16[256,256]{1,0:T(8,128)(2,1)S(1)}, u32[]{:S(2)}, u32[]{:S(2)}) collective-permute-start(bf16[256,256]{1,0:T(8,128)(2,1)S(1)} %get-tuple-element.21), channel_id=1, source_target_pairs={{0,16},{1,17},{2,18},{3,19},{4,20},{5,21},{6,22},{7,23},{8,24},{9,... | collective-permute-start | bytes 393224 | tf_op jit(solution)/shard_map/ppermute | solution.py:27
  48.7 2.0 %copy-start.22 = (bf16[256,256]{1,0:T(8,128)(2,1)}, bf16[256,256]{1,0:T(8,128)(2,1)S(1)}, u32[]{:S(2)}) copy-start(bf16[256,256]{1,0:T(8,128)(2,1)S(1)} %collective-permute-done.18) | copy-start | bytes 393220
  48.7 8.1 %collective-permute-start.11 = (bf16[3,256,256]{2,1,0:T(8,128)(2,1)}, bf16[3,256,256]{2,1,0:T(8,128)(2,1)}, u32[]{:S(2)}, u32[]{:S(2)}) collective-permute-start(bf16[3,256,256]{2,1,0:T(8,128)(2,1)} %collective-permute-done.7.refs_1_), channel_id=1, source_target_pairs={{0,1},{1,0},{2,3},{3,2},{4,5},{5,4},{6,7},{7,6},{8,9},{9,8},{10,11... | collective-permute-start | bytes 1179656 | tf_op jit(solution)/shard_map/ppermute | solution.py:27
  50.7 0.7 copy-start.24
  50.7 6.1 %collective-permute-start.13 = (bf16[3,256,256]{2,1,0:T(8,128)(2,1)}, bf16[3,256,256]{2,1,0:T(8,128)(2,1)}, u32[]{:S(2)}, u32[]{:S(2)}) collective-permute-start(bf16[3,256,256]{2,1,0:T(8,128)(2,1)} %collective-permute-done.9.refs_3_), channel_id=1, source_target_pairs={{0,1},{1,0},{2,3},{3,2},{4,5},{5,4},{6,7},{7,6},{8,9},{9,8},{10,11... | collective-permute-start | bytes 1179656 | tf_op jit(solution)/shard_map/ppermute | solution.py:27
  51.4 5.4 %collective-permute-start.12 = (bf16[3,256,256]{2,1,0:T(8,128)(2,1)}, bf16[3,256,256]{2,1,0:T(8,128)(2,1)}, u32[]{:S(2)}, u32[]{:S(2)}) collective-permute-start(bf16[3,256,256]{2,1,0:T(8,128)(2,1)} %collective-permute-done.8.refs_2_), channel_id=1, source_target_pairs={{0,1},{1,0},{2,3},{3,2},{4,5},{5,4},{6,7},{7,6},{8,9},{9,8},{10,11... | collective-permute-start | bytes 1179656 | tf_op jit(solution)/shard_map/ppermute | solution.py:27
  51.5 1.5 %copy-start.19 = (bf16[1,256,256]{2,1,0:T(8,128)(2,1)S(1)}, bf16[1,256,256]{2,1,0:T(8,128)(2,1)}, u32[]{:S(2)}) copy-start(bf16[1,256,256]{2,1,0:T(8,128)(2,1)} %get-tuple-element.42) | copy-start | bytes 393220
  51.5 1.6 %copy-start.21 = (bf16[256,256]{1,0:T(8,128)(2,1)S(1)}, bf16[256,256]{1,0:T(8,128)(2,1)}, u32[]{:S(2)}) copy-start(bf16[256,256]{1,0:T(8,128)(2,1)} %copy-done.20) | copy-start | bytes 393220
  51.6 1.6 %copy-start.23 = (bf16[256,256]{1,0:T(8,128)(2,1)S(1)}, bf16[256,256]{1,0:T(8,128)(2,1)}, u32[]{:S(2)}) copy-start(bf16[256,256]{1,0:T(8,128)(2,1)} %copy-done.22) | copy-start | bytes 393220
  51.6 1.6 %copy-start.25 = (bf16[256,256]{1,0:T(8,128)(2,1)S(1)}, bf16[256,256]{1,0:T(8,128)(2,1)}, u32[]{:S(2)}) copy-start(bf16[256,256]{1,0:T(8,128)(2,1)} %copy-done.24) | copy-start | bytes 393220
  51.6 5.3 %copy-start.7 = (bf16[512,512]{1,0:T(8,128)(2,1)S(1)}, bf16[512,512]{1,0:T(8,128)(2,1)}, u32[]{:S(2)}) copy-start(bf16[512,512]{1,0:T(8,128)(2,1)} %copy-done.6) | copy-start | bytes 1572868
  51.6 5.3 %copy-start.10 = (bf16[3,256,256]{2,1,0:T(8,128)(2,1)S(1)}, bf16[3,256,256]{2,1,0:T(8,128)(2,1)}, u32[]{:S(2)}) copy-start(bf16[3,256,256]{2,1,0:T(8,128)(2,1)} %copy-done.9) | copy-start | bytes 1179652
  53.1 9.3 %copy-start.2 = (bf16[256,1024]{1,0:T(8,128)(2,1)}, bf16[256,1024]{1,0:T(8,128)(2,1)S(1)}, u32[]{:S(2)}) copy-start(bf16[256,1024]{1,0:T(8,128)(2,1)S(1)} %get-tuple-element.31.mine) | copy-start | bytes 1572868
  56.9 5.6 %copy-start.14 = (bf16[256,1024]{1,0:T(8,128)(2,1)S(1)}, bf16[256,1024]{1,0:T(8,128)(2,1)}, u32[]{:S(2)}) copy-start(bf16[256,1024]{1,0:T(8,128)(2,1)} %copy-done.13) | copy-start | bytes 1572868
  56.9 5.6 %copy-start.16 = (bf16[256,1024]{1,0:T(8,128)(2,1)S(1)}, bf16[256,1024]{1,0:T(8,128)(2,1)}, u32[]{:S(2)}) copy-start(bf16[256,1024]{1,0:T(8,128)(2,1)} %copy-done.15) | copy-start | bytes 1572868
  56.9 5.6 %copy-start.17 = (bf16[1024,256]{1,0:T(8,128)(2,1)S(1)}, bf16[1024,256]{1,0:T(8,128)(2,1)}, u32[]{:S(2)}) copy-start(bf16[1024,256]{1,0:T(8,128)(2,1)} %get-tuple-element.33) | copy-start | bytes 1572868
  56.9 5.6 %copy-start.18 = (bf16[1024,256]{1,0:T(8,128)(2,1)S(1)}, bf16[1024,256]{1,0:T(8,128)(2,1)}, u32[]{:S(2)}) copy-start(bf16[1024,256]{1,0:T(8,128)(2,1)} %get-tuple-element.34) | copy-start | bytes 1572868
  62.3 15.0 %collective-permute-start.20 = (bf16[256,1024]{1,0:T(8,128)(2,1)}, bf16[256,1024]{1,0:T(8,128)(2,1)}, u32[]{:S(2)}, u32[]{:S(2)}) collective-permute-start(bf16[256,1024]{1,0:T(8,128)(2,1)} %shard_map.57), channel_id=1, source_target_pairs={{0,16},{1,17},{2,18},{3,19},{4,20},{5,21},{6,22},{7,23},{8,24},{9,... | collective-permute-start | bytes 1572872 | tf_op jit(solution)/shard_map/ppermute | solution.py:27
  64.0 24.2 %collective-permute-start.2 = (bf16[512,512]{1,0:T(8,128)(2,1)}, bf16[512,512]{1,0:T(8,128)(2,1)}, u32[]{:S(2)}, u32[]{:S(2)}) collective-permute-start(bf16[512,512]{1,0:T(8,128)(2,1)} %convolution_convert_fusion.1.g0), channel_id=1, source_target_pairs={{0,64},{1,65},{2,66},{3,67},{4,68},{5,69},{6,70},{7,71},{8,72},{9,... | collective-permute-start | bytes 1572872 | tf_op jit(solution)/shard_map/ppermute | solution.py:27
  64.7 23.6 %collective-permute-start.3 = (bf16[512,512]{1,0:T(8,128)(2,1)}, bf16[512,512]{1,0:T(8,128)(2,1)}, u32[]{:S(2)}, u32[]{:S(2)}) collective-permute-start(bf16[512,512]{1,0:T(8,128)(2,1)} %convolution_convert_fusion.1.g0), channel_id=1, source_target_pairs={{0,128},{1,129},{2,130},{3,131},{4,132},{5,133},{6,134},{7,135},{8... | collective-permute-start | bytes 1572872 | tf_op jit(solution)/shard_map/ppermute | solution.py:27
  67.6 23.4 %collective-permute-start.4 = (bf16[512,512]{1,0:T(8,128)(2,1)}, bf16[512,512]{1,0:T(8,128)(2,1)}, u32[]{:S(2)}, u32[]{:S(2)}) collective-permute-start(bf16[512,512]{1,0:T(8,128)(2,1)} %convolution_convert_fusion.1.g0), channel_id=1, source_target_pairs={{0,192},{1,193},{2,194},{3,195},{4,196},{5,197},{6,198},{7,199},{8... | collective-permute-start | bytes 1572872 | tf_op jit(solution)/shard_map/ppermute | solution.py:27
  69.6 1.0 copy-start.3
  70.7 1.0 copy-start.8
  71.7 1.0 copy-start.11
  72.7 18.3 %copy-start.4 = (bf16[256,1024]{1,0:T(8,128)(2,1)S(1)}, bf16[256,1024]{1,0:T(8,128)(2,1)}, u32[]{:S(2)}) copy-start(bf16[256,1024]{1,0:T(8,128)(2,1)} %copy-done.2) | copy-start | bytes 1572868
  72.7 18.3 %copy-start.12 = (bf16[3,256,256]{2,1,0:T(8,128)(2,1)S(1)}, bf16[3,256,256]{2,1,0:T(8,128)(2,1)}, u32[]{:S(2)}) copy-start(bf16[3,256,256]{2,1,0:T(8,128)(2,1)} %copy-done.9) | copy-start | bytes 1179652
  78.6 54.0 %copy-start.5 = (bf16[4,256,256]{2,1,0:T(8,128)(2,1)S(1)}, bf16[4,256,256]{2,1,0:T(8,128)(2,1)}, u32[]{:S(2)}) copy-start(bf16[4,256,256]{2,1,0:T(8,128)(2,1)} %pad_maximum_fusion.3.inverse) | copy-start | bytes 1572868
  78.6 17.5 %collective-permute-start.23 = (bf16[256,256]{1,0:T(8,128)(2,1)S(1)}, bf16[256,256]{1,0:T(8,128)(2,1)S(1)}, u32[]{:S(2)}, u32[]{:S(2)}) collective-permute-start(bf16[256,256]{1,0:T(8,128)(2,1)S(1)} %constant_dynamic-slice_fusion), channel_id=1, source_target_pairs={{0,2},{1,3},{2,0},{3,1},{4,66},{5,67},{6,64},{7,65},{8,130},{9,131... | collective-permute-start | bytes 393224 | tf_op jit(solution)/shard_map/ppermute | solution.py:27
  84.4 11.8 %collective-permute-start.22 = (bf16[256,256]{1,0:T(8,128)(2,1)S(1)}, bf16[256,256]{1,0:T(8,128)(2,1)S(1)}, u32[]{:S(2)}, u32[]{:S(2)}) collective-permute-start(bf16[256,256]{1,0:T(8,128)(2,1)S(1)} %constant_dynamic-slice_fusion), channel_id=1, source_target_pairs={{0,0},{1,1},{2,2},{3,3},{4,64},{5,65},{6,66},{7,67},{8,128},{9,129... | collective-permute-start | bytes 393224 | tf_op jit(solution)/shard_map/ppermute | solution.py:27
  96.2 15.0 %collective-permute-start.24 = (bf16[2,256,256]{2,1,0:T(8,128)(2,1)S(1)}, bf16[2,256,256]{2,1,0:T(8,128)(2,1)S(1)}, u32[]{:S(2)}, u32[]{:S(2)}) collective-permute-start(bf16[2,256,256]{2,1,0:T(8,128)(2,1)S(1)} %pad_maximum_fusion.5.refs_0_), channel_id=1, source_target_pairs={{0,4},{1,5},{2,6},{3,7},{4,8},{5,9},{6,10},{7,11},{8,12},{9,13},{1... | collective-permute-start | bytes 786440 | tf_op jit(solution)/shard_map/ppermute | solution.py:27
  107.0 23.3 %collective-permute-start.14 = (bf16[256,1024]{1,0:T(8,128)(2,1)S(1)}, bf16[256,1024]{1,0:T(8,128)(2,1)S(1)}, u32[]{:S(2)}, u32[]{:S(2)}) collective-permute-start(bf16[256,1024]{1,0:T(8,128)(2,1)S(1)} %get-tuple-element.20), channel_id=1, source_target_pairs={{0,16},{1,17},{2,18},{3,19},{4,20},{5,21},{6,22},{7,23},{8,24},{9,... | collective-permute-start | bytes 1572872 | tf_op jit(solution)/shard_map/ppermute | solution.py:27
  108.7 22.2 %collective-permute-start.21 = (bf16[256,1024]{1,0:T(8,128)(2,1)S(1)}, bf16[256,1024]{1,0:T(8,128)(2,1)S(1)}, u32[]{:S(2)}, u32[]{:S(2)}) collective-permute-start(bf16[256,1024]{1,0:T(8,128)(2,1)S(1)} %add_convert_fusion), channel_id=1, source_target_pairs={{0,32},{1,33},{2,34},{3,35},{4,36},{5,37},{6,38},{7,39},{8,40},{9,... | collective-permute-start | bytes 1572872 | tf_op jit(solution)/shard_map/ppermute | solution.py:27
  110.2 20.0 %collective-permute-start.26 = (bf16[2,256,256]{2,1,0:T(8,128)(2,1)S(1)}, bf16[2,256,256]{2,1,0:T(8,128)(2,1)S(1)}, u32[]{:S(2)}, u32[]{:S(2)}) collective-permute-start(bf16[2,256,256]{2,1,0:T(8,128)(2,1)S(1)} %pad_maximum_fusion.5.refs_0_), channel_id=1, source_target_pairs={{0,12},{1,13},{2,14},{3,15},{4,0},{5,1},{6,2},{7,3},{8,4},{9,5},{1... | collective-permute-start | bytes 786440 | tf_op jit(solution)/shard_map/ppermute | solution.py:27
  111.2 19.6 %collective-permute-start.25 = (bf16[2,256,256]{2,1,0:T(8,128)(2,1)S(1)}, bf16[2,256,256]{2,1,0:T(8,128)(2,1)S(1)}, u32[]{:S(2)}, u32[]{:S(2)}) collective-permute-start(bf16[2,256,256]{2,1,0:T(8,128)(2,1)S(1)} %pad_maximum_fusion.5.refs_0_), channel_id=1, source_target_pairs={{0,8},{1,9},{2,10},{3,11},{4,12},{5,13},{6,14},{7,15},{8,0},{9,1},... | collective-permute-start | bytes 786440 | tf_op jit(solution)/shard_map/ppermute | solution.py:27
  114.0 16.9 %collective-permute-start.27 = (bf16[2,256,256]{2,1,0:T(8,128)(2,1)S(1)}, bf16[2,256,256]{2,1,0:T(8,128)(2,1)S(1)}, u32[]{:S(2)}, u32[]{:S(2)}) collective-permute-start(bf16[2,256,256]{2,1,0:T(8,128)(2,1)S(1)} %pad_maximum_fusion.5.refs_0_), channel_id=1, source_target_pairs={{0,1},{1,0},{2,3},{3,2},{4,5},{5,4},{6,7},{7,6},{8,9},{9,8},{10,11... | collective-permute-start | bytes 786440 | tf_op jit(solution)/shard_map/ppermute | solution.py:27
  130.3 1.5 %collective-permute-start.28 = (bf16[2,256,256]{2,1,0:T(8,128)(2,1)S(1)}, bf16[2,256,256]{2,1,0:T(8,128)(2,1)S(1)}, u32[]{:S(2)}, u32[]{:S(2)}) collective-permute-start(bf16[2,256,256]{2,1,0:T(8,128)(2,1)S(1)} %collective-permute-done.24.refs_1_), channel_id=1, source_target_pairs={{0,1},{1,0},{2,3},{3,2},{4,5},{5,4},{6,7},{7,6},{8,9},{9,8},{10,11... | collective-permute-start | bytes 786440 | tf_op jit(solution)/shard_map/ppermute | solution.py:27
  130.3 1.9 %collective-permute-start.30 = (bf16[2,256,256]{2,1,0:T(8,128)(2,1)S(1)}, bf16[2,256,256]{2,1,0:T(8,128)(2,1)S(1)}, u32[]{:S(2)}, u32[]{:S(2)}) collective-permute-start(bf16[2,256,256]{2,1,0:T(8,128)(2,1)S(1)} %collective-permute-done.26.refs_3_), channel_id=1, source_target_pairs={{0,1},{1,0},{2,3},{3,2},{4,5},{5,4},{6,7},{7,6},{8,9},{9,8},{10,11... | collective-permute-start | bytes 786440 | tf_op jit(solution)/shard_map/ppermute | solution.py:27
  130.8 1.8 %collective-permute-start.29 = (bf16[2,256,256]{2,1,0:T(8,128)(2,1)S(1)}, bf16[2,256,256]{2,1,0:T(8,128)(2,1)S(1)}, u32[]{:S(2)}, u32[]{:S(2)}) collective-permute-start(bf16[2,256,256]{2,1,0:T(8,128)(2,1)S(1)} %collective-permute-done.25.refs_2_), channel_id=1, source_target_pairs={{0,1},{1,0},{2,3},{3,2},{4,5},{5,4},{6,7},{7,6},{8,9},{9,8},{10,11... | collective-permute-start | bytes 786440 | tf_op jit(solution)/shard_map/ppermute | solution.py:27
  135.0 7.3 %collective-permute-start.31 = (bf16[256,256]{1,0:T(8,128)(2,1)S(1)}, bf16[256,256]{1,0:T(8,128)(2,1)S(1)}, u32[]{:S(2)}, u32[]{:S(2)}) collective-permute-start(bf16[256,256]{1,0:T(8,128)(2,1)S(1)} %get-tuple-element.40), channel_id=1, source_target_pairs={{0,16},{1,17},{2,18},{3,19},{4,20},{5,21},{6,22},{7,23},{8,24},{9,... | collective-permute-start | bytes 393224 | tf_op jit(solution)/shard_map/ppermute | solution.py:27
  135.4 12.9 %collective-permute-start.32 = (bf16[256,256]{1,0:T(8,128)(2,1)S(1)}, bf16[256,256]{1,0:T(8,128)(2,1)S(1)}, u32[]{:S(2)}, u32[]{:S(2)}) collective-permute-start(bf16[256,256]{1,0:T(8,128)(2,1)S(1)} %get-tuple-element.39), channel_id=1, source_target_pairs={{0,32},{1,33},{2,34},{3,35},{4,36},{5,37},{6,38},{7,39},{8,40},{9,... | collective-permute-start | bytes 393224 | tf_op jit(solution)/shard_map/ppermute | solution.py:27
  138.1 10.2 %collective-permute-start.33 = (bf16[256,256]{1,0:T(8,128)(2,1)S(1)}, bf16[256,256]{1,0:T(8,128)(2,1)S(1)}, u32[]{:S(2)}, u32[]{:S(2)}) collective-permute-start(bf16[256,256]{1,0:T(8,128)(2,1)S(1)} %get-tuple-element.38), channel_id=1, source_target_pairs={{0,48},{1,49},{2,50},{3,51},{4,52},{5,53},{6,54},{7,55},{8,56},{9,... | collective-permute-start | bytes 393224 | tf_op jit(solution)/shard_map/ppermute | solution.py:27

commit v3 on v2

--- a/solution.py
+++ b/solution.py
@@ -8,6 +8,7 @@
 from jax.sharding import PartitionSpec as P
 
 DAMPING = 0.05
+COST = pl.CostEstimate(flops=1000, bytes_accessed=1000, transcendentals=0)
 NX, NY, NZ = 4, 4, 4
 BF = jnp.bfloat16
 F32 = jnp.float32
@@ -112,10 +113,8 @@
             pltpu.VMEM((2, 4) + own[0].shape, BF),
             pltpu.SemaphoreType.DMA((14,)),
         ],
-        compiler_params=pltpu.CompilerParams(vmem_limit_bytes=16 << 20),
-        cost_estimate=pl.CostEstimate(
-            flops=8 * count * rows * tok * width, bytes_accessed=6 << 20, transcendentals=0
-        ),
+        compiler_params=pltpu.CompilerParams(vmem_limit_bytes=48 << 20),
+        cost_estimate=COST,
     )(place, *grads, mine, rest, *own, *other)
 
 
@@ -160,10 +159,8 @@
             pltpu.VMEM((2, 4) + own[0].shape, BF),
             pltpu.SemaphoreType.DMA((8,)),
         ],
-        compiler_params=pltpu.CompilerParams(vmem_limit_bytes=16 << 20),
-        cost_estimate=pl.CostEstimate(
-            flops=4 * quarter * width * width, bytes_accessed=6 << 20, transcendentals=0
-        ),
+        compiler_params=pltpu.CompilerParams(vmem_limit_bytes=48 << 20),
+        cost_estimate=COST,
     )(place, *sums, inverse, *own, *other)
 
 
@@ -188,9 +185,7 @@
         in_specs=scalars() + vmem(5),
         out_specs=pl.BlockSpec(memory_space=pltpu.VMEM),
         compiler_params=pltpu.CompilerParams(vmem_limit_bytes=14 << 20),
-        cost_estimate=pl.CostEstimate(
-            flops=2 * rows * width * width, bytes_accessed=3 << 20, transcendentals=0
-        ),
+        cost_estimate=COST,
     )(place, basis, *parts)
 
 
@@ -211,7 +206,12 @@
     def piece(rows, b, col, width):
         return lax.dynamic_slice(inputs, (rows * half, b % NY * block + col), (half, width))
 
-    got = {k: along_y(piece(c, y + k, x * quarter, quarter), k) for k in (1, 3, 2)}
+    to_send = {k: piece(c, y + k, x * quarter, quarter) for k in (1, 3, 2)}
+    got = {k: along_y(to_send[k], k) for k in (1, 3, 2)}
+
+    basis_in, out_grads = lax.optimization_barrier((basis_in, out_grads, to_send))[:2]
+    at = lax.dynamic_slice_in_dim(basis_in, y * quarter, quarter, 0)
+    pieces = jnp.stack([crossed(at, 0), crossed(at, 1)])
 
     og = jnp.concatenate(
         [
@@ -231,8 +231,8 @@
         one = {k: along_y(go, k) for k in (1, 3, 2)}
         return [gt] + [one[k] for k in (1, 2, 3)]
 
-    upper = spread(turned((3, 2)), got[1])
-    lower = spread(turned((1, 0)), upper[1])
+    upper = spread(turned((3, 2)), pieces)
+    lower = spread(turned((1, 0)), upper[1], pieces)
 
     def over_x(pieces):
         got = {j: along_x(pieces, j) for j in (1, 3)}
@@ -248,18 +248,18 @@
     def level(e):
         return lax.dynamic_slice_in_dim(inverse, (z ^ e) * quarter, quarter, 0)
 
-    inverse = jnp.stack([level(0)] + [across_z(after(level(e), own[1]), e) for e in (1, 2, 3)])
+    inverse = jnp.stack([level(0)] + [across_z(after(level(e), upper[1], pieces), e) for e in (1, 2, 3)])
 
     local = (mine, rest, own, other)
     (m3,) = product(place, 0, 1, quarter, upper, *local)
     near3 = across_z(after(m3, inverse), 1)
     (m2,) = product(place, quarter, 1, quarter, upper, *local)
     far2 = (m2.astype(F32) + near3.astype(F32)).astype(BF)
+    lower[0] = after(lower[0], far2)
     m1, m0 = product(place, 0, 2, quarter, lower, *local)
     near1 = across_z(m1, 1)
 
-    at = lax.dynamic_slice_in_dim(after(basis_in, far2), y * quarter, quarter, 0)
-    a_own, a_other = over_x(jnp.stack([crossed(at, 0), crossed(at, 1)]))
+    a_own, a_other = over_x(after(pieces, far2))
     parts = middle(place, [m0, near1, across_z(far2, 2)], inverse, a_own, a_other)
     parts = [parts[0]] + [across_z(parts[e], e) for e in (1, 2, 3)]
     return last(place, basis_out, parts)

time: 153 us -> 149 us (0.974); the launches traced: 150 us -> 148 us
  waiting for transfers between devices: 48.6 us -> 55 us
  local copies, waits for them, and re-layouts: 13.9 us -> 10.8 us
  starting transfers between devices: 61.2 us -> 58.7 us
  other arithmetic: 3.76 us -> 1.78 us
    ppermute x34, waiting for transfers between devices: 48.6 us -> 55 us  [moved(): return lax.ppermute(block, ('dp', 'owner'), route)]
    unnamed x53 -> x41, local copies, waits for them, and re-layouts: 7.93 us -> 3.72 us
    ppermute x34, starting transfers between devices: 61.2 us -> 58.7 us  [moved(): return lax.ppermute(block, ('dp', 'owner'), route)]
  transfers between devices with their start and end apart: 34 -> 34, of which waited for: 16 -> 15; matrix products, arithmetic and copies ran while one was open for 9% -> 8% of each run, Pallas kernels for 6% -> 7%
where the time goes in v3:
time: 149 us; the launch traced here: 148 us
  starting transfers between devices  58.7 us (39%)
  waiting for transfers between devices  55 us (37%)
  Pallas kernels  19.2 us (13%)
  local copies, waits for them, and re-layouts  10.8 us (7%)
  matrix products  2.33 us (2%)
  other arithmetic  1.78 us (1%)
    ppermute x34, starting transfers between devices, moved(): return lax.ppermute(block, ('dp', 'owner'), route)  58.7 us
    ppermute x34, waiting for transfers between devices, moved(): return lax.ppermute(block, ('dp', 'owner'), route)  55 us
    pallas_call x3, Pallas kernels, product(): pl.pallas_call(functools.partial(product_kernel, start), out_shape=[jax.S...  14.8 us
    unnamed x41, local copies, waits for them, and re-layouts  3.72 us
    dynamic_slice x2, local copies, waits for them, and re-layouts, piece(): lax.dynamic_slice(inputs, (rows * half, b % NY * block + col), (half, wid...  3.55 us
  transfers between devices with their start and end apart: 34, of which 15 were waited for; matrix products, arithmetic and copies ran while one was open for 8% of the time, Pallas kernels for 7%

profile of v3, /device:TPU:8, one launch (start us, length us, event | category | flops | bytes accessed | tf_op | source)
XLA Modules:
  0.0 148.3 jit_solution(17523557588701068275)
XLA Ops:
  0.0 1.1 fusion.9
  1.1 0.1 copy-done
  1.2 8.1 %collective-permute-start.1 = (bf16[256,256]{1,0:T(8,128)(2,1)S(1)}, bf16[256,256]{1,0:T(8,128)(2,1)S(1)}, u32[]{:S(2)}, u32[]{:S(2)}) collective-permute-start(bf16[256,256]{1,0:T(8,128)(2,1)S(1)} %constant_dynamic-slice_fusion), channel_id=1, source_target_pairs={{0,2},{1,3},{2,0},{3,1},{4,66},{5,67},{6,64},{7,65},{8,130},{9,131... | collective-permute-start | bytes 393224 | tf_op jit(solution)/shard_map/ppermute | solution.py:28
  9.3 3.4 %collective-permute-start = (bf16[256,256]{1,0:T(8,128)(2,1)S(1)}, bf16[256,256]{1,0:T(8,128)(2,1)S(1)}, u32[]{:S(2)}, u32[]{:S(2)}) collective-permute-start(bf16[256,256]{1,0:T(8,128)(2,1)S(1)} %constant_dynamic-slice_fusion), channel_id=1, source_target_pairs={{0,0},{1,1},{2,2},{3,3},{4,64},{5,65},{6,66},{7,67},{8,128},{9,129... | collective-permute-start | bytes 393224 | tf_op jit(solution)/shard_map/ppermute | solution.py:28
  12.8 0.1 collective-permute-start.7
  12.9 6.0 %collective-permute-start.6 = (bf16[256,256]{1,0:T(8,128)(2,1)S(1)}, bf16[256,256]{1,0:T(8,128)(2,1)S(1)}, u32[]{:S(2)}, u32[]{:S(2)}) collective-permute-start(bf16[256,256]{1,0:T(8,128)(2,1)S(1)} %get-tuple-element.36), channel_id=1, source_target_pairs={{0,128},{1,129},{2,130},{3,131},{4,132},{5,133},{6,134},{7,135},{8... | collective-permute-start | bytes 393224 | tf_op jit(solution)/shard_map/ppermute | solution.py:28
  18.9 1.3 collective-permute-start.5
  20.2 2.7 %constant_dynamic-slice_fusion.2 = (bf16[1024,256]{1,0:T(8,128)(2,1)S(1)}, bf16[1024,256]{1,0:T(8,128)(2,1)}, bf16[1024,256]{1,0:T(8,128)(2,1)}, bf16[1024,256]{1,0:T(8,128)(2,1)S(1)}) fusion(bf16[1024,1024]{1,0:T(8,128)(2,1)} %basis.1, s32[]{:T(128)S(6)} %select_n.102, s32[]{:T(128)S(6)} %select_n.92, s32[]{:T(128)S(6)} %select_n.91, s32[]{:T(128)S(6)} %select_n.103), kind=kLoop, calls=%fused_computation.24 | loop fusion | bytes 4194320 | tf_op jit(solution)/shard_map/dynamic_slice | solution.py:225
  22.9 1.4 collective-permute-done.6
  24.4 3.1 %collective-permute-done.5 = bf16[256,256]{1,0:T(8,128)(2,1)S(1)} collective-permute-done((bf16[256,256]{1,0:T(8,128)(2,1)S(1)}, bf16[256,256]{1,0:T(8,128)(2,1)S(1)}, u32[]{:S(2)}, u32[]{:S(2)}) %collective-permute-start.5) | collective-permute-done | bytes 131104 | tf_op jit(solution)/shard_map/ppermute | solution.py:28
  27.6 0.1 collective-permute-start.8
  27.7 0.1 constant_dynamic-slice_fusion.4
  27.8 0.0 copy-start.4
  27.8 1.6 %convolution_convert_fusion.g0 = bf16[512,512]{1,0:T(8,128)(2,1)} fusion(bf16[1024,256]{1,0:T(8,128)(2,1)S(1)} %get-tuple-element.41, bf16[1024,256]{1,0:T(8,128)(2,1)S(1)} %get-tuple-element.38, bf16[256,1024]{1,0:T(8,128)(2,1)S(1)} %get-tuple-element.43, bf16[256,1024]{1,0:T(8,128)(2,1)S(1)} %get-tuple-element.42), kind=kOutput, calls=%fused_computation | convolution fusion | flops 541327360 | bytes 2621440 | tf_op jit(solution)/shard_map/dot_general | solution.py:52
  29.4 1.5 %collective-permute-start.2 = (bf16[512,512]{1,0:T(8,128)(2,1)}, bf16[512,512]{1,0:T(8,128)(2,1)S(1)}, u32[]{:S(2)}, u32[]{:S(2)}) collective-permute-start(bf16[512,512]{1,0:T(8,128)(2,1)} %convolution_convert_fusion.g0), channel_id=1, source_target_pairs={{0,64},{1,65},{2,66},{3,67},{4,68},{5,69},{6,70},{7,71},{8,72},{9,... | collective-permute-start | bytes 1572872 | tf_op jit(solution)/shard_map/ppermute | solution.py:28
  30.9 1.3 copy.6
  32.2 3.2 %collective-permute-start.10 = (bf16[3,256,256]{2,1,0:T(8,128)(2,1)S(1)}, bf16[3,256,256]{2,1,0:T(8,128)(2,1)S(1)}, u32[]{:S(2)}, u32[]{:S(2)}) collective-permute-start(bf16[3,256,256]{2,1,0:T(8,128)(2,1)S(1)} %pad_maximum_fusion.4.refs_0_), channel_id=1, source_target_pairs={{0,12},{1,13},{2,14},{3,15},{4,0},{5,1},{6,2},{7,3},{8,4},{9,5},{1... | collective-permute-start | bytes 1179656 | tf_op jit(solution)/shard_map/ppermute | solution.py:28
  35.5 4.9 %collective-permute-done.8.refs_1_ = bf16[3,256,256]{2,1,0:T(8,128)(2,1)S(1)} collective-permute-done((bf16[3,256,256]{2,1,0:T(8,128)(2,1)S(1)}, bf16[3,256,256]{2,1,0:T(8,128)(2,1)S(1)}, u32[]{:S(2)}, u32[]{:S(2)}) %collective-permute-start.8) | collective-permute-done | bytes 393248 | tf_op jit(solution)/shard_map/ppermute | solution.py:28
  40.3 0.7 collective-permute-start.9
  41.1 1.4 divide_convert_fusion
  42.4 0.7 dynamic-slice_bitcast_fusion.3
  43.2 0.4 collective-permute-done.2.g1
  43.5 0.8 copy-done.2
  44.3 3.6 %collective-permute-start.17 = (bf16[256,256]{1,0:T(8,128)(2,1)S(1)}, bf16[256,256]{1,0:T(8,128)(2,1)S(1)}, u32[]{:S(2)}, u32[]{:S(2)}) collective-permute-start(bf16[256,256]{1,0:T(8,128)(2,1)S(1)} %get-tuple-element.25), channel_id=1, source_target_pairs={{0,48},{1,49},{2,50},{3,51},{4,52},{5,53},{6,54},{7,55},{8,56},{9,... | collective-permute-start | bytes 393224 | tf_op jit(solution)/shard_map/ppermute | solution.py:28
  47.9 3.1 %collective-permute-start.3 = (bf16[512,512]{1,0:T(8,128)(2,1)}, bf16[512,512]{1,0:T(8,128)(2,1)}, u32[]{:S(2)}, u32[]{:S(2)}) collective-permute-start(bf16[512,512]{1,0:T(8,128)(2,1)} %convolution_convert_fusion.g0), channel_id=1, source_target_pairs={{0,128},{1,129},{2,130},{3,131},{4,132},{5,133},{6,134},{7,135},{8... | collective-permute-start | bytes 1572872 | tf_op jit(solution)/shard_map/ppermute | solution.py:28
  51.0 0.9 collective-permute-done.10.refs_3_
  51.9 1.1 collective-permute-start.4
  53.0 5.1 %collective-permute-start.16 = (bf16[256,256]{1,0:T(8,128)(2,1)S(1)}, bf16[256,256]{1,0:T(8,128)(2,1)S(1)}, u32[]{:S(2)}, u32[]{:S(2)}) collective-permute-start(bf16[256,256]{1,0:T(8,128)(2,1)S(1)} %get-tuple-element.24), channel_id=1, source_target_pairs={{0,32},{1,33},{2,34},{3,35},{4,36},{5,37},{6,38},{7,39},{8,40},{9,... | collective-permute-start | bytes 393224 | tf_op jit(solution)/shard_map/ppermute | solution.py:28
  58.1 3.8 %collective-permute-done.16 = bf16[256,256]{1,0:T(8,128)(2,1)S(1)} collective-permute-done((bf16[256,256]{1,0:T(8,128)(2,1)S(1)}, bf16[256,256]{1,0:T(8,128)(2,1)S(1)}, u32[]{:S(2)}, u32[]{:S(2)}) %collective-permute-start.16) | collective-permute-done | bytes 131104 | tf_op jit(solution)/shard_map/ppermute | solution.py:28
  61.9 1.6 %collective-permute-done.15 = bf16[256,256]{1,0:T(8,128)(2,1)S(1)} collective-permute-done((bf16[256,256]{1,0:T(8,128)(2,1)S(1)}, bf16[256,256]{1,0:T(8,128)(2,1)S(1)}, u32[]{:S(2)}, u32[]{:S(2)}) %collective-permute-start.15) | collective-permute-done | bytes 131104 | tf_op jit(solution)/shard_map/ppermute | solution.py:28
  63.6 0.6 copy-done.18
  64.2 0.2 collective-permute-start.13
  64.3 0.1 pad_add_fusion.place
  64.4 2.4 %fusion.8 = (bf16[256,1024]{1,0:T(8,128)(2,1)}, bf16[256,1024]{1,0:T(8,128)(2,1)}) fusion(bf16[512,4096]{1,0:T(8,128)(2,1)} %param.5, s32[]{:T(128)S(6)} %select_n.101, s32[]{:T(128)S(6)} %select_n.106, s32[]{:T(128)S(6)} %select_n.93), kind=kLoop, calls=%fused_computation.32 | loop fusion | bytes 2097164 | tf_op jit(solution)/shard_map/dynamic_slice | solution.py:207
  66.9 0.1 pad_maximum_fusion.3.inverse
  67.0 6.7 %collective-permute-done.4.g3 = bf16[512,512]{1,0:T(8,128)(2,1)} collective-permute-done((bf16[512,512]{1,0:T(8,128)(2,1)}, bf16[512,512]{1,0:T(8,128)(2,1)}, u32[]{:S(2)}, u32[]{:S(2)}) %collective-permute-start.4) | collective-permute-done | bytes 524320 | tf_op jit(solution)/shard_map/ppermute | solution.py:28
  73.7 4.9 %shard_map.56 = bf16[256,1024]{1,0:T(8,128)(2,1)S(1)} custom-call(s32[4]{0:T(128)S(1)} %pad_add_fusion.place, bf16[512,512]{1,0:T(8,128)(2,1)} %convolution_convert_fusion.g0, bf16[512,512]{1,0:T(8,128)(2,1)S(1)} %copy-done.3, bf16[512,512]{1,0:T(8,128)(2,1)} %collective-permute-done.3.g2, bf16[512,512]{1,0:T(8,128)(2,1)} %collective-permute-done.4.g3, ...), custom_call_target="tpu_custom_call" | custom-call | flops 1000 | bytes 1000 | tf_op jit(solution)/shard_map/pallas_call | solution.py:105
  78.7 1.7 %collective-permute-start.18 = (bf16[256,1024]{1,0:T(8,128)(2,1)S(1)}, bf16[256,1024]{1,0:T(8,128)(2,1)S(1)}, u32[]{:S(2)}, u32[]{:S(2)}) collective-permute-start(bf16[256,1024]{1,0:T(8,128)(2,1)S(1)} %shard_map.56), channel_id=1, source_target_pairs={{0,16},{1,17},{2,18},{3,19},{4,20},{5,21},{6,22},{7,23},{8,24},{9,... | collective-permute-start | bytes 1572872 | tf_op jit(solution)/shard_map/ppermute | solution.py:28
  80.4 0.8 convolution_convert_fusion.1.g0
  81.2 0.7 collective-permute-start.19
  81.9 3.0 %collective-permute-start.20 = (bf16[512,512]{1,0:T(8,128)(2,1)S(1)}, bf16[512,512]{1,0:T(8,128)(2,1)S(1)}, u32[]{:S(2)}, u32[]{:S(2)}) collective-permute-start(bf16[512,512]{1,0:T(8,128)(2,1)S(1)} %convolution_convert_fusion.1.g0), channel_id=1, source_target_pairs={{0,128},{1,129},{2,130},{3,131},{4,132},{5,133},{6,134},{7,135},{8... | collective-permute-start | bytes 1572872 | tf_op jit(solution)/shard_map/ppermute | solution.py:28
  84.9 2.0 %collective-permute-start.21 = (bf16[512,512]{1,0:T(8,128)(2,1)S(1)}, bf16[512,512]{1,0:T(8,128)(2,1)S(1)}, u32[]{:S(2)}, u32[]{:S(2)}) collective-permute-start(bf16[512,512]{1,0:T(8,128)(2,1)S(1)} %convolution_convert_fusion.1.g0), channel_id=1, source_target_pairs={{0,192},{1,193},{2,194},{3,195},{4,196},{5,197},{6,198},{7,199},{8... | collective-permute-start | bytes 1572872 | tf_op jit(solution)/shard_map/ppermute | solution.py:28
  86.9 4.9 %shard_map.55 = bf16[256,1024]{1,0:T(8,128)(2,1)S(1)} custom-call(s32[4]{0:T(128)S(1)} %pad_add_fusion.place, bf16[512,512]{1,0:T(8,128)(2,1)} %convolution_convert_fusion.g0, bf16[512,512]{1,0:T(8,128)(2,1)S(1)} %copy-done.3, bf16[512,512]{1,0:T(8,128)(2,1)} %collective-permute-done.3.g2, bf16[512,512]{1,0:T(8,128)(2,1)} %collective-permute-done.4.g3, ...), custom_call_target="tpu_custom_call" | custom-call | flops 1000 | bytes 1000 | tf_op jit(solution)/shard_map/pallas_call | solution.py:105
  91.8 0.8 collective-permute-done.18
  92.6 0.2 add_convert_fusion
  92.8 1.7 %collective-permute-start.24 = (bf16[2,256,256]{2,1,0:T(8,128)(2,1)S(1)}, bf16[2,256,256]{2,1,0:T(8,128)(2,1)S(1)}, u32[]{:S(2)}, u32[]{:S(2)}) collective-permute-start(bf16[2,256,256]{2,1,0:T(8,128)(2,1)S(1)} %pad_maximum_fusion.5.refs_0_), channel_id=1, source_target_pairs={{0,4},{1,5},{2,6},{3,7},{4,8},{5,9},{6,10},{7,11},{8,12},{9,13},{1... | collective-permute-start | bytes 786440 | tf_op jit(solution)/shard_map/ppermute | solution.py:28
  94.5 1.5 collective-permute-start.23
  95.9 0.2 collective-permute-done.19.g1
  96.1 2.4 %collective-permute-start.26 = (bf16[2,256,256]{2,1,0:T(8,128)(2,1)S(1)}, bf16[2,256,256]{2,1,0:T(8,128)(2,1)S(1)}, u32[]{:S(2)}, u32[]{:S(2)}) collective-permute-start(bf16[2,256,256]{2,1,0:T(8,128)(2,1)S(1)} %pad_maximum_fusion.5.refs_0_), channel_id=1, source_target_pairs={{0,12},{1,13},{2,14},{3,15},{4,0},{5,1},{6,2},{7,3},{8,4},{9,5},{1... | collective-permute-start | bytes 786440 | tf_op jit(solution)/shard_map/ppermute | solution.py:28
  98.5 9.2 %collective-permute-done.21.g3 = bf16[512,512]{1,0:T(8,128)(2,1)S(1)} collective-permute-done((bf16[512,512]{1,0:T(8,128)(2,1)S(1)}, bf16[512,512]{1,0:T(8,128)(2,1)S(1)}, u32[]{:S(2)}, u32[]{:S(2)}) %collective-permute-start.21) | collective-permute-done | bytes 524320 | tf_op jit(solution)/shard_map/ppermute | solution.py:28
  107.7 0.8 copy-done.6
  108.5 5.0 %shard_map.57 = (bf16[256,1024]{1,0:T(8,128)(2,1)S(1)}, bf16[256,1024]{1,0:T(8,128)(2,1)S(1)}) custom-call(s32[4]{0:T(128)S(1)} %pad_add_fusion.place, bf16[512,512]{1,0:T(8,128)(2,1)S(1)} %convolution_convert_fusion.1.g0, bf16[512,512]{1,0:T(8,128)(2,1)S(1)} %collective-permute-done.19.g1, bf16[512,512]{1,0:T(8,128)(2,1)S(1)} %collective-permute-done.20.g2, ...), custom_call_target="tpu_custom_call" | custom-call | flops 1000 | bytes 1000 | tf_op jit(solution)/shard_map/pallas_call | solution.py:105
  113.5 0.7 collective-permute-start.22
  114.1 2.5 %collective-permute-start.25 = (bf16[2,256,256]{2,1,0:T(8,128)(2,1)S(1)}, bf16[2,256,256]{2,1,0:T(8,128)(2,1)S(1)}, u32[]{:S(2)}, u32[]{:S(2)}) collective-permute-start(bf16[2,256,256]{2,1,0:T(8,128)(2,1)S(1)} %pad_maximum_fusion.5.refs_0_), channel_id=1, source_target_pairs={{0,8},{1,9},{2,10},{3,11},{4,12},{5,13},{6,14},{7,15},{8,0},{9,1},... | collective-permute-start | bytes 786440 | tf_op jit(solution)/shard_map/ppermute | solution.py:28
  116.7 0.5 collective-permute-start.30
  117.2 6.4 %collective-permute-done.25.refs_2_ = bf16[2,256,256]{2,1,0:T(8,128)(2,1)S(1)} collective-permute-done((bf16[2,256,256]{2,1,0:T(8,128)(2,1)S(1)}, bf16[2,256,256]{2,1,0:T(8,128)(2,1)S(1)}, u32[]{:S(2)}, u32[]{:S(2)}) %collective-permute-start.25) | collective-permute-done | bytes 262176 | tf_op jit(solution)/shard_map/ppermute | solution.py:28
  123.6 7.0 %collective-permute-done.22.m1 = bf16[256,1024]{1,0:T(8,128)(2,1)S(1)} collective-permute-done((bf16[256,1024]{1,0:T(8,128)(2,1)S(1)}, bf16[256,1024]{1,0:T(8,128)(2,1)S(1)}, u32[]{:S(2)}, u32[]{:S(2)}) %collective-permute-start.22) | collective-permute-done | bytes 524320 | tf_op jit(solution)/shard_map/ppermute | solution.py:28
  130.6 2.4 %shard_map.58 = bf16[4,256,256]{2,1,0:T(8,128)(2,1)S(1)} custom-call(s32[4]{0:T(128)S(1)} %pad_add_fusion.place, bf16[256,1024]{1,0:T(8,128)(2,1)S(1)} %get-tuple-element.29.m0, bf16[256,1024]{1,0:T(8,128)(2,1)S(1)} %collective-permute-done.22.m1, bf16[256,1024]{1,0:T(8,128)(2,1)S(1)} %collective-permute-done.23.m2, ...), custom_call_target="tpu_custom_call" | custom-call | flops 1000 | bytes 1000 | tf_op jit(solution)/shard_map/pallas_call | solution.py:151
  133.1 0.1 collective-permute-start.31
  133.2 2.0 %collective-permute-start.32 = (bf16[256,256]{1,0:T(8,128)(2,1)S(1)}, bf16[256,256]{1,0:T(8,128)(2,1)S(1)}, u32[]{:S(2)}, u32[]{:S(2)}) collective-permute-start(bf16[256,256]{1,0:T(8,128)(2,1)S(1)} %get-tuple-element.45), channel_id=1, source_target_pairs={{0,32},{1,33},{2,34},{3,35},{4,36},{5,37},{6,38},{7,39},{8,40},{9,... | collective-permute-start | bytes 393224 | tf_op jit(solution)/shard_map/ppermute | solution.py:28
  135.2 2.4 %collective-permute-start.33 = (bf16[256,256]{1,0:T(8,128)(2,1)S(1)}, bf16[256,256]{1,0:T(8,128)(2,1)S(1)}, u32[]{:S(2)}, u32[]{:S(2)}) collective-permute-start(bf16[256,256]{1,0:T(8,128)(2,1)S(1)} %get-tuple-element.44), channel_id=1, source_target_pairs={{0,48},{1,49},{2,50},{3,51},{4,52},{5,53},{6,54},{7,55},{8,56},{9,... | collective-permute-start | bytes 393224 | tf_op jit(solution)/shard_map/ppermute | solution.py:28
  137.5 2.6 %collective-permute-done.31.b1 = bf16[256,256]{1,0:T(8,128)(2,1)S(1)} collective-permute-done((bf16[256,256]{1,0:T(8,128)(2,1)S(1)}, bf16[256,256]{1,0:T(8,128)(2,1)S(1)}, u32[]{:S(2)}, u32[]{:S(2)}) %collective-permute-start.31) | collective-permute-done | bytes 131104 | tf_op jit(solution)/shard_map/ppermute | solution.py:28
  140.1 6.0 %collective-permute-done.32.b2 = bf16[256,256]{1,0:T(8,128)(2,1)S(1)} collective-permute-done((bf16[256,256]{1,0:T(8,128)(2,1)S(1)}, bf16[256,256]{1,0:T(8,128)(2,1)S(1)}, u32[]{:S(2)}, u32[]{:S(2)}) %collective-permute-start.32) | collective-permute-done | bytes 131104 | tf_op jit(solution)/shard_map/ppermute | solution.py:28
  146.2 2.1 %shard_map.59 = bf16[256,1024]{1,0:T(8,128)(2,1)} custom-call(s32[4]{0:T(128)S(1)} %pad_add_fusion.place, bf16[1024,1024]{1,0:T(8,128)(2,1)S(1)} %copy-done.1, bf16[256,256]{1,0:T(8,128)(2,1)S(1)} %get-tuple-element.47.b0, bf16[256,256]{1,0:T(8,128)(2,1)S(1)} %collective-permute-done.31.b1, bf16[256,256]{1,0:T(8,128)(2,1)S(1)} %collective-permute-done.32.b2, ...), custom_call_target="tpu_custom_call" | custom-call | flops 1000 | bytes 1000 | tf_op jit(solution)/shard_map/pallas_call | solution.py:182
  (65 shorter events, 0.3 us)
Async XLA Ops:
  0.0 1.2 copy-start
  1.2 28.1 %collective-permute-start.1 = (bf16[256,256]{1,0:T(8,128)(2,1)S(1)}, bf16[256,256]{1,0:T(8,128)(2,1)S(1)}, u32[]{:S(2)}, u32[]{:S(2)}) collective-permute-start(bf16[256,256]{1,0:T(8,128)(2,1)S(1)} %constant_dynamic-slice_fusion), channel_id=1, source_target_pairs={{0,2},{1,3},{2,0},{3,1},{4,66},{5,67},{6,64},{7,65},{8,130},{9,131... | collective-permute-start | bytes 393224 | tf_op jit(solution)/shard_map/ppermute | solution.py:28
  9.3 20.0 %collective-permute-start = (bf16[256,256]{1,0:T(8,128)(2,1)S(1)}, bf16[256,256]{1,0:T(8,128)(2,1)S(1)}, u32[]{:S(2)}, u32[]{:S(2)}) collective-permute-start(bf16[256,256]{1,0:T(8,128)(2,1)S(1)} %constant_dynamic-slice_fusion), channel_id=1, source_target_pairs={{0,0},{1,1},{2,2},{3,3},{4,64},{5,65},{6,66},{7,67},{8,128},{9,129... | collective-permute-start | bytes 393224 | tf_op jit(solution)/shard_map/ppermute | solution.py:28
  12.8 10.2 %collective-permute-start.7 = (bf16[256,256]{1,0:T(8,128)(2,1)S(1)}, bf16[256,256]{1,0:T(8,128)(2,1)S(1)}, u32[]{:S(2)}, u32[]{:S(2)}) collective-permute-start(bf16[256,256]{1,0:T(8,128)(2,1)S(1)} %get-tuple-element.35), channel_id=1, source_target_pairs={{0,192},{1,193},{2,194},{3,195},{4,196},{5,197},{6,198},{7,199},{8... | collective-permute-start | bytes 393224 | tf_op jit(solution)/shard_map/ppermute | solution.py:28
  12.9 11.5 %collective-permute-start.6 = (bf16[256,256]{1,0:T(8,128)(2,1)S(1)}, bf16[256,256]{1,0:T(8,128)(2,1)S(1)}, u32[]{:S(2)}, u32[]{:S(2)}) collective-permute-start(bf16[256,256]{1,0:T(8,128)(2,1)S(1)} %get-tuple-element.36), channel_id=1, source_target_pairs={{0,128},{1,129},{2,130},{3,131},{4,132},{5,133},{6,134},{7,135},{8... | collective-permute-start | bytes 393224 | tf_op jit(solution)/shard_map/ppermute | solution.py:28
  18.9 8.6 %collective-permute-start.5 = (bf16[256,256]{1,0:T(8,128)(2,1)S(1)}, bf16[256,256]{1,0:T(8,128)(2,1)S(1)}, u32[]{:S(2)}, u32[]{:S(2)}) collective-permute-start(bf16[256,256]{1,0:T(8,128)(2,1)S(1)} %get-tuple-element.37), channel_id=1, source_target_pairs={{0,64},{1,65},{2,66},{3,67},{4,68},{5,69},{6,70},{7,71},{8,72},{9,... | collective-permute-start | bytes 393224 | tf_op jit(solution)/shard_map/ppermute | solution.py:28
  20.2 7.4 %copy-start.5 = (bf16[512,1024]{1,0:T(8,128)(2,1)S(1)}, bf16[512,1024]{1,0:T(8,128)(2,1)}, u32[]{:S(2)}) copy-start(bf16[512,1024]{1,0:T(8,128)(2,1)} %param.6) | copy-start | bytes 3145732
  27.6 12.8 %collective-permute-start.8 = (bf16[3,256,256]{2,1,0:T(8,128)(2,1)S(1)}, bf16[3,256,256]{2,1,0:T(8,128)(2,1)S(1)}, u32[]{:S(2)}, u32[]{:S(2)}) collective-permute-start(bf16[3,256,256]{2,1,0:T(8,128)(2,1)S(1)} %pad_maximum_fusion.4.refs_0_), channel_id=1, source_target_pairs={{0,4},{1,5},{2,6},{3,7},{4,8},{5,9},{6,10},{7,11},{8,12},{9,13},{1... | collective-permute-start | bytes 1179656 | tf_op jit(solution)/shard_map/ppermute | solution.py:28
  27.7 1.6 %copy-start.7 = (bf16[256,1024]{1,0:T(8,128)(2,1)}, bf16[256,1024]{1,0:T(8,128)(2,1)S(1)}, u32[]{:S(2)}) copy-start(bf16[256,1024]{1,0:T(8,128)(2,1)S(1)} %get-tuple-element.42) | copy-start | bytes 1572868
  27.8 1.6 %copy-start.9 = (bf16[256,1024]{1,0:T(8,128)(2,1)}, bf16[256,1024]{1,0:T(8,128)(2,1)S(1)}, u32[]{:S(2)}) copy-start(bf16[256,1024]{1,0:T(8,128)(2,1)S(1)} %get-tuple-element.43) | copy-start | bytes 1572868
  27.8 3.1 %copy-start.4 = (f32[256,1024]{1,0:T(8,128)S(1)}, f32[256,1024]{1,0:T(8,128)}, u32[]{:S(2)}) copy-start(f32[256,1024]{1,0:T(8,128)} %param.9) | copy-start | bytes 3145732
  29.4 14.1 %collective-permute-start.2 = (bf16[512,512]{1,0:T(8,128)(2,1)}, bf16[512,512]{1,0:T(8,128)(2,1)S(1)}, u32[]{:S(2)}, u32[]{:S(2)}) collective-permute-start(bf16[512,512]{1,0:T(8,128)(2,1)} %convolution_convert_fusion.g0), channel_id=1, source_target_pairs={{0,64},{1,65},{2,66},{3,67},{4,68},{5,69},{6,70},{7,71},{8,72},{9,... | collective-permute-start | bytes 1572872 | tf_op jit(solution)/shard_map/ppermute | solution.py:28
  32.2 19.6 %collective-permute-start.10 = (bf16[3,256,256]{2,1,0:T(8,128)(2,1)S(1)}, bf16[3,256,256]{2,1,0:T(8,128)(2,1)S(1)}, u32[]{:S(2)}, u32[]{:S(2)}) collective-permute-start(bf16[3,256,256]{2,1,0:T(8,128)(2,1)S(1)} %pad_maximum_fusion.4.refs_0_), channel_id=1, source_target_pairs={{0,12},{1,13},{2,14},{3,15},{4,0},{5,1},{6,2},{7,3},{8,4},{9,5},{1... | collective-permute-start | bytes 1179656 | tf_op jit(solution)/shard_map/ppermute | solution.py:28
  35.5 17.5 %collective-permute-start.11 = (bf16[3,256,256]{2,1,0:T(8,128)(2,1)S(1)}, bf16[3,256,256]{2,1,0:T(8,128)(2,1)S(1)}, u32[]{:S(2)}, u32[]{:S(2)}) collective-permute-start(bf16[3,256,256]{2,1,0:T(8,128)(2,1)S(1)} %pad_maximum_fusion.4.refs_0_), channel_id=1, source_target_pairs={{0,1},{1,0},{2,3},{3,2},{4,5},{5,4},{6,7},{7,6},{8,9},{9,8},{10,11... | collective-permute-start | bytes 1179656 | tf_op jit(solution)/shard_map/ppermute | solution.py:28
  40.3 23.2 %collective-permute-start.9 = (bf16[3,256,256]{2,1,0:T(8,128)(2,1)S(1)}, bf16[3,256,256]{2,1,0:T(8,128)(2,1)S(1)}, u32[]{:S(2)}, u32[]{:S(2)}) collective-permute-start(bf16[3,256,256]{2,1,0:T(8,128)(2,1)S(1)} %pad_maximum_fusion.4.refs_0_), channel_id=1, source_target_pairs={{0,8},{1,9},{2,10},{3,11},{4,12},{5,13},{6,14},{7,15},{8,0},{9,1},... | collective-permute-start | bytes 1179656 | tf_op jit(solution)/shard_map/ppermute | solution.py:28
  43.5 0.8 copy-start.2
  44.3 13.8 %collective-permute-start.17 = (bf16[256,256]{1,0:T(8,128)(2,1)S(1)}, bf16[256,256]{1,0:T(8,128)(2,1)S(1)}, u32[]{:S(2)}, u32[]{:S(2)}) collective-permute-start(bf16[256,256]{1,0:T(8,128)(2,1)S(1)} %get-tuple-element.25), channel_id=1, source_target_pairs={{0,48},{1,49},{2,50},{3,51},{4,52},{5,53},{6,54},{7,55},{8,56},{9,... | collective-permute-start | bytes 393224 | tf_op jit(solution)/shard_map/ppermute | solution.py:28
  47.9 19.0 %collective-permute-start.3 = (bf16[512,512]{1,0:T(8,128)(2,1)}, bf16[512,512]{1,0:T(8,128)(2,1)}, u32[]{:S(2)}, u32[]{:S(2)}) collective-permute-start(bf16[512,512]{1,0:T(8,128)(2,1)} %convolution_convert_fusion.g0), channel_id=1, source_target_pairs={{0,128},{1,129},{2,130},{3,131},{4,132},{5,133},{6,134},{7,135},{8... | collective-permute-start | bytes 1572872 | tf_op jit(solution)/shard_map/ppermute | solution.py:28
  51.9 21.8 %collective-permute-start.4 = (bf16[512,512]{1,0:T(8,128)(2,1)}, bf16[512,512]{1,0:T(8,128)(2,1)}, u32[]{:S(2)}, u32[]{:S(2)}) collective-permute-start(bf16[512,512]{1,0:T(8,128)(2,1)} %convolution_convert_fusion.g0), channel_id=1, source_target_pairs={{0,192},{1,193},{2,194},{3,195},{4,196},{5,197},{6,198},{7,199},{8... | collective-permute-start | bytes 1572872 | tf_op jit(solution)/shard_map/ppermute | solution.py:28
  53.0 8.9 %collective-permute-start.16 = (bf16[256,256]{1,0:T(8,128)(2,1)S(1)}, bf16[256,256]{1,0:T(8,128)(2,1)S(1)}, u32[]{:S(2)}, u32[]{:S(2)}) collective-permute-start(bf16[256,256]{1,0:T(8,128)(2,1)S(1)} %get-tuple-element.24), channel_id=1, source_target_pairs={{0,32},{1,33},{2,34},{3,35},{4,36},{5,37},{6,38},{7,39},{8,40},{9,... | collective-permute-start | bytes 393224 | tf_op jit(solution)/shard_map/ppermute | solution.py:28
  58.1 5.4 %copy-start.14 = (bf16[256,256]{1,0:T(8,128)(2,1)}, bf16[256,256]{1,0:T(8,128)(2,1)S(1)}, u32[]{:S(2)}) copy-start(bf16[256,256]{1,0:T(8,128)(2,1)S(1)} %collective-permute-done.17) | copy-start | bytes 393220
  58.1 5.4 %collective-permute-start.15 = (bf16[256,256]{1,0:T(8,128)(2,1)S(1)}, bf16[256,256]{1,0:T(8,128)(2,1)S(1)}, u32[]{:S(2)}, u32[]{:S(2)}) collective-permute-start(bf16[256,256]{1,0:T(8,128)(2,1)S(1)} %get-tuple-element.23), channel_id=1, source_target_pairs={{0,16},{1,17},{2,18},{3,19},{4,20},{5,21},{6,22},{7,23},{8,24},{9,... | collective-permute-start | bytes 393224 | tf_op jit(solution)/shard_map/ppermute | solution.py:28
  61.9 1.7 %copy-start.16 = (bf16[256,256]{1,0:T(8,128)(2,1)}, bf16[256,256]{1,0:T(8,128)(2,1)S(1)}, u32[]{:S(2)}) copy-start(bf16[256,256]{1,0:T(8,128)(2,1)S(1)} %collective-permute-done.16) | copy-start | bytes 393220
  61.9 11.8 %collective-permute-start.12 = (bf16[3,256,256]{2,1,0:T(8,128)(2,1)S(1)}, bf16[3,256,256]{2,1,0:T(8,128)(2,1)S(1)}, u32[]{:S(2)}, u32[]{:S(2)}) collective-permute-start(bf16[3,256,256]{2,1,0:T(8,128)(2,1)S(1)} %collective-permute-done.8.refs_1_), channel_id=1, source_target_pairs={{0,1},{1,0},{2,3},{3,2},{4,5},{5,4},{6,7},{7,6},{8,9},{9,8},{10,11... | collective-permute-start | bytes 1179656 | tf_op jit(solution)/shard_map/ppermute | solution.py:28
  63.5 0.6 copy-start.18
  63.5 10.2 %collective-permute-start.14 = (bf16[3,256,256]{2,1,0:T(8,128)(2,1)S(1)}, bf16[3,256,256]{2,1,0:T(8,128)(2,1)S(1)}, u32[]{:S(2)}, u32[]{:S(2)}) collective-permute-start(bf16[3,256,256]{2,1,0:T(8,128)(2,1)S(1)} %collective-permute-done.10.refs_3_), channel_id=1, source_target_pairs={{0,1},{1,0},{2,3},{3,2},{4,5},{5,4},{6,7},{7,6},{8,9},{9,8},{10,11... | collective-permute-start | bytes 1179656 | tf_op jit(solution)/shard_map/ppermute | solution.py:28
  64.2 9.5 %collective-permute-start.13 = (bf16[3,256,256]{2,1,0:T(8,128)(2,1)S(1)}, bf16[3,256,256]{2,1,0:T(8,128)(2,1)}, u32[]{:S(2)}, u32[]{:S(2)}) collective-permute-start(bf16[3,256,256]{2,1,0:T(8,128)(2,1)S(1)} %collective-permute-done.9.refs_2_), channel_id=1, source_target_pairs={{0,1},{1,0},{2,3},{3,2},{4,5},{5,4},{6,7},{7,6},{8,9},{9,8},{10,11... | collective-permute-start | bytes 1179656 | tf_op jit(solution)/shard_map/ppermute | solution.py:28
  64.3 2.5 %copy-start.13 = (bf16[1,256,256]{2,1,0:T(8,128)(2,1)S(1)}, bf16[1,256,256]{2,1,0:T(8,128)(2,1)}, u32[]{:S(2)}) copy-start(bf16[1,256,256]{2,1,0:T(8,128)(2,1)} %get-tuple-element.48) | copy-start | bytes 393220
  64.3 2.5 %copy-start.15 = (bf16[256,256]{1,0:T(8,128)(2,1)S(1)}, bf16[256,256]{1,0:T(8,128)(2,1)}, u32[]{:S(2)}) copy-start(bf16[256,256]{1,0:T(8,128)(2,1)} %copy-done.14) | copy-start | bytes 393220
  64.3 2.5 %copy-start.17 = (bf16[256,256]{1,0:T(8,128)(2,1)S(1)}, bf16[256,256]{1,0:T(8,128)(2,1)}, u32[]{:S(2)}) copy-start(bf16[256,256]{1,0:T(8,128)(2,1)} %copy-done.16) | copy-start | bytes 393220
  64.3 2.5 %copy-start.19 = (bf16[256,256]{1,0:T(8,128)(2,1)S(1)}, bf16[256,256]{1,0:T(8,128)(2,1)}, u32[]{:S(2)}) copy-start(bf16[256,256]{1,0:T(8,128)(2,1)} %copy-done.18) | copy-start | bytes 393220
  64.3 9.4 %copy-start.3 = (bf16[512,512]{1,0:T(8,128)(2,1)S(1)}, bf16[512,512]{1,0:T(8,128)(2,1)}, u32[]{:S(2)}) copy-start(bf16[512,512]{1,0:T(8,128)(2,1)} %copy-done.2) | copy-start | bytes 1572868
  73.7 6.7 %copy-start.8 = (bf16[256,1024]{1,0:T(8,128)(2,1)S(1)}, bf16[256,1024]{1,0:T(8,128)(2,1)}, u32[]{:S(2)}) copy-start(bf16[256,1024]{1,0:T(8,128)(2,1)} %copy-done.7) | copy-start | bytes 1572868
  73.7 6.7 %copy-start.10 = (bf16[256,1024]{1,0:T(8,128)(2,1)S(1)}, bf16[256,1024]{1,0:T(8,128)(2,1)}, u32[]{:S(2)}) copy-start(bf16[256,1024]{1,0:T(8,128)(2,1)} %copy-done.9) | copy-start | bytes 1572868
  73.7 6.7 %copy-start.11 = (bf16[1024,256]{1,0:T(8,128)(2,1)S(1)}, bf16[1024,256]{1,0:T(8,128)(2,1)}, u32[]{:S(2)}) copy-start(bf16[1024,256]{1,0:T(8,128)(2,1)} %get-tuple-element.39) | copy-start | bytes 1572868
  73.7 6.7 %copy-start.12 = (bf16[1024,256]{1,0:T(8,128)(2,1)S(1)}, bf16[1024,256]{1,0:T(8,128)(2,1)}, u32[]{:S(2)}) copy-start(bf16[1024,256]{1,0:T(8,128)(2,1)} %get-tuple-element.40) | copy-start | bytes 1572868
  78.7 13.9 %collective-permute-start.18 = (bf16[256,1024]{1,0:T(8,128)(2,1)S(1)}, bf16[256,1024]{1,0:T(8,128)(2,1)S(1)}, u32[]{:S(2)}, u32[]{:S(2)}) collective-permute-start(bf16[256,1024]{1,0:T(8,128)(2,1)S(1)} %shard_map.56), channel_id=1, source_target_pairs={{0,16},{1,17},{2,18},{3,19},{4,20},{5,21},{6,22},{7,23},{8,24},{9,... | collective-permute-start | bytes 1572872 | tf_op jit(solution)/shard_map/ppermute | solution.py:28
  81.2 14.9 %collective-permute-start.19 = (bf16[512,512]{1,0:T(8,128)(2,1)S(1)}, bf16[512,512]{1,0:T(8,128)(2,1)S(1)}, u32[]{:S(2)}, u32[]{:S(2)}) collective-permute-start(bf16[512,512]{1,0:T(8,128)(2,1)S(1)} %convolution_convert_fusion.1.g0), channel_id=1, source_target_pairs={{0,64},{1,65},{2,66},{3,67},{4,68},{5,69},{6,70},{7,71},{8,72},{9,... | collective-permute-start | bytes 1572872 | tf_op jit(solution)/shard_map/ppermute | solution.py:28
  81.9 16.6 %collective-permute-start.20 = (bf16[512,512]{1,0:T(8,128)(2,1)S(1)}, bf16[512,512]{1,0:T(8,128)(2,1)S(1)}, u32[]{:S(2)}, u32[]{:S(2)}) collective-permute-start(bf16[512,512]{1,0:T(8,128)(2,1)S(1)} %convolution_convert_fusion.1.g0), channel_id=1, source_target_pairs={{0,128},{1,129},{2,130},{3,131},{4,132},{5,133},{6,134},{7,135},{8... | collective-permute-start | bytes 1572872 | tf_op jit(solution)/shard_map/ppermute | solution.py:28
  84.9 22.8 %collective-permute-start.21 = (bf16[512,512]{1,0:T(8,128)(2,1)S(1)}, bf16[512,512]{1,0:T(8,128)(2,1)S(1)}, u32[]{:S(2)}, u32[]{:S(2)}) collective-permute-start(bf16[512,512]{1,0:T(8,128)(2,1)S(1)} %convolution_convert_fusion.1.g0), channel_id=1, source_target_pairs={{0,192},{1,193},{2,194},{3,195},{4,196},{5,197},{6,198},{7,199},{8... | collective-permute-start | bytes 1572872 | tf_op jit(solution)/shard_map/ppermute | solution.py:28
  92.8 21.3 %collective-permute-start.24 = (bf16[2,256,256]{2,1,0:T(8,128)(2,1)S(1)}, bf16[2,256,256]{2,1,0:T(8,128)(2,1)S(1)}, u32[]{:S(2)}, u32[]{:S(2)}) collective-permute-start(bf16[2,256,256]{2,1,0:T(8,128)(2,1)S(1)} %pad_maximum_fusion.5.refs_0_), channel_id=1, source_target_pairs={{0,4},{1,5},{2,6},{3,7},{4,8},{5,9},{6,10},{7,11},{8,12},{9,13},{1... | collective-permute-start | bytes 786440 | tf_op jit(solution)/shard_map/ppermute | solution.py:28
  94.5 36.1 %collective-permute-start.23 = (bf16[256,1024]{1,0:T(8,128)(2,1)S(1)}, bf16[256,1024]{1,0:T(8,128)(2,1)S(1)}, u32[]{:S(2)}, u32[]{:S(2)}) collective-permute-start(bf16[256,1024]{1,0:T(8,128)(2,1)S(1)} %add_convert_fusion), channel_id=1, source_target_pairs={{0,32},{1,33},{2,34},{3,35},{4,36},{5,37},{6,38},{7,39},{8,40},{9,... | collective-permute-start | bytes 1572872 | tf_op jit(solution)/shard_map/ppermute | solution.py:28
  96.1 20.6 %collective-permute-start.26 = (bf16[2,256,256]{2,1,0:T(8,128)(2,1)S(1)}, bf16[2,256,256]{2,1,0:T(8,128)(2,1)S(1)}, u32[]{:S(2)}, u32[]{:S(2)}) collective-permute-start(bf16[2,256,256]{2,1,0:T(8,128)(2,1)S(1)} %pad_maximum_fusion.5.refs_0_), channel_id=1, source_target_pairs={{0,12},{1,13},{2,14},{3,15},{4,0},{5,1},{6,2},{7,3},{8,4},{9,5},{1... | collective-permute-start | bytes 786440 | tf_op jit(solution)/shard_map/ppermute | solution.py:28
  98.5 18.2 %collective-permute-start.27 = (bf16[2,256,256]{2,1,0:T(8,128)(2,1)S(1)}, bf16[2,256,256]{2,1,0:T(8,128)(2,1)S(1)}, u32[]{:S(2)}, u32[]{:S(2)}) collective-permute-start(bf16[2,256,256]{2,1,0:T(8,128)(2,1)S(1)} %pad_maximum_fusion.5.refs_0_), channel_id=1, source_target_pairs={{0,1},{1,0},{2,3},{3,2},{4,5},{5,4},{6,7},{7,6},{8,9},{9,8},{10,11... | collective-permute-start | bytes 786440 | tf_op jit(solution)/shard_map/ppermute | solution.py:28
  107.7 0.8 copy-start.6
  113.5 17.2 %collective-permute-start.22 = (bf16[256,1024]{1,0:T(8,128)(2,1)S(1)}, bf16[256,1024]{1,0:T(8,128)(2,1)S(1)}, u32[]{:S(2)}, u32[]{:S(2)}) collective-permute-start(bf16[256,1024]{1,0:T(8,128)(2,1)S(1)} %get-tuple-element.30), channel_id=1, source_target_pairs={{0,16},{1,17},{2,18},{3,19},{4,20},{5,21},{6,22},{7,23},{8,24},{9,... | collective-permute-start | bytes 1572872 | tf_op jit(solution)/shard_map/ppermute | solution.py:28
  114.1 9.5 %collective-permute-start.25 = (bf16[2,256,256]{2,1,0:T(8,128)(2,1)S(1)}, bf16[2,256,256]{2,1,0:T(8,128)(2,1)S(1)}, u32[]{:S(2)}, u32[]{:S(2)}) collective-permute-start(bf16[2,256,256]{2,1,0:T(8,128)(2,1)S(1)} %pad_maximum_fusion.5.refs_0_), channel_id=1, source_target_pairs={{0,8},{1,9},{2,10},{3,11},{4,12},{5,13},{6,14},{7,15},{8,0},{9,1},... | collective-permute-start | bytes 786440 | tf_op jit(solution)/shard_map/ppermute | solution.py:28
  116.7 6.9 %collective-permute-start.28 = (bf16[2,256,256]{2,1,0:T(8,128)(2,1)S(1)}, bf16[2,256,256]{2,1,0:T(8,128)(2,1)S(1)}, u32[]{:S(2)}, u32[]{:S(2)}) collective-permute-start(bf16[2,256,256]{2,1,0:T(8,128)(2,1)S(1)} %collective-permute-done.24.refs_1_), channel_id=1, source_target_pairs={{0,1},{1,0},{2,3},{3,2},{4,5},{5,4},{6,7},{7,6},{8,9},{9,8},{10,11... | collective-permute-start | bytes 786440 | tf_op jit(solution)/shard_map/ppermute | solution.py:28
  116.7 6.9 %collective-permute-start.30 = (bf16[2,256,256]{2,1,0:T(8,128)(2,1)S(1)}, bf16[2,256,256]{2,1,0:T(8,128)(2,1)S(1)}, u32[]{:S(2)}, u32[]{:S(2)}) collective-permute-start(bf16[2,256,256]{2,1,0:T(8,128)(2,1)S(1)} %collective-permute-done.26.refs_3_), channel_id=1, source_target_pairs={{0,1},{1,0},{2,3},{3,2},{4,5},{5,4},{6,7},{7,6},{8,9},{9,8},{10,11... | collective-permute-start | bytes 786440 | tf_op jit(solution)/shard_map/ppermute | solution.py:28
  123.6 7.0 %collective-permute-start.29 = (bf16[2,256,256]{2,1,0:T(8,128)(2,1)S(1)}, bf16[2,256,256]{2,1,0:T(8,128)(2,1)S(1)}, u32[]{:S(2)}, u32[]{:S(2)}) collective-permute-start(bf16[2,256,256]{2,1,0:T(8,128)(2,1)S(1)} %collective-permute-done.25.refs_2_), channel_id=1, source_target_pairs={{0,1},{1,0},{2,3},{3,2},{4,5},{5,4},{6,7},{7,6},{8,9},{9,8},{10,11... | collective-permute-start | bytes 786440 | tf_op jit(solution)/shard_map/ppermute | solution.py:28
  130.6 15.5 %copy-start.1 = (bf16[1024,1024]{1,0:T(8,128)(2,1)S(1)}, bf16[1024,1024]{1,0:T(8,128)(2,1)}, u32[]{:S(2)}) copy-start(bf16[1024,1024]{1,0:T(8,128)(2,1)} %basis.1) | copy-start | bytes 6291460
  133.1 7.1 %collective-permute-start.31 = (bf16[256,256]{1,0:T(8,128)(2,1)S(1)}, bf16[256,256]{1,0:T(8,128)(2,1)S(1)}, u32[]{:S(2)}, u32[]{:S(2)}) collective-permute-start(bf16[256,256]{1,0:T(8,128)(2,1)S(1)} %get-tuple-element.46), channel_id=1, source_target_pairs={{0,16},{1,17},{2,18},{3,19},{4,20},{5,21},{6,22},{7,23},{8,24},{9,... | collective-permute-start | bytes 393224 | tf_op jit(solution)/shard_map/ppermute | solution.py:28
  133.2 13.0 %collective-permute-start.32 = (bf16[256,256]{1,0:T(8,128)(2,1)S(1)}, bf16[256,256]{1,0:T(8,128)(2,1)S(1)}, u32[]{:S(2)}, u32[]{:S(2)}) collective-permute-start(bf16[256,256]{1,0:T(8,128)(2,1)S(1)} %get-tuple-element.45), channel_id=1, source_target_pairs={{0,32},{1,33},{2,34},{3,35},{4,36},{5,37},{6,38},{7,39},{8,40},{9,... | collective-permute-start | bytes 393224 | tf_op jit(solution)/shard_map/ppermute | solution.py:28
  135.2 11.0 %collective-permute-start.33 = (bf16[256,256]{1,0:T(8,128)(2,1)S(1)}, bf16[256,256]{1,0:T(8,128)(2,1)S(1)}, u32[]{:S(2)}, u32[]{:S(2)}) collective-permute-start(bf16[256,256]{1,0:T(8,128)(2,1)S(1)} %get-tuple-element.44), channel_id=1, source_target_pairs={{0,48},{1,49},{2,50},{3,51},{4,52},{5,53},{6,54},{7,55},{8,56},{9,... | collective-permute-start | bytes 393224 | tf_op jit(solution)/shard_map/ppermute | solution.py:28

commit v4 on v3

--- a/solution.py
+++ b/solution.py
@@ -248,7 +248,7 @@
     def level(e):
         return lax.dynamic_slice_in_dim(inverse, (z ^ e) * quarter, quarter, 0)
 
-    inverse = jnp.stack([level(0)] + [across_z(after(level(e), upper[1], pieces), e) for e in (1, 2, 3)])
+    inverse = jnp.stack([level(0)] + [across_z(after(level(e), upper[1], pieces, own[2]), e) for e in (1, 2, 3)])
 
     local = (mine, rest, own, other)
     (m3,) = product(place, 0, 1, quarter, upper, *local)

time: 149 us -> 152 us (1.020)
  waiting for transfers between devices: 55 us -> 57.3 us
    ppermute x34, waiting for transfers between devices: 55 us -> 57.3 us  [moved(): return lax.ppermute(block, ('dp', 'owner'), route)]
    unnamed x41 -> x39, local copies, waits for them, and re-layouts: 3.72 us -> 4.98 us
  transfers between devices with their start and end apart: 34 -> 34, of which waited for: 15 -> 14; matrix products, arithmetic and copies ran while one was open for 8% -> 8% of each run, Pallas kernels for 7% -> 7%
where the time goes in v4:
time: 152 us; the launch traced here: 151 us
  starting transfers between devices  57.8 us (38%)
  waiting for transfers between devices  57.3 us (38%)
  Pallas kernels  19.2 us (13%)
  local copies, waits for them, and re-layouts  12.1 us (8%)
  matrix products  2.32 us (2%)
  other arithmetic  1.78 us (1%)
    ppermute x34, starting transfers between devices, moved(): return lax.ppermute(block, ('dp', 'owner'), route)  57.8 us
    ppermute x34, waiting for transfers between devices, moved(): return lax.ppermute(block, ('dp', 'owner'), route)  57.3 us
    pallas_call x3, Pallas kernels, product(): pl.pallas_call(functools.partial(product_kernel, start), out_shape=[jax.S...  14.8 us
    unnamed x39, local copies, waits for them, and re-layouts  4.98 us
    dynamic_slice x2, local copies, waits for them, and re-layouts, piece(): lax.dynamic_slice(inputs, (rows * half, b % NY * block + col), (half, wid...  3.54 us
  transfers between devices with their start and end apart: 34, of which 14 were waited for; matrix products, arithmetic and copies ran while one was open for 8% of the time, Pallas kernels for 7%

profile of v4, /device:TPU:8, one launch (start us, length us, event | category | flops | bytes accessed | tf_op | source)
XLA Modules:
  0.0 150.8 jit_solution(4032953807982180579)
XLA Ops:
  0.0 1.1 fusion.9
  1.1 0.1 copy-done
  1.2 8.1 %collective-permute-start.1 = (bf16[256,256]{1,0:T(8,128)(2,1)S(1)}, bf16[256,256]{1,0:T(8,128)(2,1)S(1)}, u32[]{:S(2)}, u32[]{:S(2)}) collective-permute-start(bf16[256,256]{1,0:T(8,128)(2,1)S(1)} %constant_dynamic-slice_fusion), channel_id=1, source_target_pairs={{0,2},{1,3},{2,0},{3,1},{4,66},{5,67},{6,64},{7,65},{8,130},{9,131... | collective-permute-start | bytes 393224 | tf_op jit(solution)/shard_map/ppermute | solution.py:28
  9.3 3.4 %collective-permute-start = (bf16[256,256]{1,0:T(8,128)(2,1)S(1)}, bf16[256,256]{1,0:T(8,128)(2,1)S(1)}, u32[]{:S(2)}, u32[]{:S(2)}) collective-permute-start(bf16[256,256]{1,0:T(8,128)(2,1)S(1)} %constant_dynamic-slice_fusion), channel_id=1, source_target_pairs={{0,0},{1,1},{2,2},{3,3},{4,64},{5,65},{6,66},{7,67},{8,128},{9,129... | collective-permute-start | bytes 393224 | tf_op jit(solution)/shard_map/ppermute | solution.py:28
  12.8 0.1 collective-permute-start.7
  12.9 6.0 %collective-permute-start.6 = (bf16[256,256]{1,0:T(8,128)(2,1)S(1)}, bf16[256,256]{1,0:T(8,128)(2,1)S(1)}, u32[]{:S(2)}, u32[]{:S(2)}) collective-permute-start(bf16[256,256]{1,0:T(8,128)(2,1)S(1)} %get-tuple-element.36), channel_id=1, source_target_pairs={{0,128},{1,129},{2,130},{3,131},{4,132},{5,133},{6,134},{7,135},{8... | collective-permute-start | bytes 393224 | tf_op jit(solution)/shard_map/ppermute | solution.py:28
  18.9 1.3 collective-permute-start.5
  20.2 2.7 %constant_dynamic-slice_fusion.2 = (bf16[1024,256]{1,0:T(8,128)(2,1)S(1)}, bf16[1024,256]{1,0:T(8,128)(2,1)}, bf16[1024,256]{1,0:T(8,128)(2,1)}, bf16[1024,256]{1,0:T(8,128)(2,1)S(1)}) fusion(bf16[1024,1024]{1,0:T(8,128)(2,1)} %basis.1, s32[]{:T(128)S(6)} %select_n.102, s32[]{:T(128)S(6)} %select_n.92, s32[]{:T(128)S(6)} %select_n.91, s32[]{:T(128)S(6)} %select_n.103), kind=kLoop, calls=%fused_computation.24 | loop fusion | bytes 4194320 | tf_op jit(solution)/shard_map/dynamic_slice | solution.py:225
  22.9 1.4 collective-permute-done.6
  24.4 3.1 %collective-permute-done.5 = bf16[256,256]{1,0:T(8,128)(2,1)S(1)} collective-permute-done((bf16[256,256]{1,0:T(8,128)(2,1)S(1)}, bf16[256,256]{1,0:T(8,128)(2,1)S(1)}, u32[]{:S(2)}, u32[]{:S(2)}) %collective-permute-start.5) | collective-permute-done | bytes 131104 | tf_op jit(solution)/shard_map/ppermute | solution.py:28
  27.6 0.1 collective-permute-start.8
  27.7 0.1 constant_dynamic-slice_fusion.4
  27.8 1.6 %convolution_convert_fusion.g0 = bf16[512,512]{1,0:T(8,128)(2,1)} fusion(bf16[1024,256]{1,0:T(8,128)(2,1)S(1)} %get-tuple-element.41, bf16[1024,256]{1,0:T(8,128)(2,1)S(1)} %get-tuple-element.38, bf16[256,1024]{1,0:T(8,128)(2,1)S(1)} %get-tuple-element.43, bf16[256,1024]{1,0:T(8,128)(2,1)S(1)} %get-tuple-element.42), kind=kOutput, calls=%fused_computation | convolution fusion | flops 541327360 | bytes 2621440 | tf_op jit(solution)/shard_map/dot_general | solution.py:52
  29.4 1.5 collective-permute-start.2
  30.9 9.5 %collective-permute-done.8.refs_1_ = bf16[3,256,256]{2,1,0:T(8,128)(2,1)S(1)} collective-permute-done((bf16[3,256,256]{2,1,0:T(8,128)(2,1)S(1)}, bf16[3,256,256]{2,1,0:T(8,128)(2,1)S(1)}, u32[]{:S(2)}, u32[]{:S(2)}) %collective-permute-start.8) | collective-permute-done | bytes 393248 | tf_op jit(solution)/shard_map/ppermute | solution.py:28
  40.3 0.7 collective-permute-start.9
  41.1 1.0 collective-permute-start.10
  42.1 2.6 %copy.6 = f32[256,1024]{0,1:T(8,128)} copy(f32[256,1024]{1,0:T(8,128)} %param.9) | data formatting | bytes 2097152 | tf_op args[4]
  44.7 1.4 divide_convert_fusion
  46.0 0.7 dynamic-slice_bitcast_fusion.3
  46.8 2.9 %collective-permute-start.3 = (bf16[512,512]{1,0:T(8,128)(2,1)}, bf16[512,512]{1,0:T(8,128)(2,1)}, u32[]{:S(2)}, u32[]{:S(2)}) collective-permute-start(bf16[512,512]{1,0:T(8,128)(2,1)} %convolution_convert_fusion.g0), channel_id=1, source_target_pairs={{0,128},{1,129},{2,130},{3,131},{4,132},{5,133},{6,134},{7,135},{8... | collective-permute-start | bytes 1572872 | tf_op jit(solution)/shard_map/ppermute | solution.py:28
  49.7 0.8 copy-done.2
  50.4 0.1 collective-permute-start.4
  50.6 1.8 %collective-permute-done.9.refs_2_ = bf16[3,256,256]{2,1,0:T(8,128)(2,1)S(1)} collective-permute-done((bf16[3,256,256]{2,1,0:T(8,128)(2,1)S(1)}, bf16[3,256,256]{2,1,0:T(8,128)(2,1)S(1)}, u32[]{:S(2)}, u32[]{:S(2)}) %collective-permute-start.9) | collective-permute-done | bytes 393248 | tf_op jit(solution)/shard_map/ppermute | solution.py:28
  52.4 3.9 %collective-permute-start.17 = (bf16[256,256]{1,0:T(8,128)(2,1)S(1)}, bf16[256,256]{1,0:T(8,128)(2,1)S(1)}, u32[]{:S(2)}, u32[]{:S(2)}) collective-permute-start(bf16[256,256]{1,0:T(8,128)(2,1)S(1)} %get-tuple-element.25), channel_id=1, source_target_pairs={{0,48},{1,49},{2,50},{3,51},{4,52},{5,53},{6,54},{7,55},{8,56},{9,... | collective-permute-start | bytes 393224 | tf_op jit(solution)/shard_map/ppermute | solution.py:28
  56.3 3.3 %collective-permute-done.10.refs_3_ = bf16[3,256,256]{2,1,0:T(8,128)(2,1)S(1)} collective-permute-done((bf16[3,256,256]{2,1,0:T(8,128)(2,1)S(1)}, bf16[3,256,256]{2,1,0:T(8,128)(2,1)S(1)}, u32[]{:S(2)}, u32[]{:S(2)}) %collective-permute-start.10) | collective-permute-done | bytes 393248 | tf_op jit(solution)/shard_map/ppermute | solution.py:28
  59.6 5.1 %collective-permute-start.16 = (bf16[256,256]{1,0:T(8,128)(2,1)S(1)}, bf16[256,256]{1,0:T(8,128)(2,1)S(1)}, u32[]{:S(2)}, u32[]{:S(2)}) collective-permute-start(bf16[256,256]{1,0:T(8,128)(2,1)S(1)} %get-tuple-element.24), channel_id=1, source_target_pairs={{0,32},{1,33},{2,34},{3,35},{4,36},{5,37},{6,38},{7,39},{8,40},{9,... | collective-permute-start | bytes 393224 | tf_op jit(solution)/shard_map/ppermute | solution.py:28
  64.7 0.1 collective-permute-start.12
  64.8 3.7 %collective-permute-done.16 = bf16[256,256]{1,0:T(8,128)(2,1)S(1)} collective-permute-done((bf16[256,256]{1,0:T(8,128)(2,1)S(1)}, bf16[256,256]{1,0:T(8,128)(2,1)S(1)}, u32[]{:S(2)}, u32[]{:S(2)}) %collective-permute-start.16) | collective-permute-done | bytes 131104 | tf_op jit(solution)/shard_map/ppermute | solution.py:28
  68.5 1.5 %collective-permute-done.15 = bf16[256,256]{1,0:T(8,128)(2,1)S(1)} collective-permute-done((bf16[256,256]{1,0:T(8,128)(2,1)S(1)}, bf16[256,256]{1,0:T(8,128)(2,1)S(1)}, u32[]{:S(2)}, u32[]{:S(2)}) %collective-permute-start.15) | collective-permute-done | bytes 131104 | tf_op jit(solution)/shard_map/ppermute | solution.py:28
  70.0 0.6 copy-done.17
  70.7 0.0 collective-permute-start.13
  70.7 0.1 pad_add_fusion.place
  70.8 2.4 %fusion.8 = (bf16[256,1024]{1,0:T(8,128)(2,1)}, bf16[256,1024]{1,0:T(8,128)(2,1)}) fusion(bf16[512,4096]{1,0:T(8,128)(2,1)} %param.5, s32[]{:T(128)S(6)} %select_n.101, s32[]{:T(128)S(6)} %select_n.106, s32[]{:T(128)S(6)} %select_n.93), kind=kLoop, calls=%fused_computation.32 | loop fusion | bytes 2097164 | tf_op jit(solution)/shard_map/dynamic_slice | solution.py:207
  73.2 0.1 pad_maximum_fusion.3.inverse
  73.3 0.8 collective-permute-done.4.g3
  74.2 0.0 copy-start.10
  74.2 4.9 %shard_map.56 = bf16[256,1024]{1,0:T(8,128)(2,1)S(1)} custom-call(s32[4]{0:T(128)S(1)} %pad_add_fusion.place, bf16[512,512]{1,0:T(8,128)(2,1)} %convolution_convert_fusion.g0, bf16[512,512]{1,0:T(8,128)(2,1)S(1)} %copy-done.3, bf16[512,512]{1,0:T(8,128)(2,1)} %collective-permute-done.3.g2, bf16[512,512]{1,0:T(8,128)(2,1)} %collective-permute-done.4.g3, ...), custom_call_target="tpu_custom_call" | custom-call | flops 1000 | bytes 1000 | tf_op jit(solution)/shard_map/pallas_call | solution.py:105
  79.1 1.4 collective-permute-start.18
  80.6 0.8 convolution_convert_fusion.1.g0
  81.3 0.7 collective-permute-start.19
  82.0 3.0 %collective-permute-start.20 = (bf16[512,512]{1,0:T(8,128)(2,1)S(1)}, bf16[512,512]{1,0:T(8,128)(2,1)S(1)}, u32[]{:S(2)}, u32[]{:S(2)}) collective-permute-start(bf16[512,512]{1,0:T(8,128)(2,1)S(1)} %convolution_convert_fusion.1.g0), channel_id=1, source_target_pairs={{0,128},{1,129},{2,130},{3,131},{4,132},{5,133},{6,134},{7,135},{8... | collective-permute-start | bytes 1572872 | tf_op jit(solution)/shard_map/ppermute | solution.py:28
  85.0 2.0 %collective-permute-start.21 = (bf16[512,512]{1,0:T(8,128)(2,1)S(1)}, bf16[512,512]{1,0:T(8,128)(2,1)S(1)}, u32[]{:S(2)}, u32[]{:S(2)}) collective-permute-start(bf16[512,512]{1,0:T(8,128)(2,1)S(1)} %convolution_convert_fusion.1.g0), channel_id=1, source_target_pairs={{0,192},{1,193},{2,194},{3,195},{4,196},{5,197},{6,198},{7,199},{8... | collective-permute-start | bytes 1572872 | tf_op jit(solution)/shard_map/ppermute | solution.py:28
  87.1 4.9 %shard_map.55 = bf16[256,1024]{1,0:T(8,128)(2,1)S(1)} custom-call(s32[4]{0:T(128)S(1)} %pad_add_fusion.place, bf16[512,512]{1,0:T(8,128)(2,1)} %convolution_convert_fusion.g0, bf16[512,512]{1,0:T(8,128)(2,1)S(1)} %copy-done.3, bf16[512,512]{1,0:T(8,128)(2,1)} %collective-permute-done.3.g2, bf16[512,512]{1,0:T(8,128)(2,1)} %collective-permute-done.4.g3, ...), custom_call_target="tpu_custom_call" | custom-call | flops 1000 | bytes 1000 | tf_op jit(solution)/shard_map/pallas_call | solution.py:105
  92.0 1.2 collective-permute-done.18
  93.1 0.2 add_convert_fusion
  93.3 2.6 %collective-permute-start.24 = (bf16[2,256,256]{2,1,0:T(8,128)(2,1)S(1)}, bf16[2,256,256]{2,1,0:T(8,128)(2,1)S(1)}, u32[]{:S(2)}, u32[]{:S(2)}) collective-permute-start(bf16[2,256,256]{2,1,0:T(8,128)(2,1)S(1)} %pad_maximum_fusion.5.refs_0_), channel_id=1, source_target_pairs={{0,4},{1,5},{2,6},{3,7},{4,8},{5,9},{6,10},{7,11},{8,12},{9,13},{1... | collective-permute-start | bytes 786440 | tf_op jit(solution)/shard_map/ppermute | solution.py:28
  95.9 3.6 %collective-permute-start.23 = (bf16[256,1024]{1,0:T(8,128)(2,1)S(1)}, bf16[256,1024]{1,0:T(8,128)(2,1)S(1)}, u32[]{:S(2)}, u32[]{:S(2)}) collective-permute-start(bf16[256,1024]{1,0:T(8,128)(2,1)S(1)} %add_convert_fusion), channel_id=1, source_target_pairs={{0,32},{1,33},{2,34},{3,35},{4,36},{5,37},{6,38},{7,39},{8,40},{9,... | collective-permute-start | bytes 1572872 | tf_op jit(solution)/shard_map/ppermute | solution.py:28
  99.5 2.2 %collective-permute-start.26 = (bf16[2,256,256]{2,1,0:T(8,128)(2,1)S(1)}, bf16[2,256,256]{2,1,0:T(8,128)(2,1)S(1)}, u32[]{:S(2)}, u32[]{:S(2)}) collective-permute-start(bf16[2,256,256]{2,1,0:T(8,128)(2,1)S(1)} %pad_maximum_fusion.5.refs_0_), channel_id=1, source_target_pairs={{0,12},{1,13},{2,14},{3,15},{4,0},{5,1},{6,2},{7,3},{8,4},{9,5},{1... | collective-permute-start | bytes 786440 | tf_op jit(solution)/shard_map/ppermute | solution.py:28
  101.8 6.1 %collective-permute-done.21.g3 = bf16[512,512]{1,0:T(8,128)(2,1)S(1)} collective-permute-done((bf16[512,512]{1,0:T(8,128)(2,1)S(1)}, bf16[512,512]{1,0:T(8,128)(2,1)S(1)}, u32[]{:S(2)}, u32[]{:S(2)}) %collective-permute-start.21) | collective-permute-done | bytes 524320 | tf_op jit(solution)/shard_map/ppermute | solution.py:28
  107.8 0.8 copy-done.5
  108.6 5.0 %shard_map.57 = (bf16[256,1024]{1,0:T(8,128)(2,1)S(1)}, bf16[256,1024]{1,0:T(8,128)(2,1)S(1)}) custom-call(s32[4]{0:T(128)S(1)} %pad_add_fusion.place, bf16[512,512]{1,0:T(8,128)(2,1)S(1)} %convolution_convert_fusion.1.g0, bf16[512,512]{1,0:T(8,128)(2,1)S(1)} %collective-permute-done.19.g1, bf16[512,512]{1,0:T(8,128)(2,1)S(1)} %collective-permute-done.20.g2, ...), custom_call_target="tpu_custom_call" | custom-call | flops 1000 | bytes 1000 | tf_op jit(solution)/shard_map/pallas_call | solution.py:105
  113.6 1.0 collective-permute-start.22
  114.6 1.8 %collective-permute-start.25 = (bf16[2,256,256]{2,1,0:T(8,128)(2,1)S(1)}, bf16[2,256,256]{2,1,0:T(8,128)(2,1)S(1)}, u32[]{:S(2)}, u32[]{:S(2)}) collective-permute-start(bf16[2,256,256]{2,1,0:T(8,128)(2,1)S(1)} %pad_maximum_fusion.5.refs_0_), channel_id=1, source_target_pairs={{0,8},{1,9},{2,10},{3,11},{4,12},{5,13},{6,14},{7,15},{8,0},{9,1},... | collective-permute-start | bytes 786440 | tf_op jit(solution)/shard_map/ppermute | solution.py:28
  116.4 0.5 collective-permute-start.30
  117.0 7.1 %collective-permute-done.25.refs_2_ = bf16[2,256,256]{2,1,0:T(8,128)(2,1)S(1)} collective-permute-done((bf16[2,256,256]{2,1,0:T(8,128)(2,1)S(1)}, bf16[2,256,256]{2,1,0:T(8,128)(2,1)S(1)}, u32[]{:S(2)}, u32[]{:S(2)}) %collective-permute-start.25) | collective-permute-done | bytes 262176 | tf_op jit(solution)/shard_map/ppermute | solution.py:28
  124.1 8.9 %collective-permute-done.22.m1 = bf16[256,1024]{1,0:T(8,128)(2,1)S(1)} collective-permute-done((bf16[256,1024]{1,0:T(8,128)(2,1)S(1)}, bf16[256,1024]{1,0:T(8,128)(2,1)S(1)}, u32[]{:S(2)}, u32[]{:S(2)}) %collective-permute-start.22) | collective-permute-done | bytes 524320 | tf_op jit(solution)/shard_map/ppermute | solution.py:28
  133.0 2.4 %shard_map.58 = bf16[4,256,256]{2,1,0:T(8,128)(2,1)S(1)} custom-call(s32[4]{0:T(128)S(1)} %pad_add_fusion.place, bf16[256,1024]{1,0:T(8,128)(2,1)S(1)} %get-tuple-element.29.m0, bf16[256,1024]{1,0:T(8,128)(2,1)S(1)} %collective-permute-done.22.m1, bf16[256,1024]{1,0:T(8,128)(2,1)S(1)} %collective-permute-done.23.m2, ...), custom_call_target="tpu_custom_call" | custom-call | flops 1000 | bytes 1000 | tf_op jit(solution)/shard_map/pallas_call | solution.py:151
  135.4 0.1 collective-permute-start.31
  135.5 3.2 %collective-permute-start.32 = (bf16[256,256]{1,0:T(8,128)(2,1)S(1)}, bf16[256,256]{1,0:T(8,128)(2,1)S(1)}, u32[]{:S(2)}, u32[]{:S(2)}) collective-permute-start(bf16[256,256]{1,0:T(8,128)(2,1)S(1)} %get-tuple-element.45), channel_id=1, source_target_pairs={{0,32},{1,33},{2,34},{3,35},{4,36},{5,37},{6,38},{7,39},{8,40},{9,... | collective-permute-start | bytes 393224 | tf_op jit(solution)/shard_map/ppermute | solution.py:28
  138.8 1.1 collective-permute-start.33
  139.9 3.3 %collective-permute-done.31.b1 = bf16[256,256]{1,0:T(8,128)(2,1)S(1)} collective-permute-done((bf16[256,256]{1,0:T(8,128)(2,1)S(1)}, bf16[256,256]{1,0:T(8,128)(2,1)S(1)}, u32[]{:S(2)}, u32[]{:S(2)}) %collective-permute-start.31) | collective-permute-done | bytes 131104 | tf_op jit(solution)/shard_map/ppermute | solution.py:28
  143.2 5.6 %collective-permute-done.32.b2 = bf16[256,256]{1,0:T(8,128)(2,1)S(1)} collective-permute-done((bf16[256,256]{1,0:T(8,128)(2,1)S(1)}, bf16[256,256]{1,0:T(8,128)(2,1)S(1)}, u32[]{:S(2)}, u32[]{:S(2)}) %collective-permute-start.32) | collective-permute-done | bytes 131104 | tf_op jit(solution)/shard_map/ppermute | solution.py:28
  148.8 2.1 %shard_map.59 = bf16[256,1024]{1,0:T(8,128)(2,1)} custom-call(s32[4]{0:T(128)S(1)} %pad_add_fusion.place, bf16[1024,1024]{1,0:T(8,128)(2,1)S(1)} %copy-done.1, bf16[256,256]{1,0:T(8,128)(2,1)S(1)} %get-tuple-element.47.b0, bf16[256,256]{1,0:T(8,128)(2,1)S(1)} %collective-permute-done.31.b1, bf16[256,256]{1,0:T(8,128)(2,1)S(1)} %collective-permute-done.32.b2, ...), custom_call_target="tpu_custom_call" | custom-call | flops 1000 | bytes 1000 | tf_op jit(solution)/shard_map/pallas_call | solution.py:182
  (63 shorter events, 0.3 us)
Async XLA Ops:
  0.0 1.2 copy-start
  1.2 28.1 %collective-permute-start.1 = (bf16[256,256]{1,0:T(8,128)(2,1)S(1)}, bf16[256,256]{1,0:T(8,128)(2,1)S(1)}, u32[]{:S(2)}, u32[]{:S(2)}) collective-permute-start(bf16[256,256]{1,0:T(8,128)(2,1)S(1)} %constant_dynamic-slice_fusion), channel_id=1, source_target_pairs={{0,2},{1,3},{2,0},{3,1},{4,66},{5,67},{6,64},{7,65},{8,130},{9,131... | collective-permute-start | bytes 393224 | tf_op jit(solution)/shard_map/ppermute | solution.py:28
  9.3 20.0 %collective-permute-start = (bf16[256,256]{1,0:T(8,128)(2,1)S(1)}, bf16[256,256]{1,0:T(8,128)(2,1)S(1)}, u32[]{:S(2)}, u32[]{:S(2)}) collective-permute-start(bf16[256,256]{1,0:T(8,128)(2,1)S(1)} %constant_dynamic-slice_fusion), channel_id=1, source_target_pairs={{0,0},{1,1},{2,2},{3,3},{4,64},{5,65},{6,66},{7,67},{8,128},{9,129... | collective-permute-start | bytes 393224 | tf_op jit(solution)/shard_map/ppermute | solution.py:28
  12.8 10.2 %collective-permute-start.7 = (bf16[256,256]{1,0:T(8,128)(2,1)S(1)}, bf16[256,256]{1,0:T(8,128)(2,1)S(1)}, u32[]{:S(2)}, u32[]{:S(2)}) collective-permute-start(bf16[256,256]{1,0:T(8,128)(2,1)S(1)} %get-tuple-element.35), channel_id=1, source_target_pairs={{0,192},{1,193},{2,194},{3,195},{4,196},{5,197},{6,198},{7,199},{8... | collective-permute-start | bytes 393224 | tf_op jit(solution)/shard_map/ppermute | solution.py:28
  12.9 11.5 %collective-permute-start.6 = (bf16[256,256]{1,0:T(8,128)(2,1)S(1)}, bf16[256,256]{1,0:T(8,128)(2,1)S(1)}, u32[]{:S(2)}, u32[]{:S(2)}) collective-permute-start(bf16[256,256]{1,0:T(8,128)(2,1)S(1)} %get-tuple-element.36), channel_id=1, source_target_pairs={{0,128},{1,129},{2,130},{3,131},{4,132},{5,133},{6,134},{7,135},{8... | collective-permute-start | bytes 393224 | tf_op jit(solution)/shard_map/ppermute | solution.py:28
  18.9 8.6 %collective-permute-start.5 = (bf16[256,256]{1,0:T(8,128)(2,1)S(1)}, bf16[256,256]{1,0:T(8,128)(2,1)S(1)}, u32[]{:S(2)}, u32[]{:S(2)}) collective-permute-start(bf16[256,256]{1,0:T(8,128)(2,1)S(1)} %get-tuple-element.37), channel_id=1, source_target_pairs={{0,64},{1,65},{2,66},{3,67},{4,68},{5,69},{6,70},{7,71},{8,72},{9,... | collective-permute-start | bytes 393224 | tf_op jit(solution)/shard_map/ppermute | solution.py:28
  20.2 7.4 %copy-start.4 = (bf16[512,1024]{1,0:T(8,128)(2,1)S(1)}, bf16[512,1024]{1,0:T(8,128)(2,1)}, u32[]{:S(2)}) copy-start(bf16[512,1024]{1,0:T(8,128)(2,1)} %param.6) | copy-start | bytes 3145732
  27.6 12.8 %collective-permute-start.8 = (bf16[3,256,256]{2,1,0:T(8,128)(2,1)S(1)}, bf16[3,256,256]{2,1,0:T(8,128)(2,1)S(1)}, u32[]{:S(2)}, u32[]{:S(2)}) collective-permute-start(bf16[3,256,256]{2,1,0:T(8,128)(2,1)S(1)} %pad_maximum_fusion.4.refs_0_), channel_id=1, source_target_pairs={{0,4},{1,5},{2,6},{3,7},{4,8},{5,9},{6,10},{7,11},{8,12},{9,13},{1... | collective-permute-start | bytes 1179656 | tf_op jit(solution)/shard_map/ppermute | solution.py:28
  27.7 1.6 %copy-start.6 = (bf16[256,1024]{1,0:T(8,128)(2,1)}, bf16[256,1024]{1,0:T(8,128)(2,1)S(1)}, u32[]{:S(2)}) copy-start(bf16[256,1024]{1,0:T(8,128)(2,1)S(1)} %get-tuple-element.42) | copy-start | bytes 1572868
  27.8 1.6 %copy-start.8 = (bf16[256,1024]{1,0:T(8,128)(2,1)}, bf16[256,1024]{1,0:T(8,128)(2,1)S(1)}, u32[]{:S(2)}) copy-start(bf16[256,1024]{1,0:T(8,128)(2,1)S(1)} %get-tuple-element.43) | copy-start | bytes 1572868
  29.4 20.3 %collective-permute-start.2 = (bf16[512,512]{1,0:T(8,128)(2,1)}, bf16[512,512]{1,0:T(8,128)(2,1)S(1)}, u32[]{:S(2)}, u32[]{:S(2)}) collective-permute-start(bf16[512,512]{1,0:T(8,128)(2,1)} %convolution_convert_fusion.g0), channel_id=1, source_target_pairs={{0,64},{1,65},{2,66},{3,67},{4,68},{5,69},{6,70},{7,71},{8,72},{9,... | collective-permute-start | bytes 1572872 | tf_op jit(solution)/shard_map/ppermute | solution.py:28
  40.3 12.0 %collective-permute-start.9 = (bf16[3,256,256]{2,1,0:T(8,128)(2,1)S(1)}, bf16[3,256,256]{2,1,0:T(8,128)(2,1)S(1)}, u32[]{:S(2)}, u32[]{:S(2)}) collective-permute-start(bf16[3,256,256]{2,1,0:T(8,128)(2,1)S(1)} %pad_maximum_fusion.4.refs_0_), channel_id=1, source_target_pairs={{0,8},{1,9},{2,10},{3,11},{4,12},{5,13},{6,14},{7,15},{8,0},{9,1},... | collective-permute-start | bytes 1179656 | tf_op jit(solution)/shard_map/ppermute | solution.py:28
  41.1 18.5 %collective-permute-start.10 = (bf16[3,256,256]{2,1,0:T(8,128)(2,1)S(1)}, bf16[3,256,256]{2,1,0:T(8,128)(2,1)S(1)}, u32[]{:S(2)}, u32[]{:S(2)}) collective-permute-start(bf16[3,256,256]{2,1,0:T(8,128)(2,1)S(1)} %pad_maximum_fusion.4.refs_0_), channel_id=1, source_target_pairs={{0,12},{1,13},{2,14},{3,15},{4,0},{5,1},{6,2},{7,3},{8,4},{9,5},{1... | collective-permute-start | bytes 1179656 | tf_op jit(solution)/shard_map/ppermute | solution.py:28
  42.1 22.6 %collective-permute-start.11 = (bf16[3,256,256]{2,1,0:T(8,128)(2,1)S(1)}, bf16[3,256,256]{2,1,0:T(8,128)(2,1)S(1)}, u32[]{:S(2)}, u32[]{:S(2)}) collective-permute-start(bf16[3,256,256]{2,1,0:T(8,128)(2,1)S(1)} %pad_maximum_fusion.4.refs_0_), channel_id=1, source_target_pairs={{0,1},{1,0},{2,3},{3,2},{4,5},{5,4},{6,7},{7,6},{8,9},{9,8},{10,11... | collective-permute-start | bytes 1179656 | tf_op jit(solution)/shard_map/ppermute | solution.py:28
  46.8 26.5 %collective-permute-start.3 = (bf16[512,512]{1,0:T(8,128)(2,1)}, bf16[512,512]{1,0:T(8,128)(2,1)}, u32[]{:S(2)}, u32[]{:S(2)}) collective-permute-start(bf16[512,512]{1,0:T(8,128)(2,1)} %convolution_convert_fusion.g0), channel_id=1, source_target_pairs={{0,128},{1,129},{2,130},{3,131},{4,132},{5,133},{6,134},{7,135},{8... | collective-permute-start | bytes 1572872 | tf_op jit(solution)/shard_map/ppermute | solution.py:28
  49.6 0.8 copy-start.2
  50.4 23.7 %collective-permute-start.4 = (bf16[512,512]{1,0:T(8,128)(2,1)}, bf16[512,512]{1,0:T(8,128)(2,1)}, u32[]{:S(2)}, u32[]{:S(2)}) collective-permute-start(bf16[512,512]{1,0:T(8,128)(2,1)} %convolution_convert_fusion.g0), channel_id=1, source_target_pairs={{0,192},{1,193},{2,194},{3,195},{4,196},{5,197},{6,198},{7,199},{8... | collective-permute-start | bytes 1572872 | tf_op jit(solution)/shard_map/ppermute | solution.py:28
  52.4 12.4 %collective-permute-start.17 = (bf16[256,256]{1,0:T(8,128)(2,1)S(1)}, bf16[256,256]{1,0:T(8,128)(2,1)S(1)}, u32[]{:S(2)}, u32[]{:S(2)}) collective-permute-start(bf16[256,256]{1,0:T(8,128)(2,1)S(1)} %get-tuple-element.25), channel_id=1, source_target_pairs={{0,48},{1,49},{2,50},{3,51},{4,52},{5,53},{6,54},{7,55},{8,56},{9,... | collective-permute-start | bytes 393224 | tf_op jit(solution)/shard_map/ppermute | solution.py:28
  59.6 8.9 %collective-permute-start.16 = (bf16[256,256]{1,0:T(8,128)(2,1)S(1)}, bf16[256,256]{1,0:T(8,128)(2,1)S(1)}, u32[]{:S(2)}, u32[]{:S(2)}) collective-permute-start(bf16[256,256]{1,0:T(8,128)(2,1)S(1)} %get-tuple-element.24), channel_id=1, source_target_pairs={{0,32},{1,33},{2,34},{3,35},{4,36},{5,37},{6,38},{7,39},{8,40},{9,... | collective-permute-start | bytes 393224 | tf_op jit(solution)/shard_map/ppermute | solution.py:28
  64.7 5.3 %collective-permute-start.15 = (bf16[256,256]{1,0:T(8,128)(2,1)S(1)}, bf16[256,256]{1,0:T(8,128)(2,1)S(1)}, u32[]{:S(2)}, u32[]{:S(2)}) collective-permute-start(bf16[256,256]{1,0:T(8,128)(2,1)S(1)} %get-tuple-element.23), channel_id=1, source_target_pairs={{0,16},{1,17},{2,18},{3,19},{4,20},{5,21},{6,22},{7,23},{8,24},{9,... | collective-permute-start | bytes 393224 | tf_op jit(solution)/shard_map/ppermute | solution.py:28
  64.7 3.8 %copy-start.13 = (bf16[256,256]{1,0:T(8,128)(2,1)}, bf16[256,256]{1,0:T(8,128)(2,1)S(1)}, u32[]{:S(2)}) copy-start(bf16[256,256]{1,0:T(8,128)(2,1)S(1)} %collective-permute-done.17) | copy-start | bytes 393220
  64.7 9.4 %collective-permute-start.12 = (bf16[3,256,256]{2,1,0:T(8,128)(2,1)S(1)}, bf16[3,256,256]{2,1,0:T(8,128)(2,1)S(1)}, u32[]{:S(2)}, u32[]{:S(2)}) collective-permute-start(bf16[3,256,256]{2,1,0:T(8,128)(2,1)S(1)} %collective-permute-done.8.refs_1_), channel_id=1, source_target_pairs={{0,1},{1,0},{2,3},{3,2},{4,5},{5,4},{6,7},{7,6},{8,9},{9,8},{10,11... | collective-permute-start | bytes 1179656 | tf_op jit(solution)/shard_map/ppermute | solution.py:28
  68.5 1.5 %copy-start.15 = (bf16[256,256]{1,0:T(8,128)(2,1)}, bf16[256,256]{1,0:T(8,128)(2,1)S(1)}, u32[]{:S(2)}) copy-start(bf16[256,256]{1,0:T(8,128)(2,1)S(1)} %collective-permute-done.16) | copy-start | bytes 393220
  68.5 5.7 %collective-permute-start.14 = (bf16[3,256,256]{2,1,0:T(8,128)(2,1)S(1)}, bf16[3,256,256]{2,1,0:T(8,128)(2,1)S(1)}, u32[]{:S(2)}, u32[]{:S(2)}) collective-permute-start(bf16[3,256,256]{2,1,0:T(8,128)(2,1)S(1)} %collective-permute-done.10.refs_3_), channel_id=1, source_target_pairs={{0,1},{1,0},{2,3},{3,2},{4,5},{5,4},{6,7},{7,6},{8,9},{9,8},{10,11... | collective-permute-start | bytes 1179656 | tf_op jit(solution)/shard_map/ppermute | solution.py:28
  70.0 0.6 copy-start.17
  70.7 3.5 %collective-permute-start.13 = (bf16[3,256,256]{2,1,0:T(8,128)(2,1)S(1)}, bf16[3,256,256]{2,1,0:T(8,128)(2,1)}, u32[]{:S(2)}, u32[]{:S(2)}) collective-permute-start(bf16[3,256,256]{2,1,0:T(8,128)(2,1)S(1)} %collective-permute-done.9.refs_2_), channel_id=1, source_target_pairs={{0,1},{1,0},{2,3},{3,2},{4,5},{5,4},{6,7},{7,6},{8,9},{9,8},{10,11... | collective-permute-start | bytes 1179656 | tf_op jit(solution)/shard_map/ppermute | solution.py:28
  70.7 2.5 %copy-start.12 = (bf16[1,256,256]{2,1,0:T(8,128)(2,1)S(1)}, bf16[1,256,256]{2,1,0:T(8,128)(2,1)}, u32[]{:S(2)}) copy-start(bf16[1,256,256]{2,1,0:T(8,128)(2,1)} %get-tuple-element.48) | copy-start | bytes 393220
  70.7 2.5 %copy-start.14 = (bf16[256,256]{1,0:T(8,128)(2,1)S(1)}, bf16[256,256]{1,0:T(8,128)(2,1)}, u32[]{:S(2)}) copy-start(bf16[256,256]{1,0:T(8,128)(2,1)} %copy-done.13) | copy-start | bytes 393220
  70.7 2.5 %copy-start.16 = (bf16[256,256]{1,0:T(8,128)(2,1)S(1)}, bf16[256,256]{1,0:T(8,128)(2,1)}, u32[]{:S(2)}) copy-start(bf16[256,256]{1,0:T(8,128)(2,1)} %copy-done.15) | copy-start | bytes 393220
  70.7 2.5 %copy-start.18 = (bf16[256,256]{1,0:T(8,128)(2,1)S(1)}, bf16[256,256]{1,0:T(8,128)(2,1)}, u32[]{:S(2)}) copy-start(bf16[256,256]{1,0:T(8,128)(2,1)} %copy-done.17) | copy-start | bytes 393220
  70.7 3.5 %copy-start.3 = (bf16[512,512]{1,0:T(8,128)(2,1)S(1)}, bf16[512,512]{1,0:T(8,128)(2,1)}, u32[]{:S(2)}) copy-start(bf16[512,512]{1,0:T(8,128)(2,1)} %copy-done.2) | copy-start | bytes 1572868
  74.2 6.4 %copy-start.7 = (bf16[256,1024]{1,0:T(8,128)(2,1)S(1)}, bf16[256,1024]{1,0:T(8,128)(2,1)}, u32[]{:S(2)}) copy-start(bf16[256,1024]{1,0:T(8,128)(2,1)} %copy-done.6) | copy-start | bytes 1572868
  74.2 6.4 %copy-start.9 = (bf16[256,1024]{1,0:T(8,128)(2,1)S(1)}, bf16[256,1024]{1,0:T(8,128)(2,1)}, u32[]{:S(2)}) copy-start(bf16[256,1024]{1,0:T(8,128)(2,1)} %copy-done.8) | copy-start | bytes 1572868
  74.2 6.4 %copy-start.10 = (bf16[1024,256]{1,0:T(8,128)(2,1)S(1)}, bf16[1024,256]{1,0:T(8,128)(2,1)}, u32[]{:S(2)}) copy-start(bf16[1024,256]{1,0:T(8,128)(2,1)} %get-tuple-element.39) | copy-start | bytes 1572868
  74.2 6.4 %copy-start.11 = (bf16[1024,256]{1,0:T(8,128)(2,1)S(1)}, bf16[1024,256]{1,0:T(8,128)(2,1)}, u32[]{:S(2)}) copy-start(bf16[1024,256]{1,0:T(8,128)(2,1)} %get-tuple-element.40) | copy-start | bytes 1572868
  79.1 14.0 %collective-permute-start.18 = (bf16[256,1024]{1,0:T(8,128)(2,1)S(1)}, bf16[256,1024]{1,0:T(8,128)(2,1)S(1)}, u32[]{:S(2)}, u32[]{:S(2)}) collective-permute-start(bf16[256,1024]{1,0:T(8,128)(2,1)S(1)} %shard_map.56), channel_id=1, source_target_pairs={{0,16},{1,17},{2,18},{3,19},{4,20},{5,21},{6,22},{7,23},{8,24},{9,... | collective-permute-start | bytes 1572872 | tf_op jit(solution)/shard_map/ppermute | solution.py:28
  81.3 18.2 %collective-permute-start.19 = (bf16[512,512]{1,0:T(8,128)(2,1)S(1)}, bf16[512,512]{1,0:T(8,128)(2,1)S(1)}, u32[]{:S(2)}, u32[]{:S(2)}) collective-permute-start(bf16[512,512]{1,0:T(8,128)(2,1)S(1)} %convolution_convert_fusion.1.g0), channel_id=1, source_target_pairs={{0,64},{1,65},{2,66},{3,67},{4,68},{5,69},{6,70},{7,71},{8,72},{9,... | collective-permute-start | bytes 1572872 | tf_op jit(solution)/shard_map/ppermute | solution.py:28
  82.0 19.7 %collective-permute-start.20 = (bf16[512,512]{1,0:T(8,128)(2,1)S(1)}, bf16[512,512]{1,0:T(8,128)(2,1)S(1)}, u32[]{:S(2)}, u32[]{:S(2)}) collective-permute-start(bf16[512,512]{1,0:T(8,128)(2,1)S(1)} %convolution_convert_fusion.1.g0), channel_id=1, source_target_pairs={{0,128},{1,129},{2,130},{3,131},{4,132},{5,133},{6,134},{7,135},{8... | collective-permute-start | bytes 1572872 | tf_op jit(solution)/shard_map/ppermute | solution.py:28
  85.0 22.8 %collective-permute-start.21 = (bf16[512,512]{1,0:T(8,128)(2,1)S(1)}, bf16[512,512]{1,0:T(8,128)(2,1)S(1)}, u32[]{:S(2)}, u32[]{:S(2)}) collective-permute-start(bf16[512,512]{1,0:T(8,128)(2,1)S(1)} %convolution_convert_fusion.1.g0), channel_id=1, source_target_pairs={{0,192},{1,193},{2,194},{3,195},{4,196},{5,197},{6,198},{7,199},{8... | collective-permute-start | bytes 1572872 | tf_op jit(solution)/shard_map/ppermute | solution.py:28
  93.3 21.3 %collective-permute-start.24 = (bf16[2,256,256]{2,1,0:T(8,128)(2,1)S(1)}, bf16[2,256,256]{2,1,0:T(8,128)(2,1)S(1)}, u32[]{:S(2)}, u32[]{:S(2)}) collective-permute-start(bf16[2,256,256]{2,1,0:T(8,128)(2,1)S(1)} %pad_maximum_fusion.5.refs_0_), channel_id=1, source_target_pairs={{0,4},{1,5},{2,6},{3,7},{4,8},{5,9},{6,10},{7,11},{8,12},{9,13},{1... | collective-permute-start | bytes 786440 | tf_op jit(solution)/shard_map/ppermute | solution.py:28
  95.9 37.1 %collective-permute-start.23 = (bf16[256,1024]{1,0:T(8,128)(2,1)S(1)}, bf16[256,1024]{1,0:T(8,128)(2,1)S(1)}, u32[]{:S(2)}, u32[]{:S(2)}) collective-permute-start(bf16[256,1024]{1,0:T(8,128)(2,1)S(1)} %add_convert_fusion), channel_id=1, source_target_pairs={{0,32},{1,33},{2,34},{3,35},{4,36},{5,37},{6,38},{7,39},{8,40},{9,... | collective-permute-start | bytes 1572872 | tf_op jit(solution)/shard_map/ppermute | solution.py:28
  99.5 16.9 %collective-permute-start.26 = (bf16[2,256,256]{2,1,0:T(8,128)(2,1)S(1)}, bf16[2,256,256]{2,1,0:T(8,128)(2,1)S(1)}, u32[]{:S(2)}, u32[]{:S(2)}) collective-permute-start(bf16[2,256,256]{2,1,0:T(8,128)(2,1)S(1)} %pad_maximum_fusion.5.refs_0_), channel_id=1, source_target_pairs={{0,12},{1,13},{2,14},{3,15},{4,0},{5,1},{6,2},{7,3},{8,4},{9,5},{1... | collective-permute-start | bytes 786440 | tf_op jit(solution)/shard_map/ppermute | solution.py:28
  101.8 14.7 %collective-permute-start.27 = (bf16[2,256,256]{2,1,0:T(8,128)(2,1)S(1)}, bf16[2,256,256]{2,1,0:T(8,128)(2,1)S(1)}, u32[]{:S(2)}, u32[]{:S(2)}) collective-permute-start(bf16[2,256,256]{2,1,0:T(8,128)(2,1)S(1)} %pad_maximum_fusion.5.refs_0_), channel_id=1, source_target_pairs={{0,1},{1,0},{2,3},{3,2},{4,5},{5,4},{6,7},{7,6},{8,9},{9,8},{10,11... | collective-permute-start | bytes 786440 | tf_op jit(solution)/shard_map/ppermute | solution.py:28
  107.8 0.8 copy-start.5
  113.6 19.4 %collective-permute-start.22 = (bf16[256,1024]{1,0:T(8,128)(2,1)S(1)}, bf16[256,1024]{1,0:T(8,128)(2,1)S(1)}, u32[]{:S(2)}, u32[]{:S(2)}) collective-permute-start(bf16[256,1024]{1,0:T(8,128)(2,1)S(1)} %get-tuple-element.30), channel_id=1, source_target_pairs={{0,16},{1,17},{2,18},{3,19},{4,20},{5,21},{6,22},{7,23},{8,24},{9,... | collective-permute-start | bytes 1572872 | tf_op jit(solution)/shard_map/ppermute | solution.py:28
  114.6 9.5 %collective-permute-start.25 = (bf16[2,256,256]{2,1,0:T(8,128)(2,1)S(1)}, bf16[2,256,256]{2,1,0:T(8,128)(2,1)S(1)}, u32[]{:S(2)}, u32[]{:S(2)}) collective-permute-start(bf16[2,256,256]{2,1,0:T(8,128)(2,1)S(1)} %pad_maximum_fusion.5.refs_0_), channel_id=1, source_target_pairs={{0,8},{1,9},{2,10},{3,11},{4,12},{5,13},{6,14},{7,15},{8,0},{9,1},... | collective-permute-start | bytes 786440 | tf_op jit(solution)/shard_map/ppermute | solution.py:28
  116.4 7.7 %collective-permute-start.28 = (bf16[2,256,256]{2,1,0:T(8,128)(2,1)S(1)}, bf16[2,256,256]{2,1,0:T(8,128)(2,1)S(1)}, u32[]{:S(2)}, u32[]{:S(2)}) collective-permute-start(bf16[2,256,256]{2,1,0:T(8,128)(2,1)S(1)} %collective-permute-done.24.refs_1_), channel_id=1, source_target_pairs={{0,1},{1,0},{2,3},{3,2},{4,5},{5,4},{6,7},{7,6},{8,9},{9,8},{10,11... | collective-permute-start | bytes 786440 | tf_op jit(solution)/shard_map/ppermute | solution.py:28
  116.4 7.6 %collective-permute-start.30 = (bf16[2,256,256]{2,1,0:T(8,128)(2,1)S(1)}, bf16[2,256,256]{2,1,0:T(8,128)(2,1)S(1)}, u32[]{:S(2)}, u32[]{:S(2)}) collective-permute-start(bf16[2,256,256]{2,1,0:T(8,128)(2,1)S(1)} %collective-permute-done.26.refs_3_), channel_id=1, source_target_pairs={{0,1},{1,0},{2,3},{3,2},{4,5},{5,4},{6,7},{7,6},{8,9},{9,8},{10,11... | collective-permute-start | bytes 786440 | tf_op jit(solution)/shard_map/ppermute | solution.py:28
  124.1 8.9 %collective-permute-start.29 = (bf16[2,256,256]{2,1,0:T(8,128)(2,1)S(1)}, bf16[2,256,256]{2,1,0:T(8,128)(2,1)S(1)}, u32[]{:S(2)}, u32[]{:S(2)}) collective-permute-start(bf16[2,256,256]{2,1,0:T(8,128)(2,1)S(1)} %collective-permute-done.25.refs_2_), channel_id=1, source_target_pairs={{0,1},{1,0},{2,3},{3,2},{4,5},{5,4},{6,7},{7,6},{8,9},{9,8},{10,11... | collective-permute-start | bytes 786440 | tf_op jit(solution)/shard_map/ppermute | solution.py:28
  133.0 15.8 %copy-start.1 = (bf16[1024,1024]{1,0:T(8,128)(2,1)S(1)}, bf16[1024,1024]{1,0:T(8,128)(2,1)}, u32[]{:S(2)}) copy-start(bf16[1024,1024]{1,0:T(8,128)(2,1)} %basis.1) | copy-start | bytes 6291460
  135.4 7.7 %collective-permute-start.31 = (bf16[256,256]{1,0:T(8,128)(2,1)S(1)}, bf16[256,256]{1,0:T(8,128)(2,1)S(1)}, u32[]{:S(2)}, u32[]{:S(2)}) collective-permute-start(bf16[256,256]{1,0:T(8,128)(2,1)S(1)} %get-tuple-element.46), channel_id=1, source_target_pairs={{0,16},{1,17},{2,18},{3,19},{4,20},{5,21},{6,22},{7,23},{8,24},{9,... | collective-permute-start | bytes 393224 | tf_op jit(solution)/shard_map/ppermute | solution.py:28
  135.5 13.2 %collective-permute-start.32 = (bf16[256,256]{1,0:T(8,128)(2,1)S(1)}, bf16[256,256]{1,0:T(8,128)(2,1)S(1)}, u32[]{:S(2)}, u32[]{:S(2)}) collective-permute-start(bf16[256,256]{1,0:T(8,128)(2,1)S(1)} %get-tuple-element.45), channel_id=1, source_target_pairs={{0,32},{1,33},{2,34},{3,35},{4,36},{5,37},{6,38},{7,39},{8,40},{9,... | collective-permute-start | bytes 393224 | tf_op jit(solution)/shard_map/ppermute | solution.py:28
  138.8 10.0 %collective-permute-start.33 = (bf16[256,256]{1,0:T(8,128)(2,1)S(1)}, bf16[256,256]{1,0:T(8,128)(2,1)S(1)}, u32[]{:S(2)}, u32[]{:S(2)}) collective-permute-start(bf16[256,256]{1,0:T(8,128)(2,1)S(1)} %get-tuple-element.44), channel_id=1, source_target_pairs={{0,48},{1,49},{2,50},{3,51},{4,52},{5,53},{6,54},{7,55},{8,56},{9,... | collective-permute-start | bytes 393224 | tf_op jit(solution)/shard_map/ppermute | solution.py:28
